TPU v7x, 32 devices: a whole 2x2x4 slice. The times are simulated.
32 devices in a mesh: cuts: 8 (over z, x), row: 4 (over y, core).
Axes of the slice: x: 2, y: 2, z: 4, core: 2. Of those that a mesh axis runs over, the one named last changes fastest.
Arguments:
- operator: bfloat16 [8, 2404, 2404], P('cuts', 'row'), may hold values from -0.125 to 0.125
- incident: bfloat16 [8, 2404, 256], P('cuts', 'row'), may hold values from -6 to 6
- reflect: float32 [8, 3, 2404, 256], P('cuts', None, 'row'), may hold values from -0.8 to 0.8
- thickness_table: float32 [8], replicated, may hold values from 0.5 to 1.5
- profile: int32 [8], P('cuts'), may hold values from 0 to 7
- order_index: int32 [64], replicated, may hold values from 0 to 600
- cotangent: float32 [8, 64, 256], P('cuts'), may hold values from -6 to 6
Outputs:
- grad_operator: float32 [8, 2404, 2404], P('cuts', 'row')
- grad_incident: float32 [8, 2404, 256], P('cuts', 'row')
All inputs are finite; a program needn't handle non-finite values.
Results may differ from a plain program's by a relative error of at most 0.0095.
Values may be sent and summed in bfloat16 or wider, within the bound.
No kernel may reach another device: no remote copies, remote signals or barrier semaphores. Data moves between devices by JAX's collectives and lax.ppermute only.
A program may use at most 128 MiB of HBM per device.

v0:
```python
import math

import jax
import jax.numpy as jnp
from jax import lax
from jax.sharding import PartitionSpec as P

ORDERS = 601
TAYLOR = 3
LEVELS = 3


def partner(value, axis, stride):
    mask = 2**stride
    pairs = [(source, source ^ mask) for source in range(lax.axis_size(axis))]
    return lax.ppermute(value, axis, pairs)


def local(operator, incident, reflect, thickness_table, profile, order_index, cotangent):
    a_panel = operator[0]
    x_input = incident[0]
    row_count = a_panel.shape[0]
    full_width = a_panel.shape[1]
    columns = x_input.shape[1]
    profiles = thickness_table.shape[0]
    step_len = jnp.sum(jnp.where(profile[0] == jnp.arange(profiles), thickness_table, 0.0))
    x_wide = x_input.astype(jnp.float32)
    current = x_input
    stored = []
    for degree in range(TAYLOR, 0, -1):
        stored.append(current)
        product = jnp.dot(
            a_panel,
            lax.all_gather(current, "row", axis=0, tiled=True),
            preferred_element_type=jnp.float32,
        )
        current = (x_wide + step_len / degree * product).astype(jnp.bfloat16)
    merged = current.astype(jnp.float32)
    for section_level in range(LEVELS):
        other_field, other_reflect = partner(
            (merged, reflect[0, section_level]), "cuts", section_level
        )
        merged = merged + other_reflect * other_field
    global_row = lax.axis_index("row") * row_count + jnp.arange(row_count, dtype=jnp.int32)
    onehot = ((global_row % ORDERS)[:, None] == order_index[None, :]).astype(jnp.float32)
    cmap = jnp.dot(onehot, cotangent[0], precision=lax.Precision.HIGHEST)
    squared = merged * merged
    power, weighted = lax.psum((jnp.sum(squared, axis=0), jnp.sum(cmap * squared, axis=0)), "row")
    mean_power = power / full_width + 1e-06
    scale = 1.0 / math.sqrt(columns)
    upstream = scale * (
        2.0 * cmap * merged / mean_power[None, :]
        - 2.0 / full_width * (weighted / (mean_power * mean_power))[None, :] * merged
    )
    for section_level in range(LEVELS - 1, -1, -1):
        other_grad = partner(upstream, "cuts", section_level)
        upstream = upstream + reflect[0, section_level] * other_grad
    a_columns = lax.all_to_all(a_panel, "row", split_axis=1, concat_axis=0, tiled=True)
    grad_input = jnp.zeros((row_count, columns), jnp.float32)
    grad_matrix = jnp.zeros((row_count, full_width), jnp.float32)
    for degree in range(1, TAYLOR + 1):
        grad_input = grad_input + upstream
        scaled = (step_len / degree * upstream).astype(jnp.bfloat16)
        grad_matrix = grad_matrix + lax.dot_general(
            scaled,
            lax.all_gather(stored[TAYLOR - degree], "row", axis=0, tiled=True),
            (((1,), (1,)), ((), ())),
            preferred_element_type=jnp.float32,
        )
        upstream = lax.dot_general(
            a_columns,
            lax.all_gather(scaled, "row", axis=0, tiled=True),
            (((0,), (0,)), ((), ())),
            preferred_element_type=jnp.float32,
        )
    grad_input = grad_input + upstream
    return (grad_matrix[None], grad_input[None])


def solution(mesh):
    return jax.shard_map(
        local,
        mesh=mesh,
        in_specs=(
            P("cuts", "row", None),
            P("cuts", "row", None),
            P("cuts", None, "row", None),
            P(),
            P("cuts"),
            P(),
            P("cuts", None, None),
        ),
        out_specs=(P("cuts", "row", None), P("cuts", "row", None)),
        check_vma=False,
    )
```

profile of v0, /device:TPU:0, one launch (start us, length us, event | category | flops | bytes accessed | tf_op | source)
XLA Modules:
  0.0 338.7 jit_solution(4161867323284013756)
XLA Ops:
  7.2 2.3 copy.27
  12.1 25.4 %all-gather.13.cloned.1.call-done = bf16[1,2404,256]{2,0,1:T(2,128)(2,1)} async-done(((bf16[1,601,256]{2,0,1:T(2,128)(2,1)}), bf16[1,2404,256]{2,0,1:T(2,128)(2,1)}) %all-gather.13.cloned.1.call-update) | async-done | bytes 1230864 | tf_op jit(solution)/shard_map/all_gather | solution.py:34
  37.5 4.3 %fusion.49 = bf16[1,601,256]{2,1,0:T(8,128)(2,1)} fusion(bf16[1,601,2404]{2,1,0:T(8,128)(2,1)} %param.7, bf16[1,2404,256]{2,0,1:T(2,128)(2,1)} %all-gather.13.cloned.1.call-done, bf16[1,601,256]{2,1,0:T(8,128)(2,1)} %param.8, f32[]{:T(128)S(6)} %div.28), kind=kOutput, calls=%fused_computation.25 | convolution fusion | flops 740355072 | bytes 4735884 | tf_op jit(solution)/shard_map/dot_general | solution.py:32
  42.5 17.3 %all-gather.15.cloned.1.call-done = bf16[4,601,256]{2,1,0:T(8,128)(2,1)} async-done(((bf16[1,601,256]{2,1,0:T(8,128)(2,1)}), bf16[4,601,256]{2,1,0:T(8,128)(2,1)}) %all-gather.15.cloned.1.call-update) | async-done | bytes 1230864 | tf_op jit(solution)/shard_map/all_gather | solution.py:34
  61.5 4.0 %fusion.54 = bf16[1,601,256]{2,1,0:T(8,128)(2,1)} fusion(bf16[2404,256]{1,0:T(8,128)(2,1)S(1)} %reshape.25, bf16[1,601,2404]{2,1,0:T(8,128)(2,1)} %param.7, bf16[1,601,256]{2,1,0:T(8,128)(2,1)S(1)} %copy-done.13, f32[]{:T(128)S(6)} %div.27), kind=kOutput, calls=%fused_computation.26 | convolution fusion | flops 740355072 | bytes 4735884 | tf_op jit(solution)/shard_map/dot_general | solution.py:32
  65.5 2.7 fusion.73
  71.4 12.1 %all-gather.17.cloned.1.call-done = bf16[4,601,256]{2,1,0:T(8,128)(2,1)} async-done(((bf16[1,601,256]{2,1,0:T(8,128)(2,1)}), bf16[4,601,256]{2,1,0:T(8,128)(2,1)}) %all-gather.17.cloned.1.call-update) | async-done | bytes 1230864 | tf_op jit(solution)/shard_map/all_gather | solution.py:34
  85.1 3.4 %fusion.41 = f32[601,256]{1,0:T(8,128)S(1)} fusion(bf16[2404,256]{1,0:T(8,128)(2,1)S(1)} %reshape.27, bf16[1,601,2404]{2,1,0:T(8,128)(2,1)} %param.7, bf16[1,601,256]{2,1,0:T(8,128)(2,1)S(1)} %copy-done.13, f32[]{:T(128)} %fusion.72), kind=kOutput, calls=%fused_computation.23 | convolution fusion | flops 740508928 | bytes 5043596 | tf_op jit(solution)/shard_map/dot_general | solution.py:32
  91.7 13.1 %collective-permute-done.1 = f32[601,256]{1,0:T(8,128)S(1)} collective-permute-done((f32[601,256]{1,0:T(8,128)S(1)}, f32[601,256]{1,0:T(8,128)S(1)}, u32[]{:S(2)}, u32[]{:S(2)}) %collective-permute-start.1) | collective-permute-done | bytes 615456 | tf_op jit(solution)/shard_map/ppermute | solution.py:16
  107.4 2.4 collective-permute-start.4
  109.8 22.6 %collective-permute-done.3 = f32[601,256]{1,0:T(8,128)S(1)} collective-permute-done((f32[601,256]{1,0:T(8,128)S(1)}, f32[601,256]{1,0:T(8,128)S(1)}, u32[]{:S(2)}, u32[]{:S(2)}) %collective-permute-start.3) | collective-permute-done | bytes 615456 | tf_op jit(solution)/shard_map/ppermute | solution.py:16
  133.6 17.9 %collective-permute-done.4 = f32[601,256]{1,0:T(8,128)S(1)} collective-permute-done((f32[601,256]{1,0:T(8,128)}, f32[601,256]{1,0:T(8,128)S(1)}, u32[]{:S(2)}, u32[]{:S(2)}) %collective-permute-start.4) | collective-permute-done | bytes 615456 | tf_op jit(solution)/shard_map/ppermute | solution.py:16
  152.3 11.4 %collective-permute-done.5 = f32[601,256]{1,0:T(8,128)} collective-permute-done((f32[601,256]{1,0:T(8,128)S(1)}, f32[601,256]{1,0:T(8,128)}, u32[]{:S(2)}, u32[]{:S(2)}) %collective-permute-start.5) | collective-permute-done | bytes 615456 | tf_op jit(solution)/shard_map/ppermute | solution.py:16
  165.2 5.9 %all-reduce = (f32[256]{0:T(256)S(1)}, f32[256]{0:T(256)S(1)}) all-reduce(f32[256]{0:T(256)S(1)} %get-tuple-element.11, f32[256]{0:T(256)S(1)} %get-tuple-element.10), channel_id=1, replica_groups=mesh['cuts'=8,'row'=4] {'row'}, use_global_device_ids=true, to_apply=%region_4.5 | all-reduce | flops 512 | bytes 4096 | tf_op jit(solution)/shard_map/psum | solution.py:48
  171.4 29.5 %collective-permute-done.6 = f32[601,256]{1,0:T(8,128)S(1)} collective-permute-done((f32[601,256]{1,0:T(8,128)S(1)}, f32[601,256]{1,0:T(8,128)S(1)}, u32[]{:S(2)}, u32[]{:S(2)}) %collective-permute-start.6) | collective-permute-done | bytes 615456 | tf_op jit(solution)/shard_map/ppermute | solution.py:16
  201.1 15.9 %collective-permute-done.7 = f32[601,256]{1,0:T(8,128)S(1)} collective-permute-done((f32[601,256]{1,0:T(8,128)S(1)}, f32[601,256]{1,0:T(8,128)S(1)}, u32[]{:S(2)}, u32[]{:S(2)}) %collective-permute-start.7) | collective-permute-done | bytes 615456 | tf_op jit(solution)/shard_map/ppermute | solution.py:16
  219.6 6.3 %all_to_all.14 = bf16[601,4,601]{2,1,0:T(4,128)(2,1)S(1)} reshape(bf16[1,601,2404]{2,1,0:T(8,128)(2,1)} %param.7) | data formatting | bytes 5779216 | tf_op jit(solution)/shard_map/all_to_all | solution.py:58
  225.8 2.0 copy.31
  227.9 3.7 %all-to-all-start = ((bf16[601,4,601]{2,0,1:T(8,128)(2,1)}), bf16[601,4,601]{2,0,1:T(8,128)(2,1)S(1)}, u32[]{:S(2)}, u32[]{:S(2)}) async-start(bf16[601,4,601]{2,0,1:T(8,128)(2,1)} %copy.31), calls=%async_computation | async-start | bytes 6225920 | tf_op jit(solution)/shard_map/all_to_all | solution.py:58
  231.6 1.9 collective-permute-done.8
  233.5 3.2 fusion.63
  237.0 37.8 %all-to-all-done = bf16[601,4,601]{2,0,1:T(8,128)(2,1)S(1)} async-done(((bf16[601,4,601]{2,0,1:T(8,128)(2,1)}), bf16[601,4,601]{2,0,1:T(8,128)(2,1)S(1)}, u32[]{:S(2)}, u32[]{:S(2)}) %all-to-all-start) | async-done | bytes 2889640 | tf_op jit(solution)/shard_map/all_to_all | solution.py:58
  274.8 3.1 all_to_all.17
  279.5 3.2 convolution_bitcast_fusion.2
  284.5 15.1 %all-gather.21.cloned.1.call-done = bf16[4,601,256]{2,1,0:T(8,128)(2,1)} async-done(((bf16[1,601,256]{2,1,0:T(8,128)(2,1)}), bf16[4,601,256]{2,1,0:T(8,128)(2,1)}) %all-gather.21.cloned.1.call-update) | async-done | bytes 1230864 | tf_op jit(solution)/shard_map/all_gather | solution.py:72
  299.6 2.6 reshape.31
  302.3 2.6 convolution_bitcast_fusion.1
  306.5 2.6 fusion.65
  312.4 8.6 %copy.32 = f32[1,601,2404]{2,0,1:T(1,128)} copy(f32[1,601,2404]{2,1,0:T(8,128)S(1)} %add_bitcast_fusion) | data formatting | bytes 11558432
  321.0 3.5 %all-gather.23.cloned.1.call-done = bf16[4,601,256]{2,1,0:T(8,128)(2,1)} async-done(((bf16[1,601,256]{2,1,0:T(8,128)(2,1)}), bf16[4,601,256]{2,1,0:T(8,128)(2,1)}) %all-gather.23.cloned.1.call-update) | async-done | bytes 1230864 | tf_op jit(solution)/shard_map/all_gather | solution.py:72
  324.5 2.7 reshape.33
  327.2 3.2 add_bitcast_fusion.1
  (74 shorter events, 29.8 us)
Async XLA Ops:
  7.2 125.9 %copy-start = (f32[1,64,256]{2,1,0:T(8,128)S(1)}, f32[1,64,256]{2,1,0:T(8,128)}, u32[]{:S(2)}) copy-start(f32[1,64,256]{2,1,0:T(8,128)} %param.13) | copy-start | bytes 196612
  7.2 30.4 %all-gather.13.cloned.1.call-start = ((), (), s32[]{:S(2)}) async-start(), calls=%async_computation.1 | async-start | bytes 3077120 | tf_op jit(solution)/shard_map/all_gather | solution.py:34
  9.5 50.3 %all-gather.15.cloned.1.call-start = ((), (), s32[]{:S(2)}) async-start(), calls=%async_computation.2 | async-start | bytes 1556480 | tf_op jit(solution)/shard_map/all_gather | solution.py:34
  41.8 19.6 %copy-start.13 = (bf16[1,601,256]{2,1,0:T(8,128)(2,1)S(1)}, bf16[1,601,256]{2,1,0:T(8,128)(2,1)}, u32[]{:S(2)}) copy-start(bf16[1,601,256]{2,1,0:T(8,128)(2,1)} %param.8) | copy-start | bytes 923140
  41.8 41.6 %all-gather.17.cloned.1.call-start = ((), (), s32[]{:S(2)}) async-start(), calls=%async_computation.3 | async-start | bytes 1556480 | tf_op jit(solution)/shard_map/all_gather | solution.py:34
  61.5 4.0 %copy-start.10 = (bf16[2404,256]{1,0:T(8,128)(2,1)}, bf16[2404,256]{1,0:T(8,128)(2,1)S(1)}, u32[]{:S(2)}) copy-start(bf16[2404,256]{1,0:T(8,128)(2,1)S(1)} %reshape.25) | copy-start | bytes 3692548
  68.2 0.8 copy-start.7
  69.9 21.8 %collective-permute-start = (f32[601,256]{1,0:T(8,128)}, f32[601,256]{1,0:T(8,128)S(1)}, u32[]{:S(2)}, u32[]{:S(2)}) collective-permute-start(f32[601,256]{1,0:T(8,128)} %bitcast.119), channel_id=1, source_target_pairs={{0,4},{4,0},{8,12},{12,8},{16,20},{20,16},{24,28},{28,24},{1,5},{5... | collective-permute-start | bytes 1846280 | tf_op jit(solution)/shard_map/ppermute | solution.py:16
  85.1 3.5 %copy-start.8 = (bf16[2404,256]{1,0:T(8,128)(2,1)}, bf16[2404,256]{1,0:T(8,128)(2,1)S(1)}, u32[]{:S(2)}) copy-start(bf16[2404,256]{1,0:T(8,128)(2,1)S(1)} %reshape.27) | copy-start | bytes 3692548
  88.5 16.2 %collective-permute-start.1 = (f32[601,256]{1,0:T(8,128)S(1)}, f32[601,256]{1,0:T(8,128)S(1)}, u32[]{:S(2)}, u32[]{:S(2)}) collective-permute-start(f32[601,256]{1,0:T(8,128)S(1)} %fusion.41), channel_id=1, source_target_pairs={{0,4},{4,0},{8,12},{12,8},{16,20},{20,16},{24,28},{28,24},{1,5},{5... | collective-permute-start | bytes 1846280 | tf_op jit(solution)/shard_map/ppermute | solution.py:16
  90.1 19.7 %collective-permute-start.2 = (f32[601,256]{1,0:T(8,128)S(1)}, f32[601,256]{1,0:T(8,128)S(1)}, u32[]{:S(2)}, u32[]{:S(2)}) collective-permute-start(f32[601,256]{1,0:T(8,128)S(1)} %bitcast.122), channel_id=1, source_target_pairs={{0,8},{4,12},{8,0},{12,4},{16,24},{20,28},{24,16},{28,20},{1,9},{5... | collective-permute-start | bytes 1846280 | tf_op jit(solution)/shard_map/ppermute | solution.py:16
  104.9 28.2 %copy-start.14 = (s32[64]{0:T(128)S(1)}, s32[64]{0:T(128)}, u32[]{:S(2)}) copy-start(s32[64]{0:T(128)} %param.12) | copy-start | bytes 772
  105.0 27.5 %collective-permute-start.3 = (f32[601,256]{1,0:T(8,128)S(1)}, f32[601,256]{1,0:T(8,128)S(1)}, u32[]{:S(2)}, u32[]{:S(2)}) collective-permute-start(f32[601,256]{1,0:T(8,128)S(1)} %multiply_add_fusion.5), channel_id=1, source_target_pairs={{0,8},{4,12},{8,0},{12,4},{16,24},{20,28},{24,16},{28,20},{1,9},{5... | collective-permute-start | bytes 1846280 | tf_op jit(solution)/shard_map/ppermute | solution.py:16
  107.4 44.1 %collective-permute-start.4 = (f32[601,256]{1,0:T(8,128)}, f32[601,256]{1,0:T(8,128)S(1)}, u32[]{:S(2)}, u32[]{:S(2)}) collective-permute-start(f32[601,256]{1,0:T(8,128)} %bitcast.117), channel_id=1, source_target_pairs={{0,16},{4,20},{8,24},{12,28},{16,0},{20,4},{24,8},{28,12},{1,17},{... | collective-permute-start | bytes 1846280 | tf_op jit(solution)/shard_map/ppermute | solution.py:16
  132.5 31.2 %collective-permute-start.5 = (f32[601,256]{1,0:T(8,128)S(1)}, f32[601,256]{1,0:T(8,128)}, u32[]{:S(2)}, u32[]{:S(2)}) collective-permute-start(f32[601,256]{1,0:T(8,128)S(1)} %multiply_add_fusion.4), channel_id=1, source_target_pairs={{0,16},{4,20},{8,24},{12,28},{16,0},{20,4},{24,8},{28,12},{1,17},{... | collective-permute-start | bytes 1846280 | tf_op jit(solution)/shard_map/ppermute | solution.py:16
  151.5 0.8 copy-start.11
  171.4 29.6 %collective-permute-start.6 = (f32[601,256]{1,0:T(8,128)S(1)}, f32[601,256]{1,0:T(8,128)S(1)}, u32[]{:S(2)}, u32[]{:S(2)}) collective-permute-start(f32[601,256]{1,0:T(8,128)S(1)} %subtract_multiply_fusion), channel_id=1, source_target_pairs={{0,16},{4,20},{8,24},{12,28},{16,0},{20,4},{24,8},{28,12},{1,17},{... | collective-permute-start | bytes 1846280 | tf_op jit(solution)/shard_map/ppermute | solution.py:16
  201.1 16.0 %collective-permute-start.7 = (f32[601,256]{1,0:T(8,128)S(1)}, f32[601,256]{1,0:T(8,128)S(1)}, u32[]{:S(2)}, u32[]{:S(2)}) collective-permute-start(f32[601,256]{1,0:T(8,128)S(1)} %multiply_add_fusion.2), channel_id=1, source_target_pairs={{0,8},{4,12},{8,0},{12,4},{16,24},{20,28},{24,16},{28,20},{1,9},{5... | collective-permute-start | bytes 1846280 | tf_op jit(solution)/shard_map/ppermute | solution.py:16
  218.1 15.4 %collective-permute-start.8 = (f32[601,256]{1,0:T(8,128)}, f32[601,256]{1,0:T(8,128)}, u32[]{:S(2)}, u32[]{:S(2)}) collective-permute-start(f32[601,256]{1,0:T(8,128)} %multiply_add_fusion.1), channel_id=1, source_target_pairs={{0,4},{4,0},{8,12},{12,8},{16,20},{20,16},{24,28},{28,24},{1,5},{5... | collective-permute-start | bytes 1846280 | tf_op jit(solution)/shard_map/ppermute | solution.py:16
  227.9 46.9 %all-to-all-start = ((bf16[601,4,601]{2,0,1:T(8,128)(2,1)}), bf16[601,4,601]{2,0,1:T(8,128)(2,1)S(1)}, u32[]{:S(2)}, u32[]{:S(2)}) async-start(bf16[601,4,601]{2,0,1:T(8,128)(2,1)} %copy.31), calls=%async_computation | async-start | bytes 6225920 | tf_op jit(solution)/shard_map/all_to_all | solution.py:58
  231.6 46.3 %all-gather.19.cloned.1.call-start = ((), (), s32[]{:S(2)}) async-start(), calls=%async_computation.4 | async-start | bytes 1556480 | tf_op jit(solution)/shard_map/all_gather | solution.py:72
  236.8 62.8 %all-gather.21.cloned.1.call-start = ((), (), s32[]{:S(2)}) async-start(), calls=%async_computation.5 | async-start | bytes 1556480 | tf_op jit(solution)/shard_map/all_gather | solution.py:72
  282.7 0.9 copy-start.3
  283.6 18.6 %copy-start.2 = (bf16[2404,601]{1,0:T(8,128)(2,1)S(1)}, bf16[2404,601]{1,0:T(8,128)(2,1)}, u32[]{:S(2)}) copy-start(bf16[2404,601]{1,0:T(8,128)(2,1)} %all_to_all.17) | copy-start | bytes 8668828
  284.4 40.1 %all-gather.23.cloned.1.call-start = ((), (), s32[]{:S(2)}) async-start(), calls=%async_computation.6 | async-start | bytes 1556480 | tf_op jit(solution)/shard_map/all_gather | solution.py:72
  304.9 0.8 copy-start.4
  306.5 2.7 copy-start.5
  306.5 2.7 copy-start.12
  309.2 1.1 copy-start.6
  309.2 1.5 copy-start.9
  324.5 7.4 %copy-start.1 = (f32[1,64,256]{2,1,0:T(8,128)S(1)}, f32[1,64,256]{2,1,0:T(8,128)}, u32[]{:S(2)}) copy-start(f32[1,64,256]{2,1,0:T(8,128)} %param.13) | copy-start | bytes 196612
Sparse Core Ops, SparseCore 0:
  10.1 27.3 all-gather.12
  42.0 17.8 all-gather.14
  65.6 17.8 all-gather.16
  236.9 22.7 all-gather.18
  284.5 15.0 all-gather.20
  306.6 17.8 all-gather.22
where the time goes:
time: 340 us; the launch traced here: 339 us
  waiting for transfers between devices  224 us (66%)
  local copies, waits for them, and re-layouts  42.3 us (12%)
  matrix products  26.5 us (8%)
  between operations  16.3 us (5%)
  starting transfers between devices  14.8 us (4%)
  other arithmetic  9.17 us (3%)
  blocking collectives  5.92 us (2%)
    ppermute x9, waiting for transfers between devices, partner(): return lax.ppermute(value, axis, pairs)  112 us
    all_gather x3, waiting for transfers between devices, local(): lax.all_gather(current, 'row', axis=0, tiled=True)  54.8 us
    all_to_all x1, waiting for transfers between devices, local(): lax.all_to_all(a_panel, 'row', split_axis=1, concat_axis=0, tiled=True)  37.8 us
    unnamed x41, local copies, waits for them, and re-layouts  28.2 us
    all_gather x3, waiting for transfers between devices, local(): lax.all_gather(scaled, 'row', axis=0, tiled=True)  18.7 us
    dot_general x3, matrix products, local(): jnp.dot(a_panel, lax.all_gather(current, 'row', axis=0, tiled=True), pref...  11.7 us
    all_to_all x3, local copies, waits for them, and re-layouts, local(): lax.all_to_all(a_panel, 'row', split_axis=1, concat_axis=0, tiled=True)  11.4 us
    ppermute x9, starting transfers between devices, partner(): return lax.ppermute(value, axis, pairs)  10.7 us
  transfers between devices with their start and end apart: 16, of which 13 were waited for; matrix products, arithmetic and copies ran while one was open for 9% of the time, Pallas kernels for 0%

commit v1 on v0

v1 whole, which is shorter than its diff:
```python
import functools
import math

import jax
import jax.numpy as jnp
from jax import lax
from jax.experimental import pallas as pl
from jax.experimental.pallas import tpu as pltpu
from jax.sharding import PartitionSpec as P

ORDERS = 601
TAYLOR = 3
LEVELS = 3
CHUNKS = 1
LANES = 128
F32 = jnp.float32
BF16 = jnp.bfloat16
WHOLE = pl.BlockSpec(memory_space=pltpu.VMEM)
SCALAR = pl.BlockSpec(memory_space=pltpu.SMEM)


def call(body, out_shape, in_specs, scratch=(), limit=48):
    out_specs = jax.tree.map(lambda _: WHOLE, out_shape)
    return pl.pallas_call(
        body,
        out_shape=out_shape,
        in_specs=in_specs,
        out_specs=out_specs,
        scratch_shapes=list(scratch),
        compiler_params=pltpu.CompilerParams(vmem_limit_bytes=limit * 2**20),
    )


def over_row(value, mask):
    pairs = [(source, source ^ mask) for source in range(lax.axis_size("row"))]
    return lax.ppermute(value, "row", pairs)


def over_cuts(value):
    size = lax.axis_size("cuts")
    group = 2**LEVELS
    groups = None
    if size != group:
        groups = [list(range(first, first + group)) for first in range(0, size, group)]
    return lax.all_to_all(value, "cuts", 0, 0, axis_index_groups=groups, tiled=True)


def operator_blocks(me_ref, a_ref, out_ref):
    rows, full = a_ref.shape
    out_ref[...] = jnp.zeros_like(out_ref)
    for block in range(full // rows):
        out_ref[me_ref[0] ^ block, :rows, :rows] = a_ref[:, block * rows : (block + 1) * rows]


def turned(x_ref, out_ref, tall):
    rows = x_ref.shape[0]
    tall[rows:, :] = jnp.zeros_like(tall[rows:, :])
    tall[:rows, :] = x_ref[...].astype(F32)
    out_ref[...] = tall[...].T.astype(BF16)


def coupling(chunks, reflect_ref, cotangent_ref, out_ref, tall):
    levels, rows, columns = reflect_ref.shape
    pad = tall.shape[0]
    group = 2**levels
    part = columns // chunks // group
    tall[rows:, :] = jnp.zeros_like(tall[rows:, :])
    cot = cotangent_ref[...].T
    high = cot.astype(BF16)
    low = (cot - high.astype(F32)).astype(BF16)
    tracked = cot.shape[1]
    for piece, first in [(high, levels * pad), (low, levels * pad + tracked)]:
        for chunk in range(chunks):
            for peer in range(group):
                at = (chunk * group + peer) * part
                out_ref[peer, chunk, :, first : first + tracked] = piece[at : at + part]
    for level in range(levels):
        tall[:rows, :] = reflect_ref[level]
        flat = tall[...].T.astype(BF16)
        for chunk in range(chunks):
            for peer in range(group):
                at = (chunk * group + peer) * part
                out_ref[peer, chunk, :, level * pad : (level + 1) * pad] = flat[at : at + part]


def merge(levels, w_ref, rc_ref, onehot_ref, field_ref, cmap_ref, sums_ref):
    group, part, pad = w_ref.shape
    totals = []
    merged = [w_ref[s].astype(F32) for s in range(group)]
    for level in range(levels):
        sent = [
            rc_ref[s, :, level * pad : (level + 1) * pad].astype(F32) * merged[s] for s in range(group)
        ]
        merged = [merged[s] + sent[s ^ 2**level] for s in range(group)]
    lane = lax.broadcasted_iota(jnp.int32, (part, LANES), 1)
    for s in range(group):
        field = merged[s]
        cmap = jnp.dot(rc_ref[s, :, levels * pad :], onehot_ref[...], preferred_element_type=F32)
        squared = field * field
        power = jnp.sum(squared, axis=1, keepdims=True)
        weighted = jnp.sum(cmap * squared, axis=1, keepdims=True)
        field_ref[s] = field
        cmap_ref[s] = cmap
        totals.append(jnp.where(lane == 0, power, jnp.where(lane == 1, weighted, 0.0)))
    sums_ref[...] = jnp.concatenate(totals, axis=0).T[: sums_ref.shape[0]]


def unmerge(levels, full, scale, field_ref, cmap_ref, rc_ref, s0, s1, s2, s3, out_ref):
    group, part, pad = field_ref.shape
    sums = (s0[...] + s1[...]) + (s2[...] + s3[...])
    sums = jnp.concatenate([sums] * (LANES // sums.shape[0]), axis=0).T
    grad = []
    for s in range(group):
        power = sums[s * part : (s + 1) * part, 0:1]
        weighted = sums[s * part : (s + 1) * part, 1:2]
        inverse = 1.0 / (power / full + 1e-06)
        first = scale * 2.0 * inverse
        second = scale * 2.0 / full * (weighted * inverse * inverse)
        grad.append((first * cmap_ref[s] - second) * field_ref[s])
    for level in range(levels - 1, -1, -1):
        grad = [
            grad[s]
            + rc_ref[s, :, level * pad : (level + 1) * pad].astype(F32) * grad[s ^ 2**level]
            for s in range(group)
        ]
    for s in range(group):
        out_ref[s] = grad[s].astype(BF16)


def shape(*dims, dtype=F32):
    return jax.ShapeDtypeStruct(dims, dtype)


def times_t(block, panel):
    return lax.dot_general(block, panel, (((1,), (1,)), ((), ())), preferred_element_type=F32)


def times(block, panel):
    return lax.dot_general(block, panel, (((1,), (0,)), ((), ())), preferred_element_type=F32)


def local(operator, incident, reflect, thickness_table, profile, order_index, cotangent):
    rows, full = operator.shape[1:]
    columns = incident.shape[2]
    levels = reflect.shape[1]
    group = 2**levels
    tracked = order_index.shape[0]
    pad = -(-rows // LANES) * LANES
    width = columns // CHUNKS
    part = width // group
    me = lax.axis_index("row")
    me_arr = me.reshape(1)
    step_len = jnp.sum(jnp.where(profile[0] == jnp.arange(thickness_table.shape[0]), thickness_table, 0.0))

    x_t = call(turned, shape(columns, pad, dtype=BF16), [WHOLE], [pltpu.VMEM((pad, columns), F32)])(incident[0])
    rc = call(
        functools.partial(coupling, CHUNKS),
        shape(group, CHUNKS, part, levels * pad + 2 * tracked, dtype=BF16),
        [WHOLE, WHOLE],
        [pltpu.VMEM((pad, columns), F32)],
    )(reflect[0], cotangent[0])
    rc = over_cuts(rc)
    panel = call(operator_blocks, shape(4, pad, pad, dtype=BF16), [SCALAR, WHOLE])(me_arr, operator[0])

    lane_row = jnp.arange(pad, dtype=jnp.int32)
    lane_order = jnp.where(lane_row < rows, (me * rows + lane_row) % ORDERS, -1)
    tracked_twice = jnp.concatenate([order_index, order_index])
    onehot = (tracked_twice[:, None] == lane_order[None, :]).astype(BF16)

    outs = []
    for chunk in range(CHUNKS):
        x = x_t[chunk * width : (chunk + 1) * width]
        x_wide = x.astype(F32)
        current = x
        stored = []
        for degree in range(TAYLOR, 0, -1):
            far = over_row(current, 2)
            core = over_row(current, 1)
            product = times_t(current, panel[0]) + times_t(core, panel[1])
            diag = over_row(far, 1)
            product = product + times_t(far, panel[2])
            product = product + times_t(diag, panel[3])
            stored.append((current, core, far, diag))
            current = (x_wide + step_len / degree * product).astype(BF16)
        swapped = over_cuts(current.reshape(group, part, pad))
        coupled = rc[:, chunk]
        field, cmap, sums = call(
            functools.partial(merge, levels),
            (shape(group, part, pad), shape(group, part, pad), shape(8, group * part)),
            [WHOLE] * 3,
        )(swapped, coupled, onehot)
        s1, s2, s3 = (over_row(sums, mask) for mask in (1, 2, 3))
        grad = call(
            functools.partial(unmerge, levels, full, 1.0 / math.sqrt(columns)),
            shape(group, part, pad, dtype=BF16),
            [WHOLE] * 7,
        )(field, cmap, coupled, sums, s1, s2, s3)
        upstream = over_cuts(grad).reshape(width, pad).astype(F32)
        total = jnp.zeros((width, pad), F32)
        scaled_all = []
        for degree in range(1, TAYLOR + 1):
            total = total + upstream
            scaled = (step_len / degree * upstream).astype(BF16)
            scaled_all.append(scaled)
            diag = over_row(times(scaled, panel[3]).astype(BF16), 1)
            far = times(scaled, panel[2])
            far = over_row((far + diag.astype(F32)).astype(BF16), 2)
            core = over_row(times(scaled, panel[1]).astype(BF16), 1)
            upstream = times(scaled, panel[0]) + core.astype(F32) + far.astype(F32)
        total = total + upstream
        outs.append((total, stored, scaled_all))
    grad_incident = jnp.concatenate([out[0][:, :rows] for out in outs], axis=0).T

    left = jnp.concatenate([scaled for out in outs for scaled in out[2]], axis=0)[:, :rows]
    blocks = []
    for block in range(4):
        pieces = []
        for out in outs:
            for stored in out[1][::-1]:
                pieces.append(lax.dynamic_index_in_dim(jnp.stack(stored), me ^ block, 0, keepdims=False))
        blocks.append(jnp.concatenate(pieces, axis=0)[:, :rows])
    right = jnp.concatenate(blocks, axis=1)
    grad_matrix = lax.dot_general(left, right, (((0,), (0,)), ((), ())), preferred_element_type=F32)
    return (grad_matrix[None], grad_incident[None])


def solution(mesh):
    return jax.shard_map(
        local,
        mesh=mesh,
        in_specs=(
            P("cuts", "row", None),
            P("cuts", "row", None),
            P("cuts", None, "row", None),
            P(),
            P("cuts"),
            P(),
            P("cuts", None, None),
        ),
        out_specs=(P("cuts", "row", None), P("cuts", "row", None)),
        check_vma=False,
    )
```

time: 340 us -> 138 us (0.41)
  waiting for transfers between devices: 224 us -> 44.5 us
  local copies, waits for them, and re-layouts: 42.3 us -> 23.1 us
  between operations: 16.3 us -> 3.32 us
  starting transfers between devices: 14.8 us -> 26.2 us
  Pallas kernels: 0 us -> 6.29 us
  blocking collectives: 5.92 us -> 0 us
  matrix products: 26.5 us -> 22.7 us
    ppermute x9 -> x21, waiting for transfers between devices: 112 us -> 18.2 us  [over_row(): return lax.ppermute(value, 'row', pairs)]
    all_gather x6 -> x0, waiting for transfers between devices: 73.5 us -> none  [the longest x3 54.8 us: local(): lax.all_gather(current, 'row', axis=0, tiled=True)]
    unnamed x41 -> x59, local copies, waits for them, and re-layouts: 28.2 us -> 14.3 us
    all_to_all x1 -> x3, waiting for transfers between devices: 37.8 us -> 26.3 us  [over_cuts(): lax.all_to_all(value, 'cuts', 0, 0, axis_index_groups=groups, tiled=True)]
    all_to_all x3 -> x0, local copies, waits for them, and re-layouts: 11.4 us -> none  [local(): lax.all_to_all(a_panel, 'row', split_axis=1, concat_axis=0, tiled=True)]
    all_to_all x1 -> x3, starting transfers between devices: 3.7 us -> 14.2 us  [over_cuts(): lax.all_to_all(value, 'cuts', 0, 0, axis_index_groups=groups, tiled=True)]
    concatenate x0 -> x1, local copies, waits for them, and re-layouts: none -> 7.45 us  [local(): right = jnp.concatenate(blocks, axis=1)]
    pallas_call x0 -> x5, Pallas kernels: none -> 6.29 us  [the longest x1 2.74 us: local(): call(operator_blocks, shape(4, pad, pad, dtype=BF16), [SCALAR, WHOLE])]
  transfers between devices with their start and end apart: 16 -> 24, of which waited for: 13 -> 7; matrix products, arithmetic and copies ran while one was open for 9% -> 33% of each run, Pallas kernels for 0% -> 3%
where the time goes in v1:
time: 138 us; the launch traced here: 137 us
  waiting for transfers between devices  44.5 us (32%)
  starting transfers between devices  26.2 us (19%)
  local copies, waits for them, and re-layouts  23.1 us (17%)
  matrix products  22.7 us (16%)
  other arithmetic  11.2 us (8%)
  Pallas kernels  6.29 us (5%)
  between operations  3.32 us (2%)
    all_to_all x3, waiting for transfers between devices, over_cuts(): lax.all_to_all(value, 'cuts', 0, 0, axis_index_groups=groups, tiled=True)  26.3 us
    ppermute x21, waiting for transfers between devices, over_row(): return lax.ppermute(value, 'row', pairs)  18.2 us
    unnamed x59, local copies, waits for them, and re-layouts  14.3 us
    all_to_all x3, starting transfers between devices, over_cuts(): lax.all_to_all(value, 'cuts', 0, 0, axis_index_groups=groups, tiled=True)  14.2 us
    ppermute x21, starting transfers between devices, over_row(): return lax.ppermute(value, 'row', pairs)  12 us
    dot_general x12, matrix products, times_t(): lax.dot_general(block, panel, (((1,), (1,)), ((), ())), preferred_element...  11.9 us
    dot_general x12, matrix products, times(): lax.dot_general(block, panel, (((1,), (0,)), ((), ())), preferred_element...  8.18 us
    concatenate x1, local copies, waits for them, and re-layouts, local(): right = jnp.concatenate(blocks, axis=1)  7.45 us
  transfers between devices with their start and end apart: 24, of which 7 were waited for; matrix products, arithmetic and copies ran while one was open for 33% of the time, Pallas kernels for 3%

profile of v1, /device:TPU:0, one launch (start us, length us, event | category | flops | bytes accessed | tf_op | source)
XLA Modules:
  0.0 137.3 jit_solution(13008645924086680861)
XLA Ops:
  1.8 3.0 %collective-permute-start.1 = (bf16[256,640]{1,0:T(8,128)(2,1)S(1)}, bf16[256,640]{1,0:T(8,128)(2,1)S(1)}, u32[]{:S(2)}, u32[]{:S(2)}) collective-permute-start(bf16[256,640]{1,0:T(8,128)(2,1)S(1)} %shard_map.86), channel_id=1, source_target_pairs={{0,2},{1,3},{2,0},{3,1},{4,6},{5,7},{6,4},{7,5},{8,10},{9,11},{10,... | collective-permute-start | bytes 983048 | tf_op jit(solution)/shard_map/ppermute | solution.py:36
  5.5 1.3 fusion.27
  7.5 1.8 %copy-done = bf16[1,601,2404]{2,1,0:T(8,128)(2,1)S(1)} copy-done((bf16[1,601,2404]{2,1,0:T(8,128)(2,1)S(1)}, bf16[1,601,2404]{2,1,0:T(8,128)(2,1)}, u32[]{:S(2)}) %copy-start) | copy-done | bytes 2889632
  9.3 2.7 %shard_map.87 = bf16[4,640,640]{2,1,0:T(8,128)(2,1)} custom-call(s32[1]{0:T(128)} %bitcast.2.me_ref, bf16[601,2404]{1,0:T(8,128)(2,1)S(1)} %bitcast.127), custom_call_target="tpu_custom_call" | custom-call | tf_op jit(solution)/shard_map/pallas_call | solution.py:163
  12.1 1.8 %fusion.21 = f32[640,256]{0,1:T(8,128)S(1)} fusion(bf16[256,640]{1,0:T(8,128)(2,1)S(1)} %shard_map.86, bf16[4,640,640]{2,1,0:T(8,128)(2,1)} %shard_map.87), kind=kOutput, calls=%fused_computation.67 | convolution fusion | flops 209715200 | bytes 1802240 | tf_op jit(solution)/shard_map/dot_general | solution.py:135
  14.4 1.6 %convolution_add_fusion.11 = f32[640,256]{0,1:T(8,128)S(1)} fusion(f32[640,256]{0,1:T(8,128)S(1)} %fusion.21, bf16[256,640]{1,0:T(8,128)(2,1)S(1)} %collective-permute-done, bf16[4,640,640]{2,1,0:T(8,128)(2,1)} %shard_map.87), kind=kOutput, calls=%fused_computation.16 | convolution fusion | flops 209879040 | bytes 2457600 | tf_op jit(solution)/shard_map/dot_general | solution.py:135
  17.5 1.5 %shard_map.88 = bf16[8,1,32,2048]{3,2,1,0:T(8,128)(2,1)} custom-call(f32[3,601,256]{2,1,0:T(8,128)S(1)} %bitcast.126, f32[64,256]{1,0:T(8,128)S(1)} %bitcast.129), custom_call_target="tpu_custom_call" | custom-call | tf_op jit(solution)/shard_map/pallas_call | solution.py:156
  19.0 6.1 %all-to-all-start.1 = ((bf16[8,1,32,2048]{3,2,1,0:T(8,128)(2,1)}), bf16[8,1,32,2048]{3,2,1,0:T(8,128)(2,1)S(1)}, u32[]{:S(2)}, u32[]{:S(2)}) async-start(bf16[8,1,32,2048]{3,2,1,0:T(8,128)(2,1)} %shard_map.88), calls=%async_computation.1 | async-start | bytes 2097152 | tf_op jit(solution)/shard_map/all_to_all | solution.py:45
  25.8 1.7 %fusion.20 = f32[256,640]{1,0:T(8,128)S(1)} fusion(bf16[256,640]{1,0:T(8,128)(2,1)S(1)} %fusion.12, bf16[4,640,640]{2,1,0:T(8,128)(2,1)} %shard_map.87), kind=kOutput, calls=%fused_computation.66 | convolution fusion | flops 209715200 | bytes 1802240 | tf_op jit(solution)/shard_map/dot_general | solution.py:135
  27.9 1.7 %convolution_add_fusion.8 = f32[256,640]{1,0:T(8,128)S(1)} fusion(f32[256,640]{1,0:T(8,128)S(1)} %fusion.20, bf16[256,640]{1,0:T(8,128)(2,1)S(1)} %collective-permute-done.3, bf16[4,640,640]{2,1,0:T(8,128)(2,1)} %shard_map.87), kind=kOutput, calls=%fused_computation.13 | convolution fusion | flops 209879040 | bytes 2457600 | tf_op jit(solution)/shard_map/dot_general | solution.py:135
  30.6 1.6 %collective-permute-start.7 = (bf16[256,640]{1,0:T(8,128)(2,1)S(1)}, bf16[256,640]{1,0:T(8,128)(2,1)S(1)}, u32[]{:S(2)}, u32[]{:S(2)}) collective-permute-start(bf16[256,640]{1,0:T(8,128)(2,1)S(1)} %fusion.11), channel_id=1, source_target_pairs={{0,2},{1,3},{2,0},{3,1},{4,6},{5,7},{6,4},{7,5},{8,10},{9,11},{10,... | collective-permute-start | bytes 983048 | tf_op jit(solution)/shard_map/ppermute | solution.py:36
  32.7 7.9 %collective-permute-done.7 = bf16[256,640]{1,0:T(8,128)(2,1)S(1)} collective-permute-done((bf16[256,640]{1,0:T(8,128)(2,1)S(1)}, bf16[256,640]{1,0:T(8,128)(2,1)S(1)}, u32[]{:S(2)}, u32[]{:S(2)}) %collective-permute-start.7) | collective-permute-done | bytes 327712 | tf_op jit(solution)/shard_map/ppermute | solution.py:36
  43.1 1.9 %fusion.10 = bf16[256,640]{1,0:T(8,128)(2,1)} fusion(f32[256,640]{1,0:T(8,128)S(1)} %convolution_add_fusion.4, bf16[256,640]{1,0:T(8,128)(2,1)S(1)} %collective-permute-done.8, bf16[256,640]{1,0:T(8,128)(2,1)S(1)} %shard_map.86, bf16[4,640,640]{2,1,0:T(8,128)(2,1)S(1)} %copy-done.4, f32[]{:T(128)} %fusion.27), kind=kOutput, calls=%fused_computation.27 | convolution fusion | flops 210534400 | bytes 2457604 | tf_op jit(solution)/shard_map/dot_general | solution.py:135
  44.9 6.6 %all-to-all-done.1 = bf16[8,1,32,2048]{3,2,1,0:T(8,128)(2,1)S(1)} async-done(((bf16[8,1,32,2048]{3,2,1,0:T(8,128)(2,1)}), bf16[8,1,32,2048]{3,2,1,0:T(8,128)(2,1)S(1)}, u32[]{:S(2)}, u32[]{:S(2)}) %all-to-all-start.1) | async-done | bytes 1048608 | tf_op jit(solution)/shard_map/all_to_all | solution.py:45
  51.5 3.6 %all-to-all-start = ((bf16[8,32,640]{2,1,0:T(8,128)(2,1)}), bf16[8,32,640]{2,1,0:T(8,128)(2,1)S(1)}, u32[]{:S(2)}, u32[]{:S(2)}) async-start(bf16[8,32,640]{2,1,0:T(8,128)(2,1)} %bitcast.9), calls=%async_computation | async-start | bytes 655360 | tf_op jit(solution)/shard_map/all_to_all | solution.py:45
  55.4 10.3 %all-to-all-done.w_ref = bf16[8,32,640]{2,1,0:T(8,128)(2,1)S(1)} async-done(((bf16[8,32,640]{2,1,0:T(8,128)(2,1)}), bf16[8,32,640]{2,1,0:T(8,128)(2,1)S(1)}, u32[]{:S(2)}, u32[]{:S(2)}) %all-to-all-start) | async-done | bytes 327712 | tf_op jit(solution)/shard_map/all_to_all | solution.py:45
  66.3 1.6 %collective-permute-start.10 = (f32[8,256]{1,0:T(8,128)S(1)}, f32[8,256]{1,0:T(8,128)S(1)}, u32[]{:S(2)}, u32[]{:S(2)}) collective-permute-start(f32[8,256]{1,0:T(8,128)S(1)} %get-tuple-element.7.s0), channel_id=1, source_target_pairs={{0,2},{1,3},{2,0},{3,1},{4,6},{5,7},{6,4},{7,5},{8,10},{9,11},{10,... | collective-permute-start | bytes 24584 | tf_op jit(solution)/shard_map/ppermute | solution.py:36
  68.2 1.2 collective-permute-done.11.s3
  70.1 1.3 shard_map.90
  71.3 4.5 %all-to-all-start.2 = ((bf16[8,32,640]{2,1,0:T(8,128)(2,1)}), bf16[8,32,640]{2,1,0:T(8,128)(2,1)}, u32[]{:S(2)}, u32[]{:S(2)}) async-start(bf16[8,32,640]{2,1,0:T(8,128)(2,1)} %shard_map.90), calls=%async_computation.2 | async-start | bytes 655360 | tf_op jit(solution)/shard_map/all_to_all | solution.py:45
  77.1 9.5 %all-to-all-done.2 = bf16[8,32,640]{2,1,0:T(8,128)(2,1)} async-done(((bf16[8,32,640]{2,1,0:T(8,128)(2,1)}), bf16[8,32,640]{2,1,0:T(8,128)(2,1)}, u32[]{:S(2)}, u32[]{:S(2)}) %all-to-all-start.2) | async-done | bytes 327712 | tf_op jit(solution)/shard_map/all_to_all | solution.py:45
  86.5 1.7 %multiply_convert_fusion.2 = bf16[8,32,640]{2,1,0:T(8,128)(2,1)S(1)} fusion(f32[]{:T(128)} %fusion.27, bf16[8,32,640]{2,1,0:T(8,128)(2,1)} %all-to-all-done.2), kind=kLoop, calls=%fused_computation.61 | loop fusion | flops 491520 | bytes 655364 | tf_op jit(solution)/shard_map/convert_element_type | solution.py:203
  88.8 1.5 %pad_maximum_fusion.1 = bf16[4,256,640]{2,1,0:T(8,128)(2,1)S(1)} fusion(bf16[1,256,640]{2,1,0:T(8,128)(2,1)} %bitcast.145, bf16[1,256,640]{2,1,0:T(8,128)(2,1)} %bitcast.137, bf16[1,256,640]{2,1,0:T(8,128)(2,1)} %bitcast.138, bf16[1,256,640]{2,1,0:T(8,128)(2,1)} %bitcast.131), kind=kLoop, calls=%fused_computation.3 | loop fusion | flops 1966080 | bytes 2621440 | tf_op jit(solution)/shard_map/stack | solution.py:220
  93.1 8.4 %collective-permute-done.14 = bf16[256,640]{1,0:T(8,128)(2,1)S(1)} collective-permute-done((bf16[256,640]{1,0:T(8,128)(2,1)S(1)}, bf16[256,640]{1,0:T(8,128)(2,1)S(1)}, u32[]{:S(2)}, u32[]{:S(2)}) %collective-permute-start.14) | collective-permute-done | bytes 327712 | tf_op jit(solution)/shard_map/ppermute | solution.py:36
  106.9 1.5 %pad_maximum_fusion.3 = (bf16[768,601]{1,0:T(8,128)(2,1)}, bf16[768,601]{1,0:T(8,128)(2,1)}) fusion(bf16[256,640]{1,0:T(8,128)(2,1)S(1)} %copy-done.25, bf16[256,640]{1,0:T(8,128)(2,1)S(1)} %get-tuple-element.20, bf16[256,640]{1,0:T(8,128)(2,1)S(1)} %get-tuple-element.16, bf16[256,640]{1,0:T(8,128)(2,1)S(1)} %copy-done.26, ...), kind=kLoop, calls=%fused_computation.36 | loop fusion | flops 5538816 | bytes 3812352 | tf_op jit(solution)/shard_map/concatenate | solution.py:221
  108.3 1.5 %pad_maximum_fusion.7 = (bf16[768,601]{1,0:T(8,128)(2,1)}, bf16[768,601]{1,0:T(8,128)(2,1)}) fusion(bf16[256,640]{1,0:T(8,128)(2,1)S(1)} %copy-done.23, bf16[256,640]{1,0:T(8,128)(2,1)S(1)} %get-tuple-element.22, bf16[256,640]{1,0:T(8,128)(2,1)S(1)} %get-tuple-element.18, bf16[256,640]{1,0:T(8,128)(2,1)S(1)} %copy-done.24, ...), kind=kLoop, calls=%fused_computation.40 | loop fusion | flops 5538816 | bytes 3812352 | tf_op jit(solution)/shard_map/concatenate | solution.py:221
  109.8 7.5 %concatenate.27 = bf16[768,2404]{1,0:T(8,128)(2,1)} concatenate(bf16[768,601]{1,0:T(8,128)(2,1)} %get-tuple-element.33, bf16[768,601]{1,0:T(8,128)(2,1)} %get-tuple-element.32, bf16[768,601]{1,0:T(8,128)(2,1)} %get-tuple-element.31, bf16[768,601]{1,0:T(8,128)(2,1)} %get-tuple-element.30), dimensions={1} | concatenate | bytes 7385088 | tf_op jit(solution)/shard_map/concatenate | solution.py:222
  117.3 1.7 %multiply_convert_fusion = (bf16[256,640]{1,0:T(8,128)(2,1)S(1)}, f32[256,640]{1,0:T(8,128)S(1)}) fusion(f32[]{:T(128)S(6)} %div.5, bf16[256,640]{1,0:T(8,128)(2,1)} %collective-permute-done.17, bf16[256,640]{1,0:T(8,128)(2,1)} %collective-permute-done.15, bf16[256,640]{1,0:T(8,128)(2,1)} %copy-done.7, bf16[4,640,640]{2,1,0:T(8,128)(2,1)S(1)} %copy-done.5), kind=kOutput, calls=%fused_computation.57 | convolution fusion | flops 210698240 | bytes 2785284 | tf_op jit(solution)/shard_map/dot_general | solution.py:139
  119.5 2.0 %multiply_convert_fusion.3 = (bf16[256,640]{1,0:T(8,128)(2,1)S(1)}, f32[8,32,640]{2,1,0:T(8,128)S(1)}) fusion(f32[]{:T(128)} %fusion.27, bf16[8,32,640]{2,1,0:T(8,128)(2,1)} %all-to-all-done.2), kind=kLoop, calls=%fused_computation.62 | loop fusion | flops 491520 | bytes 1310724 | tf_op jit(solution)/shard_map/convert_element_type | solution.py:203
  122.7 1.5 %collective-permute-start.20 = (bf16[256,640]{1,0:T(8,128)(2,1)S(1)}, bf16[256,640]{1,0:T(8,128)(2,1)S(1)}, u32[]{:S(2)}, u32[]{:S(2)}) collective-permute-start(bf16[256,640]{1,0:T(8,128)(2,1)S(1)} %fusion.9), channel_id=1, source_target_pairs={{0,2},{1,3},{2,0},{3,1},{4,6},{5,7},{6,4},{7,5},{8,10},{9,11},{10,... | collective-permute-start | bytes 983048 | tf_op jit(solution)/shard_map/ppermute | solution.py:36
  124.2 2.6 %convolution_bitcast_fusion = f32[1,601,2404]{2,1,0:T(8,128)S(1)} fusion(bf16[768,2404]{1,0:T(8,128)(2,1)S(1)} %copy-done.6, bf16[256,640]{1,0:T(8,128)(2,1)S(1)} %get-tuple-element.28, bf16[256,640]{1,0:T(8,128)(2,1)S(1)} %copy-done.8, bf16[256,640]{1,0:T(8,128)(2,1)S(1)} %get-tuple-element.12), kind=kOutput, calls=%fused_computation | convolution fusion | flops 2221988352 | bytes 10454800 | tf_op jit(solution)/shard_map/dot_general | solution.py:223
  126.8 8.6 %copy.14 = f32[1,601,2404]{2,0,1:T(1,128)} copy(f32[1,601,2404]{2,1,0:T(8,128)S(1)} %convolution_bitcast_fusion) | data formatting | bytes 11558432
  (122 shorter events, 22.5 us)
Async XLA Ops:
  1.8 12.1 %collective-permute-start.1 = (bf16[256,640]{1,0:T(8,128)(2,1)S(1)}, bf16[256,640]{1,0:T(8,128)(2,1)S(1)}, u32[]{:S(2)}, u32[]{:S(2)}) collective-permute-start(bf16[256,640]{1,0:T(8,128)(2,1)S(1)} %shard_map.86), channel_id=1, source_target_pairs={{0,2},{1,3},{2,0},{3,1},{4,6},{5,7},{6,4},{7,5},{8,10},{9,11},{10,... | collective-permute-start | bytes 983048 | tf_op jit(solution)/shard_map/ppermute | solution.py:36
  4.8 9.6 %collective-permute-start = (bf16[256,640]{1,0:T(8,128)(2,1)S(1)}, bf16[256,640]{1,0:T(8,128)(2,1)S(1)}, u32[]{:S(2)}, u32[]{:S(2)}) collective-permute-start(bf16[256,640]{1,0:T(8,128)(2,1)S(1)} %shard_map.86), channel_id=1, source_target_pairs={{0,1},{1,0},{2,3},{3,2},{4,5},{5,4},{6,7},{7,6},{8,9},{9,8},{10,11... | collective-permute-start | bytes 983048 | tf_op jit(solution)/shard_map/ppermute | solution.py:36
  13.9 2.7 %collective-permute-start.2 = (bf16[256,640]{1,0:T(8,128)(2,1)S(1)}, bf16[256,640]{1,0:T(8,128)(2,1)S(1)}, u32[]{:S(2)}, u32[]{:S(2)}) collective-permute-start(bf16[256,640]{1,0:T(8,128)(2,1)S(1)} %collective-permute-done.1), channel_id=1, source_target_pairs={{0,1},{1,0},{2,3},{3,2},{4,5},{5,4},{6,7},{7,6},{8,9},{9,8},{10,11... | collective-permute-start | bytes 983048 | tf_op jit(solution)/shard_map/ppermute | solution.py:36
  17.0 10.5 %collective-permute-start.4 = (bf16[256,640]{1,0:T(8,128)(2,1)S(1)}, bf16[256,640]{1,0:T(8,128)(2,1)S(1)}, u32[]{:S(2)}, u32[]{:S(2)}) collective-permute-start(bf16[256,640]{1,0:T(8,128)(2,1)S(1)} %fusion.12), channel_id=1, source_target_pairs={{0,2},{1,3},{2,0},{3,1},{4,6},{5,7},{6,4},{7,5},{8,10},{9,11},{10,... | collective-permute-start | bytes 983048 | tf_op jit(solution)/shard_map/ppermute | solution.py:36
  17.2 10.7 %collective-permute-start.3 = (bf16[256,640]{1,0:T(8,128)(2,1)S(1)}, bf16[256,640]{1,0:T(8,128)(2,1)S(1)}, u32[]{:S(2)}, u32[]{:S(2)}) collective-permute-start(bf16[256,640]{1,0:T(8,128)(2,1)S(1)} %fusion.12), channel_id=1, source_target_pairs={{0,1},{1,0},{2,3},{3,2},{4,5},{5,4},{6,7},{7,6},{8,9},{9,8},{10,11... | collective-permute-start | bytes 983048 | tf_op jit(solution)/shard_map/ppermute | solution.py:36
  19.0 32.5 %all-to-all-start.1 = ((bf16[8,1,32,2048]{3,2,1,0:T(8,128)(2,1)}), bf16[8,1,32,2048]{3,2,1,0:T(8,128)(2,1)S(1)}, u32[]{:S(2)}, u32[]{:S(2)}) async-start(bf16[8,1,32,2048]{3,2,1,0:T(8,128)(2,1)} %shard_map.88), calls=%async_computation.1 | async-start | bytes 2097152 | tf_op jit(solution)/shard_map/all_to_all | solution.py:45
  27.6 2.5 %collective-permute-start.5 = (bf16[256,640]{1,0:T(8,128)(2,1)S(1)}, bf16[256,640]{1,0:T(8,128)(2,1)S(1)}, u32[]{:S(2)}, u32[]{:S(2)}) collective-permute-start(bf16[256,640]{1,0:T(8,128)(2,1)S(1)} %collective-permute-done.4), channel_id=1, source_target_pairs={{0,1},{1,0},{2,3},{3,2},{4,5},{5,4},{6,7},{7,6},{8,9},{9,8},{10,11... | collective-permute-start | bytes 983048 | tf_op jit(solution)/shard_map/ppermute | solution.py:36
  30.6 11.7 %copy-start.9 = (bf16[256,640]{1,0:T(8,128)(2,1)}, bf16[256,640]{1,0:T(8,128)(2,1)S(1)}, u32[]{:S(2)}) copy-start(bf16[256,640]{1,0:T(8,128)(2,1)S(1)} %fusion.11) | copy-start | bytes 983044
  30.6 10.0 %collective-permute-start.7 = (bf16[256,640]{1,0:T(8,128)(2,1)S(1)}, bf16[256,640]{1,0:T(8,128)(2,1)S(1)}, u32[]{:S(2)}, u32[]{:S(2)}) collective-permute-start(bf16[256,640]{1,0:T(8,128)(2,1)S(1)} %fusion.11), channel_id=1, source_target_pairs={{0,2},{1,3},{2,0},{3,1},{4,6},{5,7},{6,4},{7,5},{8,10},{9,11},{10,... | collective-permute-start | bytes 983048 | tf_op jit(solution)/shard_map/ppermute | solution.py:36
  32.2 8.4 %collective-permute-start.6 = (bf16[256,640]{1,0:T(8,128)(2,1)S(1)}, bf16[256,640]{1,0:T(8,128)(2,1)S(1)}, u32[]{:S(2)}, u32[]{:S(2)}) collective-permute-start(bf16[256,640]{1,0:T(8,128)(2,1)S(1)} %fusion.11), channel_id=1, source_target_pairs={{0,1},{1,0},{2,3},{3,2},{4,5},{5,4},{6,7},{7,6},{8,9},{9,8},{10,11... | collective-permute-start | bytes 983048 | tf_op jit(solution)/shard_map/ppermute | solution.py:36
  40.6 1.7 %collective-permute-start.8 = (bf16[256,640]{1,0:T(8,128)(2,1)S(1)}, bf16[256,640]{1,0:T(8,128)(2,1)S(1)}, u32[]{:S(2)}, u32[]{:S(2)}) collective-permute-start(bf16[256,640]{1,0:T(8,128)(2,1)S(1)} %collective-permute-done.7), channel_id=1, source_target_pairs={{0,1},{1,0},{2,3},{3,2},{4,5},{5,4},{6,7},{7,6},{8,9},{9,8},{10,11... | collective-permute-start | bytes 983048 | tf_op jit(solution)/shard_map/ppermute | solution.py:36
  41.8 13.4 %copy-start.27 = (s32[64]{0:T(128)S(1)}, s32[64]{0:T(128)}, u32[]{:S(2)}) copy-start(s32[64]{0:T(128)} %param.12) | copy-start | bytes 772
  51.5 14.1 %all-to-all-start = ((bf16[8,32,640]{2,1,0:T(8,128)(2,1)}), bf16[8,32,640]{2,1,0:T(8,128)(2,1)S(1)}, u32[]{:S(2)}, u32[]{:S(2)}) async-start(bf16[8,32,640]{2,1,0:T(8,128)(2,1)} %bitcast.9), calls=%async_computation | async-start | bytes 655360 | tf_op jit(solution)/shard_map/all_to_all | solution.py:45
  66.3 3.1 %collective-permute-start.11 = (f32[8,256]{1,0:T(8,128)S(1)}, f32[8,256]{1,0:T(8,128)S(1)}, u32[]{:S(2)}, u32[]{:S(2)}) collective-permute-start(f32[8,256]{1,0:T(8,128)S(1)} %get-tuple-element.7.s0), channel_id=1, source_target_pairs={{0,3},{1,2},{2,1},{3,0},{4,7},{5,6},{6,5},{7,4},{8,11},{9,10},{10,... | collective-permute-start | bytes 24584 | tf_op jit(solution)/shard_map/ppermute | solution.py:36
  66.3 3.7 %collective-permute-start.10 = (f32[8,256]{1,0:T(8,128)S(1)}, f32[8,256]{1,0:T(8,128)S(1)}, u32[]{:S(2)}, u32[]{:S(2)}) collective-permute-start(f32[8,256]{1,0:T(8,128)S(1)} %get-tuple-element.7.s0), channel_id=1, source_target_pairs={{0,2},{1,3},{2,0},{3,1},{4,6},{5,7},{6,4},{7,5},{8,10},{9,11},{10,... | collective-permute-start | bytes 24584 | tf_op jit(solution)/shard_map/ppermute | solution.py:36
  67.9 2.1 %collective-permute-start.9 = (f32[8,256]{1,0:T(8,128)S(1)}, f32[8,256]{1,0:T(8,128)S(1)}, u32[]{:S(2)}, u32[]{:S(2)}) collective-permute-start(f32[8,256]{1,0:T(8,128)S(1)} %get-tuple-element.7.s0), channel_id=1, source_target_pairs={{0,1},{1,0},{2,3},{3,2},{4,5},{5,4},{6,7},{7,6},{8,9},{9,8},{10,11... | collective-permute-start | bytes 24584 | tf_op jit(solution)/shard_map/ppermute | solution.py:36
  71.3 15.2 %all-to-all-start.2 = ((bf16[8,32,640]{2,1,0:T(8,128)(2,1)}), bf16[8,32,640]{2,1,0:T(8,128)(2,1)}, u32[]{:S(2)}, u32[]{:S(2)}) async-start(bf16[8,32,640]{2,1,0:T(8,128)(2,1)} %shard_map.90), calls=%async_computation.2 | async-start | bytes 655360 | tf_op jit(solution)/shard_map/all_to_all | solution.py:45
  76.0 12.3 %copy-start.5 = (bf16[4,640,640]{2,1,0:T(8,128)(2,1)S(1)}, bf16[4,640,640]{2,1,0:T(8,128)(2,1)}, u32[]{:S(2)}) copy-start(bf16[4,640,640]{2,1,0:T(8,128)(2,1)} %shard_map.87) | copy-start | bytes 9830404
  88.7 2.6 %collective-permute-start.13 = (bf16[256,640]{1,0:T(8,128)(2,1)S(1)}, bf16[256,640]{1,0:T(8,128)(2,1)S(1)}, u32[]{:S(2)}, u32[]{:S(2)}) collective-permute-start(bf16[256,640]{1,0:T(8,128)(2,1)S(1)} %convolution_convert_fusion.4), channel_id=1, source_target_pairs={{0,1},{1,0},{2,3},{3,2},{4,5},{5,4},{6,7},{7,6},{8,9},{9,8},{10,11... | collective-permute-start | bytes 983048 | tf_op jit(solution)/shard_map/ppermute | solution.py:36
  90.7 2.3 %collective-permute-start.12 = (bf16[256,640]{1,0:T(8,128)(2,1)S(1)}, bf16[256,640]{1,0:T(8,128)(2,1)S(1)}, u32[]{:S(2)}, u32[]{:S(2)}) collective-permute-start(bf16[256,640]{1,0:T(8,128)(2,1)S(1)} %convolution_convert_fusion.5), channel_id=1, source_target_pairs={{0,1},{1,0},{2,3},{3,2},{4,5},{5,4},{6,7},{7,6},{8,9},{9,8},{10,11... | collective-permute-start | bytes 983048 | tf_op jit(solution)/shard_map/ppermute | solution.py:36
  91.8 9.7 %collective-permute-start.14 = (bf16[256,640]{1,0:T(8,128)(2,1)S(1)}, bf16[256,640]{1,0:T(8,128)(2,1)S(1)}, u32[]{:S(2)}, u32[]{:S(2)}) collective-permute-start(bf16[256,640]{1,0:T(8,128)(2,1)S(1)} %add_convert_fusion), channel_id=1, source_target_pairs={{0,2},{1,3},{2,0},{3,1},{4,6},{5,7},{6,4},{7,5},{8,10},{9,11},{10,... | collective-permute-start | bytes 983048 | tf_op jit(solution)/shard_map/ppermute | solution.py:36
  92.6 10.4 %copy-start.10 = (bf16[256,640]{1,0:T(8,128)(2,1)S(1)}, bf16[256,640]{1,0:T(8,128)(2,1)}, u32[]{:S(2)}) copy-start(bf16[256,640]{1,0:T(8,128)(2,1)} %copy-done.9) | copy-start | bytes 983044
  92.6 10.4 %copy-start.15 = (bf16[256,640]{1,0:T(8,128)(2,1)S(1)}, bf16[256,640]{1,0:T(8,128)(2,1)}, u32[]{:S(2)}) copy-start(bf16[256,640]{1,0:T(8,128)(2,1)} %copy-done.14) | copy-start | bytes 983044
  92.6 10.4 %copy-start.17 = (bf16[256,640]{1,0:T(8,128)(2,1)S(1)}, bf16[256,640]{1,0:T(8,128)(2,1)}, u32[]{:S(2)}) copy-start(bf16[256,640]{1,0:T(8,128)(2,1)} %copy-done.16) | copy-start | bytes 983044
  92.6 10.4 %copy-start.21 = (bf16[256,640]{1,0:T(8,128)(2,1)S(1)}, bf16[256,640]{1,0:T(8,128)(2,1)}, u32[]{:S(2)}) copy-start(bf16[256,640]{1,0:T(8,128)(2,1)} %copy-done.20) | copy-start | bytes 983044
  102.9 2.0 %collective-permute-start.16 = (bf16[256,640]{1,0:T(8,128)(2,1)S(1)}, bf16[256,640]{1,0:T(8,128)(2,1)S(1)}, u32[]{:S(2)}, u32[]{:S(2)}) collective-permute-start(bf16[256,640]{1,0:T(8,128)(2,1)S(1)} %convolution_convert_fusion.2), channel_id=1, source_target_pairs={{0,1},{1,0},{2,3},{3,2},{4,5},{5,4},{6,7},{7,6},{8,9},{9,8},{10,11... | collective-permute-start | bytes 983048 | tf_op jit(solution)/shard_map/ppermute | solution.py:36
  104.4 12.8 %collective-permute-start.15 = (bf16[256,640]{1,0:T(8,128)(2,1)}, bf16[256,640]{1,0:T(8,128)(2,1)}, u32[]{:S(2)}, u32[]{:S(2)}) collective-permute-start(bf16[256,640]{1,0:T(8,128)(2,1)} %convolution_convert_fusion.3), channel_id=1, source_target_pairs={{0,1},{1,0},{2,3},{3,2},{4,5},{5,4},{6,7},{7,6},{8,9},{9,8},{10,11... | collective-permute-start | bytes 983048 | tf_op jit(solution)/shard_map/ppermute | solution.py:36
  106.1 11.2 %collective-permute-start.17 = (bf16[256,640]{1,0:T(8,128)(2,1)}, bf16[256,640]{1,0:T(8,128)(2,1)}, u32[]{:S(2)}, u32[]{:S(2)}) collective-permute-start(bf16[256,640]{1,0:T(8,128)(2,1)} %fusion.8), channel_id=1, source_target_pairs={{0,2},{1,3},{2,0},{3,1},{4,6},{5,7},{6,4},{7,5},{8,10},{9,11},{10,... | collective-permute-start | bytes 983048 | tf_op jit(solution)/shard_map/ppermute | solution.py:36
  119.4 2.8 %collective-permute-start.19 = (bf16[256,640]{1,0:T(8,128)(2,1)S(1)}, bf16[256,640]{1,0:T(8,128)(2,1)S(1)}, u32[]{:S(2)}, u32[]{:S(2)}) collective-permute-start(bf16[256,640]{1,0:T(8,128)(2,1)S(1)} %convolution_convert_fusion), channel_id=1, source_target_pairs={{0,1},{1,0},{2,3},{3,2},{4,5},{5,4},{6,7},{7,6},{8,9},{9,8},{10,11... | collective-permute-start | bytes 983048 | tf_op jit(solution)/shard_map/ppermute | solution.py:36
  122.0 14.0 %collective-permute-start.18 = (bf16[256,640]{1,0:T(8,128)(2,1)S(1)}, bf16[256,640]{1,0:T(8,128)(2,1)S(1)}, u32[]{:S(2)}, u32[]{:S(2)}) collective-permute-start(bf16[256,640]{1,0:T(8,128)(2,1)S(1)} %convolution_convert_fusion.1), channel_id=1, source_target_pairs={{0,1},{1,0},{2,3},{3,2},{4,5},{5,4},{6,7},{7,6},{8,9},{9,8},{10,11... | collective-permute-start | bytes 983048 | tf_op jit(solution)/shard_map/ppermute | solution.py:36
  122.7 13.2 %collective-permute-start.20 = (bf16[256,640]{1,0:T(8,128)(2,1)S(1)}, bf16[256,640]{1,0:T(8,128)(2,1)S(1)}, u32[]{:S(2)}, u32[]{:S(2)}) collective-permute-start(bf16[256,640]{1,0:T(8,128)(2,1)S(1)} %fusion.9), channel_id=1, source_target_pairs={{0,2},{1,3},{2,0},{3,1},{4,6},{5,7},{6,4},{7,5},{8,10},{9,11},{10,... | collective-permute-start | bytes 983048 | tf_op jit(solution)/shard_map/ppermute | solution.py:36
  126.8 9.1 %copy-start.12 = (f32[256,640]{1,0:T(8,128)S(1)}, f32[256,640]{1,0:T(8,128)}, u32[]{:S(2)}) copy-start(f32[256,640]{1,0:T(8,128)} %get-tuple-element.15) | copy-start | bytes 1966084
  (20 other events, 63.9 us)

commit v2 on v1

v2 whole, which is shorter than its diff:
```python
import functools
import math

import jax
import jax.numpy as jnp
from jax import lax
from jax.experimental import pallas as pl
from jax.experimental.pallas import tpu as pltpu
from jax.sharding import PartitionSpec as P

ORDERS = 601
TAYLOR = 3
LEVELS = 3
SPLIT = (128, 128)
CHUNKS = len(SPLIT)
LANES = 128
HALVES = 2
F32 = jnp.float32
BF16 = jnp.bfloat16
WHOLE = pl.BlockSpec(memory_space=pltpu.VMEM)
SCALAR = pl.BlockSpec(memory_space=pltpu.SMEM)


def shape(*dims, dtype=F32):
    return jax.ShapeDtypeStruct(dims, dtype)


def call(body, out_shape, *args, scratch=(), limit=8):
    return pl.pallas_call(
        body,
        out_shape=out_shape,
        in_specs=[SCALAR if arg.size <= 8 else WHOLE for arg in args],
        out_specs=jax.tree.map(lambda _: WHOLE, out_shape),
        scratch_shapes=list(scratch),
        compiler_params=pltpu.CompilerParams(vmem_limit_bytes=limit * 2**20),
        cost_estimate=pl.CostEstimate(flops=0, transcendentals=0, bytes_accessed=1),
    )(*args)


def split(refs, value):
    first = 0
    for ref in refs:
        ref[...] = value[first : first + ref.shape[0]]
        first += ref.shape[0]


def joined(refs):
    return jnp.concatenate([ref[...] for ref in refs], axis=0)


def after(value, token):
    return lax.optimization_barrier((value, token))[0]


def over_row(value, mask):
    pairs = [(source, source ^ mask) for source in range(lax.axis_size("row"))]
    return lax.ppermute(value, "row", pairs)


def over_cuts(value):
    size = lax.axis_size("cuts")
    group = 2**LEVELS
    groups = None
    if size != group:
        groups = [list(range(first, first + group)) for first in range(0, size, group)]
    return lax.all_to_all(value, "cuts", 0, 0, axis_index_groups=groups, tiled=True)


def times_t(block, panel):
    return lax.dot_general(block, panel, (((1,), (1,)), ((), ())), preferred_element_type=F32)


def times(block, panel):
    return lax.dot_general(block, panel, (((1,), (0,)), ((), ())), preferred_element_type=F32)


def operator_blocks(me_ref, profile_ref, table_ref, a_ref, out_ref, step_ref):
    rows, full = a_ref.shape
    pad = out_ref.shape[1]
    step_ref[...] = jnp.full(step_ref.shape, table_ref[profile_ref[0]], F32)
    for block in range(full // rows):
        place = me_ref[0] ^ block
        out_ref[place, rows // 16 * 16 :, :] = jnp.zeros((pad - rows // 16 * 16, pad), BF16)
        out_ref[place, :, rows // LANES * LANES :] = jnp.zeros((pad, pad - rows // LANES * LANES), BF16)
        out_ref[place, :rows, :rows] = a_ref[:, block * rows : (block + 1) * rows]


def turned(me_ref, x_ref, *refs):
    tall = refs[-1]
    rows = x_ref.shape[0]
    tall[rows:, :] = jnp.zeros_like(tall[rows:, :])
    tall[:rows, :] = x_ref[...].astype(F32)
    flat = tall[...].T.astype(BF16)
    first = 0
    for out_ref in refs[:-1]:
        out_ref[...] = flat[first : first + out_ref.shape[0]]
        first += out_ref.shape[0]


def coupling(reflect_ref, cotangent_ref, out_ref, tall):
    levels, rows, _, columns = reflect_ref.shape
    pad = tall.shape[0]
    group, part = out_ref.shape[:2]
    tall[rows:, :] = jnp.zeros_like(tall[rows:, :])
    cot = cotangent_ref[...].T
    high = cot.astype(BF16)
    low = (cot - high.astype(F32)).astype(BF16)
    tracked = cot.shape[1]
    first = levels * pad
    out_ref[:, :, first : first + tracked] = high.reshape(group, part, tracked)
    out_ref[:, :, first + tracked :] = low.reshape(group, part, tracked)
    for level in range(levels):
        tall[:rows, :] = reflect_ref[level, :, 0, :]
        out_ref[:, :, level * pad : (level + 1) * pad] = tall[...].T.astype(BF16).reshape(group, part, pad)


def forward_near(own_ref, core_ref, panel_ref, out_ref, *copies):
    out_ref[...] = times_t(own_ref[...], panel_ref[0]) + times_t(core_ref[...], panel_ref[1])
    for copy_ref in copies:
        copy_ref[...] = own_ref[...]


def forward_far(near_ref, far_ref, panel_ref, out_ref, *halves):
    out_ref[...] = near_ref[...] + times_t(far_ref[...], panel_ref[2])
    split(halves, far_ref[...])


def forward_last(degree, step_ref, x_ref, most_ref, panel_ref, *refs):
    product = most_ref[...] + times_t(joined(refs[:HALVES]), panel_ref[3])
    value = (x_ref[...].astype(F32) + step_ref[0:1, 0:1] / degree * product).astype(BF16)
    out_ref = refs[-1]
    first = 0
    for ref in refs[HALVES:-1]:
        out_ref[first : first + ref.shape[0]] = ref[...]
        first += ref.shape[0]
    out_ref[first:] = value


def merge(levels, rows, me_ref, order_ref, w_ref, rc_ref, field_ref, cmap_ref, level_ref, sums_ref):
    group, part, pad = w_ref.shape
    tracked = order_ref.shape[1]
    tail = level_ref.shape[2]
    place = lax.broadcasted_iota(jnp.int32, (pad, tracked), 0)
    order = jnp.where(place < rows, (place + me_ref[0] * rows) % ORDERS, -1)
    onehot = jnp.where(order == order_ref[...], 1.0, 0.0).astype(BF16)
    onehot = jnp.concatenate([onehot, onehot], axis=1)
    totals = []
    merged = [w_ref[s].astype(F32) for s in range(group)]
    level_ref[...] = rc_ref[:, :, :tail]
    for level in range(levels):
        sent = [
            rc_ref[s, :, level * pad : (level + 1) * pad].astype(F32) * merged[s] for s in range(group)
        ]
        merged = [merged[s] + sent[s ^ 2**level] for s in range(group)]
    lane = lax.broadcasted_iota(jnp.int32, (part, LANES), 1)
    for s in range(group):
        field = merged[s]
        cmap = times_t(rc_ref[s, :, tail:], onehot)
        squared = field * field
        power = jnp.sum(squared, axis=1, keepdims=True)
        weighted = jnp.sum(cmap * squared, axis=1, keepdims=True)
        field_ref[s] = field
        cmap_ref[s] = cmap
        totals.append(jnp.where(lane == 0, power, jnp.where(lane == 1, weighted, 0.0)))
    sums_ref[...] = jnp.concatenate(totals, axis=0).T[: sums_ref.shape[0]]


def unmerge(levels, full, scale, field_ref, cmap_ref, rc_ref, s0, s1, s2, s3, out_ref):
    group, part, pad = field_ref.shape
    sums = (s0[...] + s1[...]) + (s2[...] + s3[...])
    sums = jnp.concatenate([sums] * (LANES // sums.shape[0]), axis=0).T
    grad = []
    for s in range(group):
        power = sums[s * part : (s + 1) * part, 0:1]
        weighted = sums[s * part : (s + 1) * part, 1:2]
        inverse = 1.0 / (power / full + 1e-06)
        first = scale * 2.0 * inverse
        second = scale * 2.0 / full * (weighted * inverse * inverse)
        grad.append((first * cmap_ref[s] - second) * field_ref[s])
    for level in range(levels - 1, -1, -1):
        grad = [
            grad[s]
            + rc_ref[s, :, level * pad : (level + 1) * pad].astype(F32) * grad[s ^ 2**level]
            for s in range(group)
        ]
    for s in range(group):
        out_ref[s] = grad[s].astype(BF16)


def columns_of(me_ref, *refs):
    out_ref, pile = refs[-2:]
    places = pile.shape[0]
    rows = out_ref.shape[1] // places
    first = 0
    each = places - 1 + HALVES
    for chunk in range((len(refs) - 2) // each):
        group = refs[chunk * each : (chunk + 1) * each]
        width = group[0].shape[0]
        for place in range(places - 1):
            pile[me_ref[0] ^ place, first : first + width, :] = group[place][...]
        pile[me_ref[0] ^ (places - 1), first : first + width, :] = joined(group[places - 1 :])
        first += width
    for block in range(places):
        out_ref[:, block * rows : (block + 1) * rows] = pile[block, :, :rows]


def backward_first(first, step_ref, whole_ref, panel_ref, scaled_ref, total_ref, *refs):
    width = scaled_ref.shape[0]
    upstream = whole_ref[first : first + width]
    for ref in refs[HALVES:]:
        ref[...] = whole_ref[width:]
    total_ref[...] = upstream.astype(F32)
    scaled = (step_ref[0:1, 0:1] * upstream.astype(F32)).astype(BF16)
    scaled_ref[...] = scaled
    split(refs[:HALVES], times(scaled, panel_ref[3]).astype(BF16))


def backward_next(degree, step_ref, near_ref, core_ref, far_ref, before_ref, panel_ref, scaled_ref, total_ref, *sent):
    upstream = near_ref[...] + core_ref[...].astype(F32) + far_ref[...].astype(F32)
    total_ref[...] = before_ref[...] + upstream
    scaled = (step_ref[0:1, 0:1] / degree * upstream).astype(BF16)
    scaled_ref[...] = scaled
    split(sent, times(scaled, panel_ref[3]).astype(BF16))


def backward_far(scaled_ref, panel_ref, *refs):
    product = times(scaled_ref[...], panel_ref[2])
    refs[-1][...] = (product + joined(refs[:-1]).astype(F32)).astype(BF16)


def backward_near(scaled_ref, panel_ref, sent_ref, near_ref):
    sent_ref[...] = times(scaled_ref[...], panel_ref[1]).astype(BF16)
    near_ref[...] = times(scaled_ref[...], panel_ref[0])


def outer(chunks, *refs):
    out_ref = refs[-1]
    rights = refs[-1 - TAYLOR : -1]
    total = None
    for degree, right in enumerate(rights):
        left = jnp.concatenate([ref[...] for ref in refs[degree * chunks : (degree + 1) * chunks]], axis=0)
        value = lax.dot_general(left, right[...], (((0,), (0,)), ((), ())), preferred_element_type=F32)
        total = value if total is None else total + value
    out_ref[:, 0, :] = total


def finish(*refs):
    out_ref = refs[-1]
    rows = out_ref.shape[0]
    values = []
    for chunk in range(len(refs) // 4):
        near, total, core, far = (ref[...].astype(F32) for ref in refs[4 * chunk : 4 * chunk + 4])
        values.append((near + total) + (core + far))
    value = jnp.concatenate(values, axis=0).T
    out_ref[:, 0, :] = value[:rows]


def local(operator, incident, reflect, thickness_table, profile, order_index, cotangent):
    rows, full = operator.shape[1:]
    columns = incident.shape[2]
    levels = reflect.shape[1]
    group = 2**levels
    tracked = order_index.shape[0]
    pad = -(-rows // LANES) * LANES
    part = columns // group
    count = range(CHUNKS)
    me = lax.axis_index("row")
    me_arr = me.reshape(1)
    widths = [columns * share // sum(SPLIT) for share in SPLIT]
    blocks = [shape(width, pad, dtype=BF16) for width in widths]
    wides = [shape(width, pad) for width in widths]
    parts = [[shape(width // HALVES, pad, dtype=BF16)] * HALVES for width in widths]

    rc = call(
        coupling,
        shape(group, part, levels * pad + 2 * tracked, dtype=BF16),
        reflect.transpose(1, 2, 0, 3),
        cotangent[0],
        scratch=[pltpu.VMEM((pad, columns), F32)],
        limit=10,
    )
    x = call(turned, blocks, after(me_arr, rc), incident[0], scratch=[pltpu.VMEM((pad, columns), F32)])
    rc = over_cuts(rc)
    fars = [over_row(value, 2) for value in x]
    cores = [over_row(value, 1) for value in x]
    panel, step = call(
        operator_blocks,
        (shape(4, pad, pad, dtype=BF16), shape(8, LANES)),
        after(me_arr, x[0]), profile, thickness_table, operator[0],
        limit=12,
    )
    token = panel

    current = list(x)
    stored = [[] for _ in count]
    rights = []
    x = list(x)

    def write_columns(place, pieces):
        return call(
            columns_of,
            shape(columns, full, dtype=BF16),
            place, *pieces,
            scratch=[pltpu.VMEM((4, columns, pad), BF16)],
            limit=6,
        )

    for degree in range(TAYLOR, 0, -1):
        next_fars, next_cores = [], []
        for chunk in count:
            near = call(
                forward_near,
                [wides[chunk]] + [blocks[chunk]] * (degree == TAYLOR),
                current[chunk], after(cores[chunk], token), panel,
            )
            if degree == TAYLOR:
                x[chunk] = near[1]
            far = after(fars[chunk], near[0])
            most, *halves = call(
                forward_far, [wides[chunk]] + parts[chunk], near[0], far, panel
            )
            diag = [over_row(half, 1) for half in halves]
            stored[chunk].append((current[chunk], cores[chunk], far, *diag))
            final = degree == 1 and chunk == CHUNKS - 1
            value = call(
                functools.partial(forward_last, degree),
                shape(columns, pad, dtype=BF16) if final else blocks[chunk],
                step, x[chunk], most, panel, *diag,
                *(current[:-1] if final else []),
            )
            current[chunk] = value
            token = value
            if degree > 1:
                next_fars.append(over_row(value, 2))
                next_cores.append(over_row(value, 1))
        fars, cores = next_fars, next_cores
        pieces = [piece for chunk in count for piece in stored[chunk][-1]]
        place = after(me_arr, token)
        if degree > 1:
            token = write_columns(place, pieces)
            rights.append(token)

    current[-1], rc = lax.optimization_barrier((current[-1], rc))
    swapped = over_cuts(current[-1].reshape(group, part, pad))
    field, cmap, coupled, sums = call(
        functools.partial(merge, levels, rows),
        (
            shape(group, part, pad),
            shape(group, part, pad),
            shape(group, part, levels * pad, dtype=BF16),
            shape(8, group * part),
        ),
        me_arr, order_index.reshape(1, tracked), swapped, rc,
        limit=12,
    )
    s1, s2, s3 = (over_row(sums, mask) for mask in (1, 2, 3))
    grad = call(
        functools.partial(unmerge, levels, full, 1.0 / math.sqrt(columns)),
        shape(group, part, pad, dtype=BF16),
        field, cmap, coupled, sums, s1, s2, s3,
    )
    whole = over_cuts(grad).reshape(columns, pad)
    token = write_columns(after(place, grad), pieces)
    rights.append(token)

    total = [None] * CHUNKS
    pending = [None] * CHUNKS
    scaled_all = []
    for degree in range(1, TAYLOR + 1):
        for chunk in count:
            outs = [blocks[chunk], wides[chunk]] + parts[chunk]
            if degree == 1:
                scaled, total[chunk], *sent = call(
                    functools.partial(backward_first, 0),
                    outs + ([blocks[1]] if chunk == 0 and CHUNKS == 2 else []),
                    step, after(whole, token), panel,
                )
                if chunk == 0 and CHUNKS == 2:
                    whole = sent.pop()
            else:
                near, core, far = pending[chunk]
                scaled, total[chunk], *sent = call(
                    functools.partial(backward_next, degree), outs,
                    step, near, core, after(far, token), total[chunk], panel,
                )
            scaled_all.append(scaled)
            diag = [over_row(half, 1) for half in sent]
            sent = call(backward_far, blocks[chunk], scaled, panel, *diag)
            far = over_row(sent, 2)
            sent, near = call(backward_near, (blocks[chunk], wides[chunk]), after(scaled, sent), panel)
            core = over_row(sent, 1)
            token = near
            pending[chunk] = (near, core, far)
    grad_matrix = pl.pallas_call(
        functools.partial(outer, CHUNKS),
        grid=(pad // LANES,),
        out_shape=shape(rows, 1, full),
        in_specs=[pl.BlockSpec((scaled.shape[0], LANES), lambda i: (0, i)) for scaled in scaled_all]
        + [WHOLE] * TAYLOR,
        out_specs=pl.BlockSpec((LANES, 1, full), lambda i: (i, 0, 0)),
        compiler_params=pltpu.CompilerParams(vmem_limit_bytes=20 * 2**20),
        cost_estimate=pl.CostEstimate(flops=0, transcendentals=0, bytes_accessed=1),
    )(*scaled_all[:-1], after(scaled_all[-1], token), *rights[::-1])
    args = []
    for chunk in count:
        near, core, far = pending[chunk]
        args += [near, total[chunk], core, far]
    args[-1] = after(args[-1], grad_matrix)
    grad_incident = call(finish, shape(rows, 1, columns), *args)
    return (grad_matrix.transpose(1, 0, 2), grad_incident.transpose(1, 0, 2))


def solution(mesh):
    return jax.shard_map(
        local,
        mesh=mesh,
        in_specs=(
            P("cuts", "row", None),
            P("cuts", "row", None),
            P("cuts", None, "row", None),
            P(),
            P("cuts"),
            P(),
            P("cuts", None, None),
        ),
        out_specs=(P("cuts", "row", None), P("cuts", "row", None)),
        check_vma=False,
    )
```

time: 138 us -> 122 us (0.88)
  waiting for transfers between devices: 44.5 us -> 19.7 us
  Pallas kernels: 6.29 us -> 29.9 us
  matrix products: 22.7 us -> 0 us
  blocking collectives: 0 us -> 17.4 us
  other arithmetic: 11.2 us -> 0 us
  starting transfers between devices: 26.2 us -> 34.3 us
  local copies, waits for them, and re-layouts: 23.1 us -> 18.1 us
  between operations: 3.32 us -> 1.89 us
    all_to_all x3 -> x2, waiting for transfers between devices: 26.3 us -> 2.07 us  [over_cuts(): lax.all_to_all(value, 'cuts', 0, 0, axis_index_groups=groups, tiled=True)]
    pallas_call x5 -> x46, Pallas kernels: 6.29 us -> 29.9 us  [the longest x45 24.4 us: call(): pl.pallas_call(body, out_shape=out_shape, in_specs=[SCALAR if arg.size <=...]
    dot_general x25 -> x0, matrix products: 22.7 us -> none  [the longest x12 11.9 us: times_t(): lax.dot_general(block, panel, (((1,), (1,)), ((), ())), preferred_element...]
    all_to_all x0 -> x1, blocking collectives: none -> 17.4 us  [over_cuts(): lax.all_to_all(value, 'cuts', 0, 0, axis_index_groups=groups, tiled=True)]
    ppermute x21 -> x51, starting transfers between devices: 12 us -> 22.9 us  [over_row(): return lax.ppermute(value, 'row', pairs)]
    concatenate x1 -> x0, local copies, waits for them, and re-layouts: 7.45 us -> none  [local(): right = jnp.concatenate(blocks, axis=1)]
    convert_element_type x4 -> x0, other arithmetic: 4.78 us -> none  [the longest x3 4.68 us: local(): scaled = (step_len / degree * upstream).astype(BF16)]
    unnamed x59 -> x60, local copies, waits for them, and re-layouts: 14.3 us -> 18.1 us
  transfers between devices with their start and end apart: 24 -> 53, of which waited for: 7 -> 32; matrix products, arithmetic and copies ran while one was open for 33% -> 0% of each run, Pallas kernels for 3% -> 18%
where the time goes in v2:
time: 122 us; the launch traced here: 121 us
  starting transfers between devices  34.3 us (28%)
  Pallas kernels  29.9 us (25%)
  waiting for transfers between devices  19.7 us (16%)
  local copies, waits for them, and re-layouts  18.1 us (15%)
  blocking collectives  17.4 us (14%)
  between operations  1.89 us (2%)
    pallas_call x45, Pallas kernels, call(): pl.pallas_call(body, out_shape=out_shape, in_specs=[SCALAR if arg.size <=...  24.4 us
    ppermute x51, starting transfers between devices, over_row(): return lax.ppermute(value, 'row', pairs)  22.9 us
    unnamed x60, local copies, waits for them, and re-layouts  18.1 us
    ppermute x51, waiting for transfers between devices, over_row(): return lax.ppermute(value, 'row', pairs)  17.7 us
    all_to_all x1, blocking collectives, over_cuts(): lax.all_to_all(value, 'cuts', 0, 0, axis_index_groups=groups, tiled=True)  17.4 us
    all_to_all x2, starting transfers between devices, over_cuts(): lax.all_to_all(value, 'cuts', 0, 0, axis_index_groups=groups, tiled=True)  11.5 us
    pallas_call x1, Pallas kernels, local(): pl.pallas_call(functools.partial(outer, CHUNKS), grid=(pad // LANES,), ou...  5.51 us
  transfers between devices with their start and end apart: 53, of which 32 were waited for; matrix products, arithmetic and copies ran while one was open for 0% of the time, Pallas kernels for 18%

profile of v2, /device:TPU:0, one launch (start us, length us, event | category | flops | bytes accessed | tf_op | source)
XLA Modules:
  0.0 121.4 jit_solution(11396410481040297571)
XLA Ops:
  0.6 1.5 %copy-done.7 = f32[1,3,601,256]{3,0,2,1:T(1,128)S(1)} copy-done((f32[1,3,601,256]{3,0,2,1:T(1,128)S(1)}, f32[1,3,601,256]{3,0,2,1:T(1,128)}, u32[]{:S(2)}) %copy-start.7) | copy-done | bytes 1846296
  3.0 1.8 %shard_map.86 = bf16[8,32,2048]{2,1,0:T(8,128)(2,1)} custom-call(f32[3,601,1,256]{3,2,1,0:T(1,128)S(1)} %bitcast.11, f32[64,256]{1,0:T(8,128)S(1)} %bitcast.14), custom_call_target="tpu_custom_call" | custom-call | bytes 1 | tf_op jit(solution)/shard_map/pallas_call | solution.py:29
  4.8 7.4 %all-to-all-start = ((bf16[8,32,2048]{2,1,0:T(8,128)(2,1)}), bf16[8,32,2048]{2,1,0:T(8,128)(2,1)}, u32[]{:S(2)}, u32[]{:S(2)}) async-start(bf16[8,32,2048]{2,1,0:T(8,128)(2,1)} %shard_map.86), calls=%async_computation | async-start | bytes 2097152 | tf_op jit(solution)/shard_map/all_to_all | solution.py:66
  12.4 1.6 %collective-permute-start.2 = (bf16[128,640]{1,0:T(8,128)(2,1)S(1)}, bf16[128,640]{1,0:T(8,128)(2,1)S(1)}, u32[]{:S(2)}, u32[]{:S(2)}) collective-permute-start(bf16[128,640]{1,0:T(8,128)(2,1)S(1)} %get-tuple-element.104.own_ref.refs_0_), channel_id=1, source_target_pairs={{0,2},{1,3},{2,0},{3,1},{4,6},{5,7},{6,4},{7,5},{8,10},{9,11},{10,... | collective-permute-start | bytes 491528 | tf_op jit(solution)/shard_map/ppermute | solution.py:57
  15.4 1.8 %copy-done.6 = bf16[1,601,2404]{2,1,0:T(8,128)(2,1)S(1)} copy-done((bf16[1,601,2404]{2,1,0:T(8,128)(2,1)S(1)}, bf16[1,601,2404]{2,1,0:T(8,128)(2,1)}, u32[]{:S(2)}) %copy-start.6) | copy-done | bytes 2889632
  17.2 1.4 %shard_map.88 = (bf16[4,640,640]{2,1,0:T(8,128)(2,1)S(1)}, f32[8,128]{1,0:T(8,128)S(1)}) custom-call(s32[1]{0:T(128)} %bitcast.me_ref, s32[1]{0:T(128)S(6)} %copy.9.profile_ref, f32[8]{0:T(128)S(1)} %copy-done.28, bf16[601,2404]{1,0:T(8,128)(2,1)S(1)} %bitcast.10), custom_call_target="tpu_custom_call" | custom-call | bytes 1 | tf_op jit(solution)/shard_map/pallas_call | solution.py:29
  21.7 1.6 %collective-permute-start.10 = (bf16[128,640]{1,0:T(8,128)(2,1)S(1)}, bf16[128,640]{1,0:T(8,128)(2,1)S(1)}, u32[]{:S(2)}, u32[]{:S(2)}) collective-permute-start(bf16[128,640]{1,0:T(8,128)(2,1)S(1)} %shard_map.91.own_ref.refs_0_), channel_id=1, source_target_pairs={{0,2},{1,3},{2,0},{3,1},{4,6},{5,7},{6,4},{7,5},{8,10},{9,11},{10,... | collective-permute-start | bytes 491528 | tf_op jit(solution)/shard_map/ppermute | solution.py:57
  27.8 1.0 copy-done
  31.7 1.6 %collective-permute-start.18 = (bf16[128,640]{1,0:T(8,128)(2,1)S(1)}, bf16[128,640]{1,0:T(8,128)(2,1)S(1)}, u32[]{:S(2)}, u32[]{:S(2)}) collective-permute-start(bf16[128,640]{1,0:T(8,128)(2,1)S(1)} %shard_map.98.own_ref.refs_0_), channel_id=1, source_target_pairs={{0,2},{1,3},{2,0},{3,1},{4,6},{5,7},{6,4},{7,5},{8,10},{9,11},{10,... | collective-permute-start | bytes 491528 | tf_op jit(solution)/shard_map/ppermute | solution.py:57
  37.7 1.0 copy-done.2
  47.7 17.4 %all_to_all.15.w_ref = bf16[8,32,640]{2,1,0:T(8,128)(2,1)S(1)} all-to-all(bf16[8,32,640]{2,1,0:T(8,128)(2,1)} %bitcast.12), channel_id=1, replica_groups=mesh['cuts'=8,'row'=4] {'cuts'}, dimensions={0} | all-to-all | bytes 655360 | tf_op jit(solution)/shard_map/all_to_all | solution.py:66
  65.1 2.3 %shard_map.109 = (f32[8,32,640]{2,1,0:T(8,128)S(1)}, f32[8,32,640]{2,1,0:T(8,128)S(1)}, bf16[8,32,1920]{2,1,0:T(8,128)(2,1)S(1)}, f32[8,256]{1,0:T(8,128)S(1)}) custom-call(s32[1]{0:T(128)} %bitcast.me_ref, s32[1,64]{1,0:T(1,128)S(1)} %bitcast.15, bf16[8,32,640]{2,1,0:T(8,128)(2,1)S(1)} %all_to_all.15.w_ref, bf16[8,32,2048]{2,1,0:T(8,128)(2,1)} %all-to-all-done.rc_ref), custom_call_target="tpu_custom_call" | custom-call | bytes 1 | tf_op jit(solution)/shard_map/pallas_call | solution.py:29
  67.4 1.2 %collective-permute-start.25 = (f32[8,256]{1,0:T(8,128)S(1)}, f32[8,256]{1,0:T(8,128)S(1)}, u32[]{:S(2)}, u32[]{:S(2)}) collective-permute-start(f32[8,256]{1,0:T(8,128)S(1)} %get-tuple-element.150.s0), channel_id=1, source_target_pairs={{0,2},{1,3},{2,0},{3,1},{4,6},{5,7},{6,4},{7,5},{8,10},{9,11},{10,... | collective-permute-start | bytes 24584 | tf_op jit(solution)/shard_map/ppermute | solution.py:57
  69.3 1.2 collective-permute-done.26.s3
  72.4 4.1 %all-to-all-start.2 = ((bf16[8,32,640]{2,1,0:T(8,128)(2,1)}), bf16[8,32,640]{2,1,0:T(8,128)(2,1)}, u32[]{:S(2)}, u32[]{:S(2)}) async-start(bf16[8,32,640]{2,1,0:T(8,128)(2,1)} %copy-done.11), calls=%async_computation.2 | async-start | bytes 655360 | tf_op jit(solution)/shard_map/all_to_all | solution.py:66
  77.4 0.9 copy-done.13
  78.3 0.9 copy-done.15
  79.2 0.9 copy-done.17
  80.1 0.9 copy-done.19
  84.2 1.0 copy-done.4
  85.2 2.1 %all-to-all-done.2 = bf16[8,32,640]{2,1,0:T(8,128)(2,1)} async-done(((bf16[8,32,640]{2,1,0:T(8,128)(2,1)}), bf16[8,32,640]{2,1,0:T(8,128)(2,1)}, u32[]{:S(2)}, u32[]{:S(2)}) %all-to-all-start.2) | async-done | bytes 327712 | tf_op jit(solution)/shard_map/all_to_all | solution.py:66
  87.3 1.3 %shard_map.112 = (bf16[128,640]{1,0:T(8,128)(2,1)S(1)}, f32[128,640]{1,0:T(8,128)S(1)}, bf16[64,640]{1,0:T(8,128)(2,1)S(1)}, bf16[64,640]{1,0:T(8,128)(2,1)S(1)}, bf16[128,640]{1,0:T(8,128)(2,1)S(1)}) custom-call(f32[8,128]{1,0:T(8,128)S(1)} %get-tuple-element.106.step_ref, bf16[256,640]{1,0:T(8,128)(2,1)} %bitcast.7.whole_ref, ...), custom_call_target="tpu_custom_call" | custom-call | bytes 1 | tf_op jit(solution)/shard_map/pallas_call | solution.py:29
  90.4 1.2 collective-permute-start.30
  94.6 1.0 collective-permute-start.34
  99.1 1.2 collective-permute-start.38
  103.3 1.0 collective-permute-start.42
  108.3 1.4 %collective-permute-done.42.far_ref = bf16[128,640]{1,0:T(8,128)(2,1)S(1)} collective-permute-done((bf16[128,640]{1,0:T(8,128)(2,1)S(1)}, bf16[128,640]{1,0:T(8,128)(2,1)S(1)}, u32[]{:S(2)}, u32[]{:S(2)}) %collective-permute-start.42) | collective-permute-done | bytes 163872 | tf_op jit(solution)/shard_map/ppermute | solution.py:57
  110.6 0.9 collective-permute-start.48
  111.9 1.2 collective-permute-start.50
  113.8 5.5 %shard_map.130 = f32[601,1,2404]{2,1,0:T(1,128)} custom-call(bf16[128,640]{1,0:T(8,128)(2,1)S(1)} %get-tuple-element.158.scaled_ref.refs_0_, bf16[128,640]{1,0:T(8,128)(2,1)S(1)} %get-tuple-element.165.scaled_ref.refs_1_, bf16[128,640]{1,0:T(8,128)(2,1)S(1)} %get-tuple-element.173.scaled_ref.refs_2_, ...), custom_call_target="tpu_custom_call" | custom-call | bytes 1 | tf_op jit(solution)/shard_map/pallas_call | solution.py:394
  119.3 1.0 collective-permute-done.50.refs_7_
  120.3 1.1 shard_map.131
  (181 shorter events, 49.1 us)
Async XLA Ops:
  4.8 42.9 %all-to-all-start = ((bf16[8,32,2048]{2,1,0:T(8,128)(2,1)}), bf16[8,32,2048]{2,1,0:T(8,128)(2,1)}, u32[]{:S(2)}, u32[]{:S(2)}) async-start(bf16[8,32,2048]{2,1,0:T(8,128)(2,1)} %shard_map.86), calls=%async_computation | async-start | bytes 2097152 | tf_op jit(solution)/shard_map/all_to_all | solution.py:66
  12.4 6.2 %collective-permute-start.1 = (bf16[128,640]{1,0:T(8,128)(2,1)S(1)}, bf16[128,640]{1,0:T(8,128)(2,1)S(1)}, u32[]{:S(2)}, u32[]{:S(2)}) collective-permute-start(bf16[128,640]{1,0:T(8,128)(2,1)S(1)} %get-tuple-element.104.own_ref.refs_0_), channel_id=1, source_target_pairs={{0,1},{1,0},{2,3},{3,2},{4,5},{5,4},{6,7},{7,6},{8,9},{9,8},{10,11... | collective-permute-start | bytes 491528 | tf_op jit(solution)/shard_map/ppermute | solution.py:57
  12.4 7.1 %collective-permute-start.2 = (bf16[128,640]{1,0:T(8,128)(2,1)S(1)}, bf16[128,640]{1,0:T(8,128)(2,1)S(1)}, u32[]{:S(2)}, u32[]{:S(2)}) collective-permute-start(bf16[128,640]{1,0:T(8,128)(2,1)S(1)} %get-tuple-element.104.own_ref.refs_0_), channel_id=1, source_target_pairs={{0,2},{1,3},{2,0},{3,1},{4,6},{5,7},{6,4},{7,5},{8,10},{9,11},{10,... | collective-permute-start | bytes 491528 | tf_op jit(solution)/shard_map/ppermute | solution.py:57
  14.0 9.4 %collective-permute-start = (bf16[128,640]{1,0:T(8,128)(2,1)S(1)}, bf16[128,640]{1,0:T(8,128)(2,1)S(1)}, u32[]{:S(2)}, u32[]{:S(2)}) collective-permute-start(bf16[128,640]{1,0:T(8,128)(2,1)S(1)} %get-tuple-element.107.own_ref.refs_5_), channel_id=1, source_target_pairs={{0,1},{1,0},{2,3},{3,2},{4,5},{5,4},{6,7},{7,6},{8,9},{9,8},{10,11... | collective-permute-start | bytes 491528 | tf_op jit(solution)/shard_map/ppermute | solution.py:57
  14.2 9.9 %collective-permute-start.5 = (bf16[128,640]{1,0:T(8,128)(2,1)S(1)}, bf16[128,640]{1,0:T(8,128)(2,1)S(1)}, u32[]{:S(2)}, u32[]{:S(2)}) collective-permute-start(bf16[128,640]{1,0:T(8,128)(2,1)S(1)} %get-tuple-element.107.own_ref.refs_5_), channel_id=1, source_target_pairs={{0,2},{1,3},{2,0},{3,1},{4,6},{5,7},{6,4},{7,5},{8,10},{9,11},{10,... | collective-permute-start | bytes 491528 | tf_op jit(solution)/shard_map/ppermute | solution.py:57
  21.7 7.7 %collective-permute-start.10 = (bf16[128,640]{1,0:T(8,128)(2,1)S(1)}, bf16[128,640]{1,0:T(8,128)(2,1)S(1)}, u32[]{:S(2)}, u32[]{:S(2)}) collective-permute-start(bf16[128,640]{1,0:T(8,128)(2,1)S(1)} %shard_map.91.own_ref.refs_0_), channel_id=1, source_target_pairs={{0,2},{1,3},{2,0},{3,1},{4,6},{5,7},{6,4},{7,5},{8,10},{9,11},{10,... | collective-permute-start | bytes 491528 | tf_op jit(solution)/shard_map/ppermute | solution.py:57
  23.3 5.5 %collective-permute-start.9 = (bf16[128,640]{1,0:T(8,128)(2,1)S(1)}, bf16[128,640]{1,0:T(8,128)(2,1)S(1)}, u32[]{:S(2)}, u32[]{:S(2)}) collective-permute-start(bf16[128,640]{1,0:T(8,128)(2,1)S(1)} %shard_map.91.own_ref.refs_0_), channel_id=1, source_target_pairs={{0,1},{1,0},{2,3},{3,2},{4,5},{5,4},{6,7},{7,6},{8,9},{9,8},{10,11... | collective-permute-start | bytes 491528 | tf_op jit(solution)/shard_map/ppermute | solution.py:57
  26.6 6.8 %collective-permute-start.8 = (bf16[128,640]{1,0:T(8,128)(2,1)S(1)}, bf16[128,640]{1,0:T(8,128)(2,1)S(1)}, u32[]{:S(2)}, u32[]{:S(2)}) collective-permute-start(bf16[128,640]{1,0:T(8,128)(2,1)S(1)} %shard_map.94.own_ref.refs_5_), channel_id=1, source_target_pairs={{0,1},{1,0},{2,3},{3,2},{4,5},{5,4},{6,7},{7,6},{8,9},{9,8},{10,11... | collective-permute-start | bytes 491528 | tf_op jit(solution)/shard_map/ppermute | solution.py:57
  26.8 7.2 %collective-permute-start.13 = (bf16[128,640]{1,0:T(8,128)(2,1)S(1)}, bf16[128,640]{1,0:T(8,128)(2,1)S(1)}, u32[]{:S(2)}, u32[]{:S(2)}) collective-permute-start(bf16[128,640]{1,0:T(8,128)(2,1)S(1)} %shard_map.94.own_ref.refs_5_), channel_id=1, source_target_pairs={{0,2},{1,3},{2,0},{3,1},{4,6},{5,7},{6,4},{7,5},{8,10},{9,11},{10,... | collective-permute-start | bytes 491528 | tf_op jit(solution)/shard_map/ppermute | solution.py:57
  31.7 7.7 %collective-permute-start.18 = (bf16[128,640]{1,0:T(8,128)(2,1)S(1)}, bf16[128,640]{1,0:T(8,128)(2,1)S(1)}, u32[]{:S(2)}, u32[]{:S(2)}) collective-permute-start(bf16[128,640]{1,0:T(8,128)(2,1)S(1)} %shard_map.98.own_ref.refs_0_), channel_id=1, source_target_pairs={{0,2},{1,3},{2,0},{3,1},{4,6},{5,7},{6,4},{7,5},{8,10},{9,11},{10,... | collective-permute-start | bytes 491528 | tf_op jit(solution)/shard_map/ppermute | solution.py:57
  33.3 5.5 %collective-permute-start.17 = (bf16[128,640]{1,0:T(8,128)(2,1)S(1)}, bf16[128,640]{1,0:T(8,128)(2,1)S(1)}, u32[]{:S(2)}, u32[]{:S(2)}) collective-permute-start(bf16[128,640]{1,0:T(8,128)(2,1)S(1)} %shard_map.98.own_ref.refs_0_), channel_id=1, source_target_pairs={{0,1},{1,0},{2,3},{3,2},{4,5},{5,4},{6,7},{7,6},{8,9},{9,8},{10,11... | collective-permute-start | bytes 491528 | tf_op jit(solution)/shard_map/ppermute | solution.py:57
  36.5 5.7 %collective-permute-start.16 = (bf16[128,640]{1,0:T(8,128)(2,1)S(1)}, bf16[128,640]{1,0:T(8,128)(2,1)S(1)}, u32[]{:S(2)}, u32[]{:S(2)}) collective-permute-start(bf16[128,640]{1,0:T(8,128)(2,1)S(1)} %shard_map.101.own_ref.refs_5_), channel_id=1, source_target_pairs={{0,1},{1,0},{2,3},{3,2},{4,5},{5,4},{6,7},{7,6},{8,9},{9,8},{10,11... | collective-permute-start | bytes 491528 | tf_op jit(solution)/shard_map/ppermute | solution.py:57
  36.7 6.5 %collective-permute-start.21 = (bf16[128,640]{1,0:T(8,128)(2,1)S(1)}, bf16[128,640]{1,0:T(8,128)(2,1)S(1)}, u32[]{:S(2)}, u32[]{:S(2)}) collective-permute-start(bf16[128,640]{1,0:T(8,128)(2,1)S(1)} %shard_map.101.own_ref.refs_5_), channel_id=1, source_target_pairs={{0,2},{1,3},{2,0},{3,1},{4,6},{5,7},{6,4},{7,5},{8,10},{9,11},{10,... | collective-permute-start | bytes 491528 | tf_op jit(solution)/shard_map/ppermute | solution.py:57
  67.4 3.1 %collective-permute-start.26 = (f32[8,256]{1,0:T(8,128)S(1)}, f32[8,256]{1,0:T(8,128)S(1)}, u32[]{:S(2)}, u32[]{:S(2)}) collective-permute-start(f32[8,256]{1,0:T(8,128)S(1)} %get-tuple-element.150.s0), channel_id=1, source_target_pairs={{0,3},{1,2},{2,1},{3,0},{4,7},{5,6},{6,5},{7,4},{8,11},{9,10},{10,... | collective-permute-start | bytes 24584 | tf_op jit(solution)/shard_map/ppermute | solution.py:57
  67.4 3.7 %collective-permute-start.25 = (f32[8,256]{1,0:T(8,128)S(1)}, f32[8,256]{1,0:T(8,128)S(1)}, u32[]{:S(2)}, u32[]{:S(2)}) collective-permute-start(f32[8,256]{1,0:T(8,128)S(1)} %get-tuple-element.150.s0), channel_id=1, source_target_pairs={{0,2},{1,3},{2,0},{3,1},{4,6},{5,7},{6,4},{7,5},{8,10},{9,11},{10,... | collective-permute-start | bytes 24584 | tf_op jit(solution)/shard_map/ppermute | solution.py:57
  68.7 2.5 %collective-permute-start.24 = (f32[8,256]{1,0:T(8,128)S(1)}, f32[8,256]{1,0:T(8,128)S(1)}, u32[]{:S(2)}, u32[]{:S(2)}) collective-permute-start(f32[8,256]{1,0:T(8,128)S(1)} %get-tuple-element.150.s0), channel_id=1, source_target_pairs={{0,1},{1,0},{2,3},{3,2},{4,5},{5,4},{6,7},{7,6},{8,9},{9,8},{10,11... | collective-permute-start | bytes 24584 | tf_op jit(solution)/shard_map/ppermute | solution.py:57
  72.4 14.9 %all-to-all-start.2 = ((bf16[8,32,640]{2,1,0:T(8,128)(2,1)}), bf16[8,32,640]{2,1,0:T(8,128)(2,1)}, u32[]{:S(2)}, u32[]{:S(2)}) async-start(bf16[8,32,640]{2,1,0:T(8,128)(2,1)} %copy-done.11), calls=%async_computation.2 | async-start | bytes 655360 | tf_op jit(solution)/shard_map/all_to_all | solution.py:66
  90.4 6.5 %collective-permute-start.30 = (bf16[128,640]{1,0:T(8,128)(2,1)S(1)}, bf16[128,640]{1,0:T(8,128)(2,1)S(1)}, u32[]{:S(2)}, u32[]{:S(2)}) collective-permute-start(bf16[128,640]{1,0:T(8,128)(2,1)S(1)} %shard_map.113), channel_id=1, source_target_pairs={{0,2},{1,3},{2,0},{3,1},{4,6},{5,7},{6,4},{7,5},{8,10},{9,11},{10,... | collective-permute-start | bytes 491528 | tf_op jit(solution)/shard_map/ppermute | solution.py:57
  92.1 4.9 %collective-permute-start.29 = (bf16[128,640]{1,0:T(8,128)(2,1)S(1)}, bf16[128,640]{1,0:T(8,128)(2,1)S(1)}, u32[]{:S(2)}, u32[]{:S(2)}) collective-permute-start(bf16[128,640]{1,0:T(8,128)(2,1)S(1)} %get-tuple-element.162), channel_id=1, source_target_pairs={{0,1},{1,0},{2,3},{3,2},{4,5},{5,4},{6,7},{7,6},{8,9},{9,8},{10,11... | collective-permute-start | bytes 491528 | tf_op jit(solution)/shard_map/ppermute | solution.py:57
  92.5 1.4 %collective-permute-start.31 = (bf16[64,640]{1,0:T(8,128)(2,1)S(1)}, bf16[64,640]{1,0:T(8,128)(2,1)S(1)}, u32[]{:S(2)}, u32[]{:S(2)}) collective-permute-start(bf16[64,640]{1,0:T(8,128)(2,1)S(1)} %get-tuple-element.163), channel_id=1, source_target_pairs={{0,1},{1,0},{2,3},{3,2},{4,5},{5,4},{6,7},{7,6},{8,9},{9,8},{10,11... | collective-permute-start | bytes 245768 | tf_op jit(solution)/shard_map/ppermute | solution.py:57
  94.6 6.3 %collective-permute-start.34 = (bf16[128,640]{1,0:T(8,128)(2,1)S(1)}, bf16[128,640]{1,0:T(8,128)(2,1)S(1)}, u32[]{:S(2)}, u32[]{:S(2)}) collective-permute-start(bf16[128,640]{1,0:T(8,128)(2,1)S(1)} %shard_map.116), channel_id=1, source_target_pairs={{0,2},{1,3},{2,0},{3,1},{4,6},{5,7},{6,4},{7,5},{8,10},{9,11},{10,... | collective-permute-start | bytes 491528 | tf_op jit(solution)/shard_map/ppermute | solution.py:57
  96.1 4.9 %collective-permute-start.33 = (bf16[128,640]{1,0:T(8,128)(2,1)S(1)}, bf16[128,640]{1,0:T(8,128)(2,1)S(1)}, u32[]{:S(2)}, u32[]{:S(2)}) collective-permute-start(bf16[128,640]{1,0:T(8,128)(2,1)S(1)} %get-tuple-element.170), channel_id=1, source_target_pairs={{0,1},{1,0},{2,3},{3,2},{4,5},{5,4},{6,7},{7,6},{8,9},{9,8},{10,11... | collective-permute-start | bytes 491528 | tf_op jit(solution)/shard_map/ppermute | solution.py:57
  99.1 6.5 %collective-permute-start.38 = (bf16[128,640]{1,0:T(8,128)(2,1)S(1)}, bf16[128,640]{1,0:T(8,128)(2,1)S(1)}, u32[]{:S(2)}, u32[]{:S(2)}) collective-permute-start(bf16[128,640]{1,0:T(8,128)(2,1)S(1)} %shard_map.119), channel_id=1, source_target_pairs={{0,2},{1,3},{2,0},{3,1},{4,6},{5,7},{6,4},{7,5},{8,10},{9,11},{10,... | collective-permute-start | bytes 491528 | tf_op jit(solution)/shard_map/ppermute | solution.py:57
  100.7 4.9 %collective-permute-start.37 = (bf16[128,640]{1,0:T(8,128)(2,1)S(1)}, bf16[128,640]{1,0:T(8,128)(2,1)S(1)}, u32[]{:S(2)}, u32[]{:S(2)}) collective-permute-start(bf16[128,640]{1,0:T(8,128)(2,1)S(1)} %get-tuple-element.178), channel_id=1, source_target_pairs={{0,1},{1,0},{2,3},{3,2},{4,5},{5,4},{6,7},{7,6},{8,9},{9,8},{10,11... | collective-permute-start | bytes 491528 | tf_op jit(solution)/shard_map/ppermute | solution.py:57
  103.3 6.3 %collective-permute-start.42 = (bf16[128,640]{1,0:T(8,128)(2,1)S(1)}, bf16[128,640]{1,0:T(8,128)(2,1)S(1)}, u32[]{:S(2)}, u32[]{:S(2)}) collective-permute-start(bf16[128,640]{1,0:T(8,128)(2,1)S(1)} %shard_map.122), channel_id=1, source_target_pairs={{0,2},{1,3},{2,0},{3,1},{4,6},{5,7},{6,4},{7,5},{8,10},{9,11},{10,... | collective-permute-start | bytes 491528 | tf_op jit(solution)/shard_map/ppermute | solution.py:57
  104.8 4.9 %collective-permute-start.41 = (bf16[128,640]{1,0:T(8,128)(2,1)S(1)}, bf16[128,640]{1,0:T(8,128)(2,1)S(1)}, u32[]{:S(2)}, u32[]{:S(2)}) collective-permute-start(bf16[128,640]{1,0:T(8,128)(2,1)S(1)} %get-tuple-element.186), channel_id=1, source_target_pairs={{0,1},{1,0},{2,3},{3,2},{4,5},{5,4},{6,7},{7,6},{8,9},{9,8},{10,11... | collective-permute-start | bytes 491528 | tf_op jit(solution)/shard_map/ppermute | solution.py:57
  110.0 1.5 %collective-permute-start.45 = (bf16[64,640]{1,0:T(8,128)(2,1)S(1)}, bf16[64,640]{1,0:T(8,128)(2,1)S(1)}, u32[]{:S(2)}, u32[]{:S(2)}) collective-permute-start(bf16[64,640]{1,0:T(8,128)(2,1)S(1)} %get-tuple-element.194), channel_id=1, source_target_pairs={{0,1},{1,0},{2,3},{3,2},{4,5},{5,4},{6,7},{7,6},{8,9},{9,8},{10,11... | collective-permute-start | bytes 245768 | tf_op jit(solution)/shard_map/ppermute | solution.py:57
  110.1 1.4 %collective-permute-start.46 = (bf16[64,640]{1,0:T(8,128)(2,1)S(1)}, bf16[64,640]{1,0:T(8,128)(2,1)S(1)}, u32[]{:S(2)}, u32[]{:S(2)}) collective-permute-start(bf16[64,640]{1,0:T(8,128)(2,1)S(1)} %get-tuple-element.195), channel_id=1, source_target_pairs={{0,1},{1,0},{2,3},{3,2},{4,5},{5,4},{6,7},{7,6},{8,9},{9,8},{10,11... | collective-permute-start | bytes 245768 | tf_op jit(solution)/shard_map/ppermute | solution.py:57
  110.6 9.7 %collective-permute-start.48 = (bf16[128,640]{1,0:T(8,128)(2,1)S(1)}, bf16[128,640]{1,0:T(8,128)(2,1)S(1)}, u32[]{:S(2)}, u32[]{:S(2)}) collective-permute-start(bf16[128,640]{1,0:T(8,128)(2,1)S(1)} %shard_map.125), channel_id=1, source_target_pairs={{0,2},{1,3},{2,0},{3,1},{4,6},{5,7},{6,4},{7,5},{8,10},{9,11},{10,... | collective-permute-start | bytes 491528 | tf_op jit(solution)/shard_map/ppermute | solution.py:57
  111.5 8.8 %collective-permute-start.47 = (bf16[128,640]{1,0:T(8,128)(2,1)S(1)}, bf16[128,640]{1,0:T(8,128)(2,1)S(1)}, u32[]{:S(2)}, u32[]{:S(2)}) collective-permute-start(bf16[128,640]{1,0:T(8,128)(2,1)S(1)} %get-tuple-element.200), channel_id=1, source_target_pairs={{0,1},{1,0},{2,3},{3,2},{4,5},{5,4},{6,7},{7,6},{8,9},{9,8},{10,11... | collective-permute-start | bytes 491528 | tf_op jit(solution)/shard_map/ppermute | solution.py:57
  111.9 8.4 %collective-permute-start.50 = (bf16[128,640]{1,0:T(8,128)(2,1)S(1)}, bf16[128,640]{1,0:T(8,128)(2,1)S(1)}, u32[]{:S(2)}, u32[]{:S(2)}) collective-permute-start(bf16[128,640]{1,0:T(8,128)(2,1)S(1)} %shard_map.128), channel_id=1, source_target_pairs={{0,2},{1,3},{2,0},{3,1},{4,6},{5,7},{6,4},{7,5},{8,10},{9,11},{10,... | collective-permute-start | bytes 491528 | tf_op jit(solution)/shard_map/ppermute | solution.py:57
  113.5 6.8 %collective-permute-start.49 = (bf16[128,640]{1,0:T(8,128)(2,1)S(1)}, bf16[128,640]{1,0:T(8,128)(2,1)S(1)}, u32[]{:S(2)}, u32[]{:S(2)}) collective-permute-start(bf16[128,640]{1,0:T(8,128)(2,1)S(1)} %get-tuple-element.202), channel_id=1, source_target_pairs={{0,1},{1,0},{2,3},{3,2},{4,5},{5,4},{6,7},{7,6},{8,9},{9,8},{10,11... | collective-permute-start | bytes 491528 | tf_op jit(solution)/shard_map/ppermute | solution.py:57
  (51 other events, 100.3 us)

commit v3 on v2

--- a/solution.py
+++ b/solution.py
@@ -14,6 +14,7 @@
 SPLIT = (128, 128)
 CHUNKS = len(SPLIT)
 LANES = 128
+COST = 5000000000
 HALVES = 2
 F32 = jnp.float32
 BF16 = jnp.bfloat16
@@ -114,15 +115,13 @@
         out_ref[:, :, level * pad : (level + 1) * pad] = tall[...].T.astype(BF16).reshape(group, part, pad)
 
 
-def forward_near(own_ref, core_ref, panel_ref, out_ref, *copies):
-    out_ref[...] = times_t(own_ref[...], panel_ref[0]) + times_t(core_ref[...], panel_ref[1])
-    for copy_ref in copies:
-        copy_ref[...] = own_ref[...]
-
-
-def forward_far(near_ref, far_ref, panel_ref, out_ref, *halves):
-    out_ref[...] = near_ref[...] + times_t(far_ref[...], panel_ref[2])
-    split(halves, far_ref[...])
+def halved(value_ref, *refs):
+    split(refs, value_ref[...])
+
+
+def forward_most(own_ref, core_ref, far_ref, panel_ref, out_ref):
+    near = times_t(own_ref[...], panel_ref[0]) + times_t(core_ref[...], panel_ref[1])
+    out_ref[...] = near + times_t(far_ref[...], panel_ref[2])
 
 
 def forward_last(degree, step_ref, x_ref, most_ref, panel_ref, *refs):
@@ -141,7 +140,10 @@
     tracked = order_ref.shape[1]
     tail = level_ref.shape[2]
     place = lax.broadcasted_iota(jnp.int32, (pad, tracked), 0)
-    order = jnp.where(place < rows, (place + me_ref[0] * rows) % ORDERS, -1)
+    order = place + lax.rem(me_ref[0] * rows, ORDERS)
+    for _ in range(-(-rows // ORDERS)):
+        order = jnp.where(order >= ORDERS, order - ORDERS, order)
+    order = jnp.where(place < rows, order, -1)
     onehot = jnp.where(order == order_ref[...], 1.0, 0.0).astype(BF16)
     onehot = jnp.concatenate([onehot, onehot], axis=1)
     totals = []
@@ -153,9 +155,10 @@
         ]
         merged = [merged[s] + sent[s ^ 2**level] for s in range(group)]
     lane = lax.broadcasted_iota(jnp.int32, (part, LANES), 1)
+    cmaps = times_t(rc_ref[:, :, tail:].reshape(group * part, 2 * tracked), onehot).reshape(group, part, pad)
     for s in range(group):
         field = merged[s]
-        cmap = times_t(rc_ref[s, :, tail:], onehot)
+        cmap = cmaps[s]
         squared = field * field
         power = jnp.sum(squared, axis=1, keepdims=True)
         weighted = jnp.sum(cmap * squared, axis=1, keepdims=True)
@@ -223,25 +226,44 @@
     split(sent, times(scaled, panel_ref[3]).astype(BF16))
 
 
-def backward_far(scaled_ref, panel_ref, *refs):
-    product = times(scaled_ref[...], panel_ref[2])
-    refs[-1][...] = (product + joined(refs[:-1]).astype(F32)).astype(BF16)
-
-
-def backward_near(scaled_ref, panel_ref, sent_ref, near_ref):
-    sent_ref[...] = times(scaled_ref[...], panel_ref[1]).astype(BF16)
-    near_ref[...] = times(scaled_ref[...], panel_ref[0])
+def backward_most(scaled_ref, panel_ref, sent_ref, near_ref, most_ref):
+    scaled = scaled_ref[...]
+    most_ref[...] = times(scaled, panel_ref[2])
+    sent_ref[...] = times(scaled, panel_ref[1]).astype(BF16)
+    near_ref[...] = times(scaled, panel_ref[0])
+
+
+def backward_last(most_ref, *refs):
+    refs[-1][...] = (most_ref[...] + joined(refs[:-1]).astype(F32)).astype(BF16)
 
 
 def outer(chunks, *refs):
     out_ref = refs[-1]
-    rights = refs[-1 - TAYLOR : -1]
+    rights = refs[TAYLOR * chunks : TAYLOR * chunks + TAYLOR]
     total = None
     for degree, right in enumerate(rights):
         left = jnp.concatenate([ref[...] for ref in refs[degree * chunks : (degree + 1) * chunks]], axis=0)
         value = lax.dot_general(left, right[...], (((0,), (0,)), ((), ())), preferred_element_type=F32)
         total = value if total is None else total + value
     out_ref[:, 0, :] = total
+
+
+def outer_rows(first, tiles, lefts, rights, target, rows, full):
+    body = functools.partial(outer, len(lefts) // TAYLOR)
+    specs = [pl.BlockSpec((left.shape[0], LANES), lambda i: (0, i + first)) for left in lefts]
+    args = [*lefts, *rights[::-1]]
+    if target is not None:
+        args.append(target)
+    return pl.pallas_call(
+        body,
+        grid=(tiles,),
+        out_shape=shape(rows, 1, full),
+        in_specs=specs + [WHOLE] * TAYLOR + [pl.BlockSpec(memory_space=pl.ANY)] * (target is not None),
+        out_specs=pl.BlockSpec((LANES, 1, full), lambda i: (i + first, 0, 0)),
+        input_output_aliases={} if target is None else {len(args) - 1: 0},
+        compiler_params=pltpu.CompilerParams(vmem_limit_bytes=20 * 2**20),
+        cost_estimate=pl.CostEstimate(flops=0 if target is None else COST, transcendentals=0, bytes_accessed=1),
+    )(*args)
 
 
 def finish(*refs):
@@ -296,10 +318,10 @@
     rights = []
     x = list(x)
 
-    def write_columns(place, pieces):
+    def write_columns(place, pieces, hbm=True):
         return call(
             columns_of,
-            shape(columns, full, dtype=BF16),
+            (pltpu.HBM if hbm else jax.ShapeDtypeStruct)((columns, full), BF16),
             place, *pieces,
             scratch=[pltpu.VMEM((4, columns, pad), BF16)],
             limit=6,
@@ -308,23 +330,17 @@
     for degree in range(TAYLOR, 0, -1):
         next_fars, next_cores = [], []
         for chunk in count:
-            near = call(
-                forward_near,
-                [wides[chunk]] + [blocks[chunk]] * (degree == TAYLOR),
-                current[chunk], after(cores[chunk], token), panel,
-            )
-            if degree == TAYLOR:
-                x[chunk] = near[1]
-            far = after(fars[chunk], near[0])
-            most, *halves = call(
-                forward_far, [wides[chunk]] + parts[chunk], near[0], far, panel
+            far = after(fars[chunk], token)
+            halves = call(halved, parts[chunk], far)
+            most = call(
+                forward_most, wides[chunk], current[chunk], after(cores[chunk], halves[0]), far, panel
             )
             diag = [over_row(half, 1) for half in halves]
             stored[chunk].append((current[chunk], cores[chunk], far, *diag))
             final = degree == 1 and chunk == CHUNKS - 1
             value = call(
                 functools.partial(forward_last, degree),
-                shape(columns, pad, dtype=BF16) if final else blocks[chunk],
+                pltpu.HBM((columns, pad), BF16) if final else blocks[chunk],
                 step, x[chunk], most, panel, *diag,
                 *(current[:-1] if final else []),
             )
@@ -336,11 +352,11 @@
         fars, cores = next_fars, next_cores
         pieces = [piece for chunk in count for piece in stored[chunk][-1]]
         place = after(me_arr, token)
-        if degree > 1:
-            token = write_columns(place, pieces)
-            rights.append(token)
-
-    current[-1], rc = lax.optimization_barrier((current[-1], rc))
+        token = write_columns(place, pieces)
+        rights.append(token)
+
+    current[-1], rc, token = lax.optimization_barrier((current[-1], rc, token))
+    rights[-1] = token
     swapped = over_cuts(current[-1].reshape(group, part, pad))
     field, cmap, coupled, sums = call(
         functools.partial(merge, levels, rows),
@@ -356,12 +372,11 @@
     s1, s2, s3 = (over_row(sums, mask) for mask in (1, 2, 3))
     grad = call(
         functools.partial(unmerge, levels, full, 1.0 / math.sqrt(columns)),
-        shape(group, part, pad, dtype=BF16),
+        pltpu.HBM((group, part, pad), BF16),
         field, cmap, coupled, sums, s1, s2, s3,
     )
     whole = over_cuts(grad).reshape(columns, pad)
-    token = write_columns(after(place, grad), pieces)
-    rights.append(token)
+    token = whole
 
     total = [None] * CHUNKS
     pending = [None] * CHUNKS
@@ -385,22 +400,21 @@
                 )
             scaled_all.append(scaled)
             diag = [over_row(half, 1) for half in sent]
-            sent = call(backward_far, blocks[chunk], scaled, panel, *diag)
+            sent, near, most = call(
+                backward_most, [blocks[chunk], wides[chunk], wides[chunk]], after(scaled, sent[0]), panel
+            )
+            core = over_row(sent, 1)
+            sent = call(backward_last, blocks[chunk], most, *diag)
             far = over_row(sent, 2)
-            sent, near = call(backward_near, (blocks[chunk], wides[chunk]), after(scaled, sent), panel)
-            core = over_row(sent, 1)
-            token = near
+            token = sent
             pending[chunk] = (near, core, far)
-    grad_matrix = pl.pallas_call(
-        functools.partial(outer, CHUNKS),
-        grid=(pad // LANES,),
-        out_shape=shape(rows, 1, full),
-        in_specs=[pl.BlockSpec((scaled.shape[0], LANES), lambda i: (0, i)) for scaled in scaled_all]
-        + [WHOLE] * TAYLOR,
-        out_specs=pl.BlockSpec((LANES, 1, full), lambda i: (i, 0, 0)),
-        compiler_params=pltpu.CompilerParams(vmem_limit_bytes=20 * 2**20),
-        cost_estimate=pl.CostEstimate(flops=0, transcendentals=0, bytes_accessed=1),
-    )(*scaled_all[:-1], after(scaled_all[-1], token), *rights[::-1])
+    lefts = [*scaled_all[:-1], after(scaled_all[-1], token)]
+    tiles = -(-rows // LANES)
+    top = tiles * 3 // 5
+    grad_matrix = outer_rows(0, top, lefts, rights, None, rows, full)
+    for late in pending[:-1]:
+        grad_matrix = after(grad_matrix, late[2])
+    grad_matrix = outer_rows(top, tiles - top, lefts, rights, grad_matrix, rows, full)
     args = []
     for chunk in count:
         near, core, far = pending[chunk]

time: 122 us -> 116 us (0.951)
  blocking collectives: 17.4 us -> 32.5 us
  local copies, waits for them, and re-layouts: 18.1 us -> 4.2 us
  waiting for transfers between devices: 19.7 us -> 14.3 us
  starting transfers between devices: 34.3 us -> 30.2 us
  Pallas kernels: 29.9 us -> 32.8 us
    all_to_all x1 -> x2, blocking collectives: 17.4 us -> 32.5 us  [over_cuts(): lax.all_to_all(value, 'cuts', 0, 0, axis_index_groups=groups, tiled=True)]
    unnamed x60 -> x18, local copies, waits for them, and re-layouts: 18.1 us -> 4.2 us
    all_to_all x2 -> x1, starting transfers between devices: 11.5 us -> 7.25 us  [over_cuts(): lax.all_to_all(value, 'cuts', 0, 0, axis_index_groups=groups, tiled=True)]
    ppermute x51, waiting for transfers between devices: 17.7 us -> 14.3 us  [over_row(): return lax.ppermute(value, 'row', pairs)]
    all_to_all x2 -> x1, waiting for transfers between devices: 2.07 us -> 0.01 us  [over_cuts(): lax.all_to_all(value, 'cuts', 0, 0, axis_index_groups=groups, tiled=True)]
    pallas_call x45, Pallas kernels: 24.4 us -> 26.4 us  [call(): pl.pallas_call(body, out_shape=out_shape, in_specs=[SCALAR if arg.size <=...]
    pallas_call x1 -> x2, Pallas kernels: 5.51 us -> 6.4 us  [outer_rows(): pl.pallas_call(body, grid=(tiles,), out_shape=shape(rows, 1, full), in_sp...]
  transfers between devices with their start and end apart: 53 -> 52, of which waited for: 32 -> 21; matrix products, arithmetic and copies ran while one was open for 0% -> 0% of each run, Pallas kernels for 18% -> 23%
where the time goes in v3:
time: 116 us
  Pallas kernels  32.8 us (28%)
  blocking collectives  32.5 us (28%)
  starting transfers between devices  30.2 us (26%)
  waiting for transfers between devices  14.3 us (12%)
  local copies, waits for them, and re-layouts  4.2 us (4%)
  between operations  1.81 us (2%)
    all_to_all x2, blocking collectives, over_cuts(): lax.all_to_all(value, 'cuts', 0, 0, axis_index_groups=groups, tiled=True)  32.5 us
    pallas_call x45, Pallas kernels, call(): pl.pallas_call(body, out_shape=out_shape, in_specs=[SCALAR if arg.size <=...  26.4 us
    ppermute x51, starting transfers between devices, over_row(): return lax.ppermute(value, 'row', pairs)  22.9 us
    ppermute x51, waiting for transfers between devices, over_row(): return lax.ppermute(value, 'row', pairs)  14.3 us
    all_to_all x1, starting transfers between devices, over_cuts(): lax.all_to_all(value, 'cuts', 0, 0, axis_index_groups=groups, tiled=True)  7.25 us
    pallas_call x2, Pallas kernels, outer_rows(): pl.pallas_call(body, grid=(tiles,), out_shape=shape(rows, 1, full), in_sp...  6.4 us
    unnamed x18, local copies, waits for them, and re-layouts  4.2 us
  transfers between devices with their start and end apart: 52, of which 21 were waited for; matrix products, arithmetic and copies ran while one was open for 0% of the time, Pallas kernels for 23%

profile of v3, /device:TPU:0, one launch (start us, length us, event | category | flops | bytes accessed | tf_op | source)
XLA Modules:
  0.0 115.8 jit_solution(9267763579972530631)
XLA Ops:
  0.7 1.5 %copy-done.4 = f32[1,3,601,256]{3,0,2,1:T(1,128)S(1)} copy-done((f32[1,3,601,256]{3,0,2,1:T(1,128)S(1)}, f32[1,3,601,256]{3,0,2,1:T(1,128)}, u32[]{:S(2)}) %copy-start.4) | copy-done | bytes 1846296
  2.2 0.8 copy-done.6
  3.0 1.9 %shard_map.86 = bf16[8,32,2048]{2,1,0:T(8,128)(2,1)} custom-call(f32[3,601,1,256]{3,2,1,0:T(1,128)S(1)} %bitcast.11, f32[64,256]{1,0:T(8,128)S(1)} %bitcast.14), custom_call_target="tpu_custom_call" | custom-call | bytes 1 | tf_op jit(solution)/shard_map/pallas_call | solution.py:30
  4.8 7.3 %all-to-all-start = ((bf16[8,32,2048]{2,1,0:T(8,128)(2,1)}), bf16[8,32,2048]{2,1,0:T(8,128)(2,1)}, u32[]{:S(2)}, u32[]{:S(2)}) async-start(bf16[8,32,2048]{2,1,0:T(8,128)(2,1)} %shard_map.86), calls=%async_computation | async-start | bytes 2097152 | tf_op jit(solution)/shard_map/all_to_all | solution.py:67
  12.3 1.6 %collective-permute-start.3 = (bf16[128,640]{1,0:T(8,128)(2,1)S(1)}, bf16[128,640]{1,0:T(8,128)(2,1)S(1)}, u32[]{:S(2)}, u32[]{:S(2)}) collective-permute-start(bf16[128,640]{1,0:T(8,128)(2,1)S(1)} %get-tuple-element.100.own_ref.x_ref.refs_0_), channel_id=1, source_target_pairs={{0,2},{1,3},{2,0},{3,1},{4,6},{5,7},{6,4},{7,5},{8,10},{9,11},{10,... | collective-permute-start | bytes 491528 | tf_op jit(solution)/shard_map/ppermute | solution.py:58
  15.0 1.8 %copy-done.3 = bf16[1,601,2404]{2,1,0:T(8,128)(2,1)S(1)} copy-done((bf16[1,601,2404]{2,1,0:T(8,128)(2,1)S(1)}, bf16[1,601,2404]{2,1,0:T(8,128)(2,1)}, u32[]{:S(2)}) %copy-start.3) | copy-done | bytes 2889632
  16.9 1.4 %shard_map.88 = (bf16[4,640,640]{2,1,0:T(8,128)(2,1)S(1)}, f32[8,128]{1,0:T(8,128)S(1)}) custom-call(s32[1]{0:T(128)} %bitcast.me_ref, s32[1]{0:T(128)S(6)} %copy.11.profile_ref, f32[8]{0:T(128)S(1)} %copy-done.7, bf16[601,2404]{1,0:T(8,128)(2,1)S(1)} %bitcast.10), custom_call_target="tpu_custom_call" | custom-call | bytes 1 | tf_op jit(solution)/shard_map/pallas_call | solution.py:30
  21.0 2.0 %collective-permute-start.11 = (bf16[128,640]{1,0:T(8,128)(2,1)S(1)}, bf16[128,640]{1,0:T(8,128)(2,1)S(1)}, u32[]{:S(2)}, u32[]{:S(2)}) collective-permute-start(bf16[128,640]{1,0:T(8,128)(2,1)S(1)} %shard_map.91.own_ref.refs_0_), channel_id=1, source_target_pairs={{0,2},{1,3},{2,0},{3,1},{4,6},{5,7},{6,4},{7,5},{8,10},{9,11},{10,... | collective-permute-start | bytes 491528 | tf_op jit(solution)/shard_map/ppermute | solution.py:58
  25.3 1.5 %shard_map.95.refs_8_ = bf16[256,2404]{1,0:T(8,128)(2,1)} custom-call(s32[1]{0:T(128)} %bitcast.me_ref, bf16[128,640]{1,0:T(8,128)(2,1)S(1)} %get-tuple-element.100.own_ref.x_ref.refs_0_, bf16[128,640]{1,0:T(8,128)(2,1)S(1)} %collective-permute-done.2.core_ref.refs_1_, bf16[128,640]{1,0:T(8,128)(2,1)S(1)} %collective-permute-done.3.value_ref.far_ref.refs_2_, ...), custom_call_target="tpu_custom_call" | custom-call | bytes 1 | tf_op jit(solution)/shard_map/pallas_call | solution.py:30
  26.9 0.9 collective-permute-done.11.value_ref.far_ref.refs_2_
  29.7 2.3 %collective-permute-start.19 = (bf16[128,640]{1,0:T(8,128)(2,1)S(1)}, bf16[128,640]{1,0:T(8,128)(2,1)S(1)}, u32[]{:S(2)}, u32[]{:S(2)}) collective-permute-start(bf16[128,640]{1,0:T(8,128)(2,1)S(1)} %shard_map.98.own_ref.refs_0_), channel_id=1, source_target_pairs={{0,2},{1,3},{2,0},{3,1},{4,6},{5,7},{6,4},{7,5},{8,10},{9,11},{10,... | collective-permute-start | bytes 491528 | tf_op jit(solution)/shard_map/ppermute | solution.py:58
  34.0 1.0 collective-permute-start.17
  35.0 1.5 %shard_map.102.refs_7_ = bf16[256,2404]{1,0:T(8,128)(2,1)} custom-call(s32[1]{0:T(128)} %bitcast.me_ref, bf16[128,640]{1,0:T(8,128)(2,1)S(1)} %shard_map.91.own_ref.refs_0_, bf16[128,640]{1,0:T(8,128)(2,1)S(1)} %collective-permute-done.10.core_ref.refs_1_, bf16[128,640]{1,0:T(8,128)(2,1)S(1)} %collective-permute-done.11.value_ref.far_ref.refs_2_, ...), custom_call_target="tpu_custom_call" | custom-call | bytes 1 | tf_op jit(solution)/shard_map/pallas_call | solution.py:30
  37.4 0.8 shard_map.104.most_ref
  38.7 1.8 %collective-permute-done.17.value_ref.far_ref.refs_7_ = bf16[128,640]{1,0:T(8,128)(2,1)S(1)} collective-permute-done((bf16[128,640]{1,0:T(8,128)(2,1)S(1)}, bf16[128,640]{1,0:T(8,128)(2,1)S(1)}, u32[]{:S(2)}, u32[]{:S(2)}) %collective-permute-start.17) | collective-permute-done | bytes 163872 | tf_op jit(solution)/shard_map/ppermute | solution.py:58
  42.0 1.1 shard_map.108
  43.1 1.5 %shard_map.109.refs_6_ = bf16[256,2404]{1,0:T(8,128)(2,1)} custom-call(s32[1]{0:T(128)} %bitcast.me_ref, bf16[128,640]{1,0:T(8,128)(2,1)S(1)} %shard_map.98.own_ref.refs_0_, bf16[128,640]{1,0:T(8,128)(2,1)S(1)} %collective-permute-done.18.core_ref.refs_1_, bf16[128,640]{1,0:T(8,128)(2,1)S(1)} %collective-permute-done.19.value_ref.far_ref.refs_2_, ...), custom_call_target="tpu_custom_call" | custom-call | bytes 1 | tf_op jit(solution)/shard_map/pallas_call | solution.py:30
  44.6 17.4 %all_to_all.15.w_ref = bf16[8,32,640]{2,1,0:T(8,128)(2,1)S(1)} all-to-all(bf16[8,32,640]{2,1,0:T(8,128)(2,1)} %bitcast.17), channel_id=1, replica_groups=mesh['cuts'=8,'row'=4] {'cuts'}, dimensions={0} | all-to-all | bytes 655360 | tf_op jit(solution)/shard_map/all_to_all | solution.py:67
  62.1 2.0 %shard_map.110 = (f32[8,32,640]{2,1,0:T(8,128)S(1)}, f32[8,32,640]{2,1,0:T(8,128)S(1)}, bf16[8,32,1920]{2,1,0:T(8,128)(2,1)S(1)}, f32[8,256]{1,0:T(8,128)S(1)}) custom-call(s32[1]{0:T(128)} %bitcast.me_ref, s32[1,64]{1,0:T(1,128)S(1)} %bitcast.15, bf16[8,32,640]{2,1,0:T(8,128)(2,1)S(1)} %all_to_all.15.w_ref, bf16[8,32,2048]{2,1,0:T(8,128)(2,1)} %all-to-all-done.rc_ref), custom_call_target="tpu_custom_call" | custom-call | bytes 1 | tf_op jit(solution)/shard_map/pallas_call | solution.py:30
  64.1 1.6 %collective-permute-start.25 = (f32[8,256]{1,0:T(8,128)S(1)}, f32[8,256]{1,0:T(8,128)S(1)}, u32[]{:S(2)}, u32[]{:S(2)}) collective-permute-start(f32[8,256]{1,0:T(8,128)S(1)} %get-tuple-element.137.s0), channel_id=1, source_target_pairs={{0,2},{1,3},{2,0},{3,1},{4,6},{5,7},{6,4},{7,5},{8,10},{9,11},{10,... | collective-permute-start | bytes 24584 | tf_op jit(solution)/shard_map/ppermute | solution.py:58
  65.9 1.2 %collective-permute-done.26.s3 = f32[8,256]{1,0:T(8,128)S(1)} collective-permute-done((f32[8,256]{1,0:T(8,128)S(1)}, f32[8,256]{1,0:T(8,128)S(1)}, u32[]{:S(2)}, u32[]{:S(2)}) %collective-permute-start.26) | collective-permute-done | bytes 8224 | tf_op jit(solution)/shard_map/ppermute | solution.py:58
  67.8 1.3 %shard_map.111 = bf16[8,32,640]{2,1,0:T(8,128)(2,1)} custom-call(f32[8,32,640]{2,1,0:T(8,128)S(1)} %get-tuple-element.134.field_ref, f32[8,32,640]{2,1,0:T(8,128)S(1)} %get-tuple-element.135.cmap_ref, bf16[8,32,1920]{2,1,0:T(8,128)(2,1)S(1)} %get-tuple-element.136.rc_ref, f32[8,256]{1,0:T(8,128)S(1)} %get-tuple-element.137.s0, ...), custom_call_target="tpu_custom_call" | custom-call | bytes 1 | tf_op jit(solution)/shard_map/pallas_call | solution.py:30
  69.0 15.1 %all_to_all.16 = bf16[8,32,640]{2,1,0:T(8,128)(2,1)S(1)} all-to-all(bf16[8,32,640]{2,1,0:T(8,128)(2,1)} %shard_map.111), channel_id=1, replica_groups=mesh['cuts'=8,'row'=4] {'cuts'}, dimensions={0} | all-to-all | bytes 655360 | tf_op jit(solution)/shard_map/all_to_all | solution.py:67
  88.9 1.5 %collective-permute-start.34 = (bf16[128,640]{1,0:T(8,128)(2,1)S(1)}, bf16[128,640]{1,0:T(8,128)(2,1)S(1)}, u32[]{:S(2)}, u32[]{:S(2)}) collective-permute-start(bf16[128,640]{1,0:T(8,128)(2,1)S(1)} %shard_map.117), channel_id=1, source_target_pairs={{0,2},{1,3},{2,0},{3,1},{4,6},{5,7},{6,4},{7,5},{8,10},{9,11},{10,... | collective-permute-start | bytes 491528 | tf_op jit(solution)/shard_map/ppermute | solution.py:58
  90.4 2.7 %collective-permute-done.30.far_ref = bf16[128,640]{1,0:T(8,128)(2,1)S(1)} collective-permute-done((bf16[128,640]{1,0:T(8,128)(2,1)S(1)}, bf16[128,640]{1,0:T(8,128)(2,1)S(1)}, u32[]{:S(2)}, u32[]{:S(2)}) %collective-permute-start.30) | collective-permute-done | bytes 163872 | tf_op jit(solution)/shard_map/ppermute | solution.py:58
  97.9 1.5 %collective-permute-start.42 = (bf16[128,640]{1,0:T(8,128)(2,1)S(1)}, bf16[128,640]{1,0:T(8,128)(2,1)S(1)}, u32[]{:S(2)}, u32[]{:S(2)}) collective-permute-start(bf16[128,640]{1,0:T(8,128)(2,1)S(1)} %shard_map.123), channel_id=1, source_target_pairs={{0,2},{1,3},{2,0},{3,1},{4,6},{5,7},{6,4},{7,5},{8,10},{9,11},{10,... | collective-permute-start | bytes 491528 | tf_op jit(solution)/shard_map/ppermute | solution.py:58
  99.4 2.6 %collective-permute-done.38.far_ref = bf16[128,640]{1,0:T(8,128)(2,1)S(1)} collective-permute-done((bf16[128,640]{1,0:T(8,128)(2,1)S(1)}, bf16[128,640]{1,0:T(8,128)(2,1)S(1)}, u32[]{:S(2)}, u32[]{:S(2)}) %collective-permute-start.38) | collective-permute-done | bytes 163872 | tf_op jit(solution)/shard_map/ppermute | solution.py:58
  104.0 1.1 collective-permute-done.42.far_ref
  107.2 1.0 collective-permute-start.50
  108.3 3.8 %shard_map.130.refs_9_ = f32[601,1,2404]{2,1,0:T(1,128)} custom-call(bf16[128,640]{1,0:T(8,128)(2,1)S(1)} %get-tuple-element.141.scaled_ref.refs_0_, bf16[128,640]{1,0:T(8,128)(2,1)S(1)} %get-tuple-element.149.scaled_ref.refs_1_, bf16[128,640]{1,0:T(8,128)(2,1)S(1)} %get-tuple-element.158.scaled_ref.refs_2_, ...), custom_call_target="tpu_custom_call" | custom-call | bytes 1 | tf_op jit(solution)/shard_map/pallas_call | solution.py:257
  112.0 2.6 %shard_map.131 = f32[601,1,2404]{2,1,0:T(1,128)} custom-call(bf16[128,640]{1,0:T(8,128)(2,1)S(1)} %get-tuple-element.141.scaled_ref.refs_0_, bf16[128,640]{1,0:T(8,128)(2,1)S(1)} %get-tuple-element.149.scaled_ref.refs_1_, bf16[128,640]{1,0:T(8,128)(2,1)S(1)} %get-tuple-element.158.scaled_ref.refs_2_, ...), custom_call_target="tpu_custom_call", output_to_operand_aliasing={{}: (9, {})} | custom-call | flops 5000000000 | bytes 1 | tf_op jit(solution)/shard_map/pallas_call | solution.py:257
  114.7 1.2 %shard_map.132 = f32[601,1,256]{2,1,0:T(1,128)} custom-call(f32[128,640]{1,0:T(8,128)S(1)} %get-tuple-element.189.refs_0_, f32[128,640]{1,0:T(8,128)S(1)} %get-tuple-element.190.refs_1_, bf16[128,640]{1,0:T(8,128)(2,1)S(1)} %collective-permute-done.48.refs_2_, bf16[128,640]{1,0:T(8,128)(2,1)S(1)} %collective-permute-done.47.refs_3_, ...), custom_call_target="tpu_custom_call" | custom-call | bytes 1 | tf_op jit(solution)/shard_map/pallas_call | solution.py:30
  (139 shorter events, 26.8 us)
Async XLA Ops:
  4.8 39.8 %all-to-all-start = ((bf16[8,32,2048]{2,1,0:T(8,128)(2,1)}), bf16[8,32,2048]{2,1,0:T(8,128)(2,1)}, u32[]{:S(2)}, u32[]{:S(2)}) async-start(bf16[8,32,2048]{2,1,0:T(8,128)(2,1)} %shard_map.86), calls=%async_computation | async-start | bytes 2097152 | tf_op jit(solution)/shard_map/all_to_all | solution.py:67
  12.3 6.8 %collective-permute-start.3 = (bf16[128,640]{1,0:T(8,128)(2,1)S(1)}, bf16[128,640]{1,0:T(8,128)(2,1)S(1)}, u32[]{:S(2)}, u32[]{:S(2)}) collective-permute-start(bf16[128,640]{1,0:T(8,128)(2,1)S(1)} %get-tuple-element.100.own_ref.x_ref.refs_0_), channel_id=1, source_target_pairs={{0,2},{1,3},{2,0},{3,1},{4,6},{5,7},{6,4},{7,5},{8,10},{9,11},{10,... | collective-permute-start | bytes 491528 | tf_op jit(solution)/shard_map/ppermute | solution.py:58
  13.9 5.8 %collective-permute-start.2 = (bf16[128,640]{1,0:T(8,128)(2,1)S(1)}, bf16[128,640]{1,0:T(8,128)(2,1)S(1)}, u32[]{:S(2)}, u32[]{:S(2)}) collective-permute-start(bf16[128,640]{1,0:T(8,128)(2,1)S(1)} %get-tuple-element.100.own_ref.x_ref.refs_0_), channel_id=1, source_target_pairs={{0,1},{1,0},{2,3},{3,2},{4,5},{5,4},{6,7},{7,6},{8,9},{9,8},{10,11... | collective-permute-start | bytes 491528 | tf_op jit(solution)/shard_map/ppermute | solution.py:58
  13.9 9.1 %collective-permute-start.1 = (bf16[128,640]{1,0:T(8,128)(2,1)S(1)}, bf16[128,640]{1,0:T(8,128)(2,1)S(1)}, u32[]{:S(2)}, u32[]{:S(2)}) collective-permute-start(bf16[128,640]{1,0:T(8,128)(2,1)S(1)} %get-tuple-element.103.own_ref.x_ref.refs_5_), channel_id=1, source_target_pairs={{0,2},{1,3},{2,0},{3,1},{4,6},{5,7},{6,4},{7,5},{8,10},{9,11},{10,... | collective-permute-start | bytes 491528 | tf_op jit(solution)/shard_map/ppermute | solution.py:58
  19.6 4.1 %collective-permute-start = (bf16[128,640]{1,0:T(8,128)(2,1)S(1)}, bf16[128,640]{1,0:T(8,128)(2,1)S(1)}, u32[]{:S(2)}, u32[]{:S(2)}) collective-permute-start(bf16[128,640]{1,0:T(8,128)(2,1)S(1)} %get-tuple-element.103.own_ref.x_ref.refs_5_), channel_id=1, source_target_pairs={{0,1},{1,0},{2,3},{3,2},{4,5},{5,4},{6,7},{7,6},{8,9},{9,8},{10,11... | collective-permute-start | bytes 491528 | tf_op jit(solution)/shard_map/ppermute | solution.py:58
  21.0 6.8 %collective-permute-start.11 = (bf16[128,640]{1,0:T(8,128)(2,1)S(1)}, bf16[128,640]{1,0:T(8,128)(2,1)S(1)}, u32[]{:S(2)}, u32[]{:S(2)}) collective-permute-start(bf16[128,640]{1,0:T(8,128)(2,1)S(1)} %shard_map.91.own_ref.refs_0_), channel_id=1, source_target_pairs={{0,2},{1,3},{2,0},{3,1},{4,6},{5,7},{6,4},{7,5},{8,10},{9,11},{10,... | collective-permute-start | bytes 491528 | tf_op jit(solution)/shard_map/ppermute | solution.py:58
  23.0 1.6 %collective-permute-start.7 = (bf16[64,640]{1,0:T(8,128)(2,1)S(1)}, bf16[64,640]{1,0:T(8,128)(2,1)S(1)}, u32[]{:S(2)}, u32[]{:S(2)}) collective-permute-start(bf16[64,640]{1,0:T(8,128)(2,1)S(1)} %get-tuple-element.112), channel_id=1, source_target_pairs={{0,1},{1,0},{2,3},{3,2},{4,5},{5,4},{6,7},{7,6},{8,9},{9,8},{10,11... | collective-permute-start | bytes 245768 | tf_op jit(solution)/shard_map/ppermute | solution.py:58
  23.6 4.9 %collective-permute-start.10 = (bf16[128,640]{1,0:T(8,128)(2,1)S(1)}, bf16[128,640]{1,0:T(8,128)(2,1)S(1)}, u32[]{:S(2)}, u32[]{:S(2)}) collective-permute-start(bf16[128,640]{1,0:T(8,128)(2,1)S(1)} %shard_map.91.own_ref.refs_0_), channel_id=1, source_target_pairs={{0,1},{1,0},{2,3},{3,2},{4,5},{5,4},{6,7},{7,6},{8,9},{9,8},{10,11... | collective-permute-start | bytes 491528 | tf_op jit(solution)/shard_map/ppermute | solution.py:58
  25.0 7.0 %collective-permute-start.9 = (bf16[128,640]{1,0:T(8,128)(2,1)S(1)}, bf16[128,640]{1,0:T(8,128)(2,1)S(1)}, u32[]{:S(2)}, u32[]{:S(2)}) collective-permute-start(bf16[128,640]{1,0:T(8,128)(2,1)S(1)} %shard_map.94.own_ref.refs_5_), channel_id=1, source_target_pairs={{0,2},{1,3},{2,0},{3,1},{4,6},{5,7},{6,4},{7,5},{8,10},{9,11},{10,... | collective-permute-start | bytes 491528 | tf_op jit(solution)/shard_map/ppermute | solution.py:58
  28.4 4.4 %collective-permute-start.8 = (bf16[128,640]{1,0:T(8,128)(2,1)S(1)}, bf16[128,640]{1,0:T(8,128)(2,1)S(1)}, u32[]{:S(2)}, u32[]{:S(2)}) collective-permute-start(bf16[128,640]{1,0:T(8,128)(2,1)S(1)} %shard_map.94.own_ref.refs_5_), channel_id=1, source_target_pairs={{0,1},{1,0},{2,3},{3,2},{4,5},{5,4},{6,7},{7,6},{8,9},{9,8},{10,11... | collective-permute-start | bytes 491528 | tf_op jit(solution)/shard_map/ppermute | solution.py:58
  29.7 7.1 %collective-permute-start.19 = (bf16[128,640]{1,0:T(8,128)(2,1)S(1)}, bf16[128,640]{1,0:T(8,128)(2,1)S(1)}, u32[]{:S(2)}, u32[]{:S(2)}) collective-permute-start(bf16[128,640]{1,0:T(8,128)(2,1)S(1)} %shard_map.98.own_ref.refs_0_), channel_id=1, source_target_pairs={{0,2},{1,3},{2,0},{3,1},{4,6},{5,7},{6,4},{7,5},{8,10},{9,11},{10,... | collective-permute-start | bytes 491528 | tf_op jit(solution)/shard_map/ppermute | solution.py:58
  32.0 1.6 %collective-permute-start.15 = (bf16[64,640]{1,0:T(8,128)(2,1)S(1)}, bf16[64,640]{1,0:T(8,128)(2,1)S(1)}, u32[]{:S(2)}, u32[]{:S(2)}) collective-permute-start(bf16[64,640]{1,0:T(8,128)(2,1)S(1)} %get-tuple-element.121), channel_id=1, source_target_pairs={{0,1},{1,0},{2,3},{3,2},{4,5},{5,4},{6,7},{7,6},{8,9},{9,8},{10,11... | collective-permute-start | bytes 245768 | tf_op jit(solution)/shard_map/ppermute | solution.py:58
  32.6 4.9 %collective-permute-start.18 = (bf16[128,640]{1,0:T(8,128)(2,1)S(1)}, bf16[128,640]{1,0:T(8,128)(2,1)S(1)}, u32[]{:S(2)}, u32[]{:S(2)}) collective-permute-start(bf16[128,640]{1,0:T(8,128)(2,1)S(1)} %shard_map.98.own_ref.refs_0_), channel_id=1, source_target_pairs={{0,1},{1,0},{2,3},{3,2},{4,5},{5,4},{6,7},{7,6},{8,9},{9,8},{10,11... | collective-permute-start | bytes 491528 | tf_op jit(solution)/shard_map/ppermute | solution.py:58
  34.0 6.5 %collective-permute-start.17 = (bf16[128,640]{1,0:T(8,128)(2,1)S(1)}, bf16[128,640]{1,0:T(8,128)(2,1)S(1)}, u32[]{:S(2)}, u32[]{:S(2)}) collective-permute-start(bf16[128,640]{1,0:T(8,128)(2,1)S(1)} %shard_map.101.own_ref.refs_5_), channel_id=1, source_target_pairs={{0,2},{1,3},{2,0},{3,1},{4,6},{5,7},{6,4},{7,5},{8,10},{9,11},{10,... | collective-permute-start | bytes 491528 | tf_op jit(solution)/shard_map/ppermute | solution.py:58
  37.4 3.7 %collective-permute-start.16 = (bf16[128,640]{1,0:T(8,128)(2,1)S(1)}, bf16[128,640]{1,0:T(8,128)(2,1)S(1)}, u32[]{:S(2)}, u32[]{:S(2)}) collective-permute-start(bf16[128,640]{1,0:T(8,128)(2,1)S(1)} %shard_map.101.own_ref.refs_5_), channel_id=1, source_target_pairs={{0,1},{1,0},{2,3},{3,2},{4,5},{5,4},{6,7},{7,6},{8,9},{9,8},{10,11... | collective-permute-start | bytes 491528 | tf_op jit(solution)/shard_map/ppermute | solution.py:58
  64.0 3.1 %collective-permute-start.26 = (f32[8,256]{1,0:T(8,128)S(1)}, f32[8,256]{1,0:T(8,128)S(1)}, u32[]{:S(2)}, u32[]{:S(2)}) collective-permute-start(f32[8,256]{1,0:T(8,128)S(1)} %get-tuple-element.137.s0), channel_id=1, source_target_pairs={{0,3},{1,2},{2,1},{3,0},{4,7},{5,6},{6,5},{7,4},{8,11},{9,10},{10,... | collective-permute-start | bytes 24584 | tf_op jit(solution)/shard_map/ppermute | solution.py:58
  64.1 3.7 %collective-permute-start.25 = (f32[8,256]{1,0:T(8,128)S(1)}, f32[8,256]{1,0:T(8,128)S(1)}, u32[]{:S(2)}, u32[]{:S(2)}) collective-permute-start(f32[8,256]{1,0:T(8,128)S(1)} %get-tuple-element.137.s0), channel_id=1, source_target_pairs={{0,2},{1,3},{2,0},{3,1},{4,6},{5,7},{6,4},{7,5},{8,10},{9,11},{10,... | collective-permute-start | bytes 24584 | tf_op jit(solution)/shard_map/ppermute | solution.py:58
  65.7 2.1 %collective-permute-start.24 = (f32[8,256]{1,0:T(8,128)S(1)}, f32[8,256]{1,0:T(8,128)S(1)}, u32[]{:S(2)}, u32[]{:S(2)}) collective-permute-start(f32[8,256]{1,0:T(8,128)S(1)} %get-tuple-element.137.s0), channel_id=1, source_target_pairs={{0,1},{1,0},{2,3},{3,2},{4,5},{5,4},{6,7},{7,6},{8,9},{9,8},{10,11... | collective-permute-start | bytes 24584 | tf_op jit(solution)/shard_map/ppermute | solution.py:58
  86.0 7.1 %collective-permute-start.30 = (bf16[128,640]{1,0:T(8,128)(2,1)S(1)}, bf16[128,640]{1,0:T(8,128)(2,1)S(1)}, u32[]{:S(2)}, u32[]{:S(2)}) collective-permute-start(bf16[128,640]{1,0:T(8,128)(2,1)S(1)} %shard_map.114), channel_id=1, source_target_pairs={{0,2},{1,3},{2,0},{3,1},{4,6},{5,7},{6,4},{7,5},{8,10},{9,11},{10,... | collective-permute-start | bytes 491528 | tf_op jit(solution)/shard_map/ppermute | solution.py:58
  86.7 6.4 %collective-permute-start.29 = (bf16[128,640]{1,0:T(8,128)(2,1)S(1)}, bf16[128,640]{1,0:T(8,128)(2,1)S(1)}, u32[]{:S(2)}, u32[]{:S(2)}) collective-permute-start(bf16[128,640]{1,0:T(8,128)(2,1)S(1)} %get-tuple-element.147), channel_id=1, source_target_pairs={{0,1},{1,0},{2,3},{3,2},{4,5},{5,4},{6,7},{7,6},{8,9},{9,8},{10,11... | collective-permute-start | bytes 491528 | tf_op jit(solution)/shard_map/ppermute | solution.py:58
  88.9 7.2 %collective-permute-start.34 = (bf16[128,640]{1,0:T(8,128)(2,1)S(1)}, bf16[128,640]{1,0:T(8,128)(2,1)S(1)}, u32[]{:S(2)}, u32[]{:S(2)}) collective-permute-start(bf16[128,640]{1,0:T(8,128)(2,1)S(1)} %shard_map.117), channel_id=1, source_target_pairs={{0,2},{1,3},{2,0},{3,1},{4,6},{5,7},{6,4},{7,5},{8,10},{9,11},{10,... | collective-permute-start | bytes 491528 | tf_op jit(solution)/shard_map/ppermute | solution.py:58
  90.4 5.7 %collective-permute-start.33 = (bf16[128,640]{1,0:T(8,128)(2,1)S(1)}, bf16[128,640]{1,0:T(8,128)(2,1)S(1)}, u32[]{:S(2)}, u32[]{:S(2)}) collective-permute-start(bf16[128,640]{1,0:T(8,128)(2,1)S(1)} %get-tuple-element.156), channel_id=1, source_target_pairs={{0,1},{1,0},{2,3},{3,2},{4,5},{5,4},{6,7},{7,6},{8,9},{9,8},{10,11... | collective-permute-start | bytes 491528 | tf_op jit(solution)/shard_map/ppermute | solution.py:58
  95.0 7.0 %collective-permute-start.38 = (bf16[128,640]{1,0:T(8,128)(2,1)S(1)}, bf16[128,640]{1,0:T(8,128)(2,1)S(1)}, u32[]{:S(2)}, u32[]{:S(2)}) collective-permute-start(bf16[128,640]{1,0:T(8,128)(2,1)S(1)} %shard_map.120), channel_id=1, source_target_pairs={{0,2},{1,3},{2,0},{3,1},{4,6},{5,7},{6,4},{7,5},{8,10},{9,11},{10,... | collective-permute-start | bytes 491528 | tf_op jit(solution)/shard_map/ppermute | solution.py:58
  95.1 6.9 %collective-permute-start.37 = (bf16[128,640]{1,0:T(8,128)(2,1)S(1)}, bf16[128,640]{1,0:T(8,128)(2,1)S(1)}, u32[]{:S(2)}, u32[]{:S(2)}) collective-permute-start(bf16[128,640]{1,0:T(8,128)(2,1)S(1)} %get-tuple-element.165), channel_id=1, source_target_pairs={{0,1},{1,0},{2,3},{3,2},{4,5},{5,4},{6,7},{7,6},{8,9},{9,8},{10,11... | collective-permute-start | bytes 491528 | tf_op jit(solution)/shard_map/ppermute | solution.py:58
  97.9 7.1 %collective-permute-start.42 = (bf16[128,640]{1,0:T(8,128)(2,1)S(1)}, bf16[128,640]{1,0:T(8,128)(2,1)S(1)}, u32[]{:S(2)}, u32[]{:S(2)}) collective-permute-start(bf16[128,640]{1,0:T(8,128)(2,1)S(1)} %shard_map.123), channel_id=1, source_target_pairs={{0,2},{1,3},{2,0},{3,1},{4,6},{5,7},{6,4},{7,5},{8,10},{9,11},{10,... | collective-permute-start | bytes 491528 | tf_op jit(solution)/shard_map/ppermute | solution.py:58
  99.4 5.6 %collective-permute-start.41 = (bf16[128,640]{1,0:T(8,128)(2,1)S(1)}, bf16[128,640]{1,0:T(8,128)(2,1)S(1)}, u32[]{:S(2)}, u32[]{:S(2)}) collective-permute-start(bf16[128,640]{1,0:T(8,128)(2,1)S(1)} %get-tuple-element.174), channel_id=1, source_target_pairs={{0,1},{1,0},{2,3},{3,2},{4,5},{5,4},{6,7},{7,6},{8,9},{9,8},{10,11... | collective-permute-start | bytes 491528 | tf_op jit(solution)/shard_map/ppermute | solution.py:58
  103.9 8.2 %collective-permute-start.47 = (bf16[128,640]{1,0:T(8,128)(2,1)S(1)}, bf16[128,640]{1,0:T(8,128)(2,1)S(1)}, u32[]{:S(2)}, u32[]{:S(2)}) collective-permute-start(bf16[128,640]{1,0:T(8,128)(2,1)S(1)} %shard_map.126), channel_id=1, source_target_pairs={{0,2},{1,3},{2,0},{3,1},{4,6},{5,7},{6,4},{7,5},{8,10},{9,11},{10,... | collective-permute-start | bytes 491528 | tf_op jit(solution)/shard_map/ppermute | solution.py:58
  105.4 1.8 %collective-permute-start.46 = (bf16[64,640]{1,0:T(8,128)(2,1)S(1)}, bf16[64,640]{1,0:T(8,128)(2,1)S(1)}, u32[]{:S(2)}, u32[]{:S(2)}) collective-permute-start(bf16[64,640]{1,0:T(8,128)(2,1)S(1)} %get-tuple-element.185), channel_id=1, source_target_pairs={{0,1},{1,0},{2,3},{3,2},{4,5},{5,4},{6,7},{7,6},{8,9},{9,8},{10,11... | collective-permute-start | bytes 245768 | tf_op jit(solution)/shard_map/ppermute | solution.py:58
  105.5 1.7 %collective-permute-start.45 = (bf16[64,640]{1,0:T(8,128)(2,1)S(1)}, bf16[64,640]{1,0:T(8,128)(2,1)S(1)}, u32[]{:S(2)}, u32[]{:S(2)}) collective-permute-start(bf16[64,640]{1,0:T(8,128)(2,1)S(1)} %get-tuple-element.182), channel_id=1, source_target_pairs={{0,1},{1,0},{2,3},{3,2},{4,5},{5,4},{6,7},{7,6},{8,9},{9,8},{10,11... | collective-permute-start | bytes 245768 | tf_op jit(solution)/shard_map/ppermute | solution.py:58
  106.0 8.7 %collective-permute-start.48 = (bf16[128,640]{1,0:T(8,128)(2,1)S(1)}, bf16[128,640]{1,0:T(8,128)(2,1)S(1)}, u32[]{:S(2)}, u32[]{:S(2)}) collective-permute-start(bf16[128,640]{1,0:T(8,128)(2,1)S(1)} %get-tuple-element.191), channel_id=1, source_target_pairs={{0,1},{1,0},{2,3},{3,2},{4,5},{5,4},{6,7},{7,6},{8,9},{9,8},{10,11... | collective-permute-start | bytes 491528 | tf_op jit(solution)/shard_map/ppermute | solution.py:58
  106.7 8.0 %collective-permute-start.49 = (bf16[128,640]{1,0:T(8,128)(2,1)S(1)}, bf16[128,640]{1,0:T(8,128)(2,1)S(1)}, u32[]{:S(2)}, u32[]{:S(2)}) collective-permute-start(bf16[128,640]{1,0:T(8,128)(2,1)S(1)} %get-tuple-element.194), channel_id=1, source_target_pairs={{0,1},{1,0},{2,3},{3,2},{4,5},{5,4},{6,7},{7,6},{8,9},{9,8},{10,11... | collective-permute-start | bytes 491528 | tf_op jit(solution)/shard_map/ppermute | solution.py:58
  107.2 7.4 %collective-permute-start.50 = (bf16[128,640]{1,0:T(8,128)(2,1)S(1)}, bf16[128,640]{1,0:T(8,128)(2,1)S(1)}, u32[]{:S(2)}, u32[]{:S(2)}) collective-permute-start(bf16[128,640]{1,0:T(8,128)(2,1)S(1)} %shard_map.129), channel_id=1, source_target_pairs={{0,2},{1,3},{2,0},{3,1},{4,6},{5,7},{6,4},{7,5},{8,10},{9,11},{10,... | collective-permute-start | bytes 491528 | tf_op jit(solution)/shard_map/ppermute | solution.py:58
  (29 other events, 84.6 us)

commit v4 on v3

--- a/solution.py
+++ b/solution.py
@@ -98,21 +98,26 @@
         first += out_ref.shape[0]
 
 
-def coupling(reflect_ref, cotangent_ref, out_ref, tall):
-    levels, rows, _, columns = reflect_ref.shape
+def coupling(levels, reflect_ref, cotangent_ref, out_ref, tall):
+    rows = reflect_ref.shape[1]
     pad = tall.shape[0]
     group, part = out_ref.shape[:2]
-    tall[rows:, :] = jnp.zeros_like(tall[rows:, :])
-    cot = cotangent_ref[...].T
-    high = cot.astype(BF16)
-    low = (cot - high.astype(F32)).astype(BF16)
-    tracked = cot.shape[1]
-    first = levels * pad
-    out_ref[:, :, first : first + tracked] = high.reshape(group, part, tracked)
-    out_ref[:, :, first + tracked :] = low.reshape(group, part, tracked)
-    for level in range(levels):
-        tall[:rows, :] = reflect_ref[level, :, 0, :]
-        out_ref[:, :, level * pad : (level + 1) * pad] = tall[...].T.astype(BF16).reshape(group, part, pad)
+    level = pl.program_id(0)
+
+    @pl.when(level < levels)
+    def _():
+        tall[rows // 8 * 8 :, :] = jnp.zeros_like(tall[rows // 8 * 8 :, :])
+        tall[:rows, :] = reflect_ref[0, :, 0, :]
+        out_ref[...] = tall[...].T.astype(BF16).reshape(group, part, pad)
+
+    @pl.when(level == levels)
+    def _():
+        cot = cotangent_ref[...].T
+        high = cot.astype(BF16)
+        low = (cot - high.astype(F32)).astype(BF16)
+        tracked = cot.shape[1]
+        out_ref[:, :, :tracked] = high.reshape(group, part, tracked)
+        out_ref[:, :, tracked : 2 * tracked] = low.reshape(group, part, tracked)
 
 
 def halved(value_ref, *refs):
@@ -125,14 +130,36 @@
 
 
 def forward_last(degree, step_ref, x_ref, most_ref, panel_ref, *refs):
-    product = most_ref[...] + times_t(joined(refs[:HALVES]), panel_ref[3])
-    value = (x_ref[...].astype(F32) + step_ref[0:1, 0:1] / degree * product).astype(BF16)
-    out_ref = refs[-1]
-    first = 0
-    for ref in refs[HALVES:-1]:
-        out_ref[first : first + ref.shape[0]] = ref[...]
-        first += ref.shape[0]
+    product = most_ref[...] + times_t(joined(refs[:-1]), panel_ref[3])
+    refs[-1][...] = (x_ref[...].astype(F32) + step_ref[0:1, 0:1] / degree * product).astype(BF16)
+
+
+def forward_end(step_ref, x_ref, most_ref, panel_ref, me_ref, before_ref, *refs):
+    out_ref, pile_ref = refs[-2:]
+    pieces = refs[:-2]
+    diag = pieces[-HALVES:]
+    product = most_ref[...] + times_t(joined(diag), panel_ref[3])
+    value = (x_ref[...].astype(F32) + step_ref[0:1, 0:1] * product).astype(BF16)
+    first = before_ref.shape[0]
+    out_ref[:first] = before_ref[...]
     out_ref[first:] = value
+    places = pile_ref.shape[0]
+    each = places - 1 + HALVES
+    row = 0
+    for chunk in range(len(pieces) // each):
+        group = pieces[chunk * each : (chunk + 1) * each]
+        width = group[0].shape[0]
+        for place in range(places - 1):
+            pile_ref[me_ref[0] ^ place, row : row + width, :] = group[place][...]
+        pile_ref[me_ref[0] ^ (places - 1), row : row + width, :] = joined(group[places - 1 :])
+        row += width
+
+
+def columns_from(pile_ref, out_ref):
+    places = pile_ref.shape[0]
+    rows = out_ref.shape[1] // places
+    for block in range(places):
+        out_ref[:, block * rows : (block + 1) * rows] = pile_ref[block, :, :rows]
 
 
 def merge(levels, rows, me_ref, order_ref, w_ref, rc_ref, field_ref, cmap_ref, level_ref, sums_ref):
@@ -237,31 +264,45 @@
     refs[-1][...] = (most_ref[...] + joined(refs[:-1]).astype(F32)).astype(BF16)
 
 
-def outer(chunks, *refs):
-    out_ref = refs[-1]
-    rights = refs[TAYLOR * chunks : TAYLOR * chunks + TAYLOR]
-    total = None
-    for degree, right in enumerate(rights):
-        left = jnp.concatenate([ref[...] for ref in refs[degree * chunks : (degree + 1) * chunks]], axis=0)
-        value = lax.dot_general(left, right[...], (((0,), (0,)), ((), ())), preferred_element_type=F32)
-        total = value if total is None else total + value
-    out_ref[:, 0, :] = total
-
-
-def outer_rows(first, tiles, lefts, rights, target, rows, full):
-    body = functools.partial(outer, len(lefts) // TAYLOR)
+def product_rows(lefts, right, columns):
+    left = jnp.concatenate([ref[:, columns] for ref in lefts], axis=0)
+    return lax.dot_general(left, right[...], (((0,), (0,)), ((), ())), preferred_element_type=F32)
+
+
+def outer_early(*refs):
+    rights, out_ref = refs[-TAYLOR:-1], refs[-1]
+    chunks = (len(refs) - TAYLOR) // len(rights)
+
+    @pl.loop(0, out_ref.shape[0] // LANES)
+    def _(tile):
+        place = pl.ds(pl.multiple_of(tile * LANES, LANES), LANES)
+        values = [
+            product_rows(refs[term * chunks : (term + 1) * chunks], right, place)
+            for term, right in enumerate(rights)
+        ]
+        out_ref[place, :] = functools.reduce(jnp.add, values)
+
+
+def outer(chunks, first, *refs):
+    right, early, out_ref = refs[chunks], refs[chunks + 1], refs[-1]
+    tile = pl.program_id(0) + first
+    place = pl.ds(pl.multiple_of(tile * LANES, LANES), LANES)
+    out_ref[:, 0, :] = product_rows(refs[:chunks], right, slice(None)) + early[place, :]
+
+
+def outer_rows(first, tiles, lefts, right, early, target, rows, full):
     specs = [pl.BlockSpec((left.shape[0], LANES), lambda i: (0, i + first)) for left in lefts]
-    args = [*lefts, *rights[::-1]]
+    args = [*lefts, right, early]
     if target is not None:
         args.append(target)
     return pl.pallas_call(
-        body,
+        functools.partial(outer, len(lefts), first),
         grid=(tiles,),
         out_shape=shape(rows, 1, full),
-        in_specs=specs + [WHOLE] * TAYLOR + [pl.BlockSpec(memory_space=pl.ANY)] * (target is not None),
+        in_specs=specs + [WHOLE] * 2 + [pl.BlockSpec(memory_space=pl.ANY)] * (target is not None),
         out_specs=pl.BlockSpec((LANES, 1, full), lambda i: (i + first, 0, 0)),
         input_output_aliases={} if target is None else {len(args) - 1: 0},
-        compiler_params=pltpu.CompilerParams(vmem_limit_bytes=20 * 2**20),
+        compiler_params=pltpu.CompilerParams(vmem_limit_bytes=16 * 2**20),
         cost_estimate=pl.CostEstimate(flops=0 if target is None else COST, transcendentals=0, bytes_accessed=1),
     )(*args)
 
@@ -293,13 +334,21 @@
     wides = [shape(width, pad) for width in widths]
     parts = [[shape(width // HALVES, pad, dtype=BF16)] * HALVES for width in widths]
 
-    rc = call(
-        coupling,
-        shape(group, part, levels * pad + 2 * tracked, dtype=BF16),
-        reflect.transpose(1, 2, 0, 3),
-        cotangent[0],
-        scratch=[pltpu.VMEM((pad, columns), F32)],
-        limit=10,
+    rc = pl.pallas_call(
+        functools.partial(coupling, levels),
+        grid=(levels + 1,),
+        out_shape=pltpu.HBM((group, part, levels * pad + 2 * tracked), BF16),
+        in_specs=[
+            pl.BlockSpec((1, rows, 1, columns), lambda i: (jnp.minimum(i, levels - 1), 0, 0, 0)),
+            pl.BlockSpec((tracked, columns), lambda i: (0, 0)),
+        ],
+        out_specs=pl.BlockSpec((group, part, pad), lambda i: (0, 0, i)),
+        scratch_shapes=[pltpu.VMEM((pad, columns), F32)],
+        compiler_params=pltpu.CompilerParams(vmem_limit_bytes=10 * 2**20),
+        cost_estimate=pl.CostEstimate(flops=0, transcendentals=0, bytes_accessed=1),
+    )(
+        pltpu.with_memory_space_constraint(reflect.transpose(1, 2, 0, 3), pltpu.HBM),
+        pltpu.with_memory_space_constraint(cotangent[0], pltpu.HBM),
     )
     x = call(turned, blocks, after(me_arr, rc), incident[0], scratch=[pltpu.VMEM((pad, columns), F32)])
     rc = over_cuts(rc)
@@ -337,13 +386,18 @@
             )
             diag = [over_row(half, 1) for half in halves]
             stored[chunk].append((current[chunk], cores[chunk], far, *diag))
-            final = degree == 1 and chunk == CHUNKS - 1
-            value = call(
-                functools.partial(forward_last, degree),
-                pltpu.HBM((columns, pad), BF16) if final else blocks[chunk],
-                step, x[chunk], most, panel, *diag,
-                *(current[:-1] if final else []),
-            )
+            if degree == 1 and chunk == CHUNKS - 1:
+                value, pile = call(
+                    forward_end,
+                    (pltpu.HBM((columns, pad), BF16), pltpu.HBM((4, columns, pad), BF16)),
+                    step, x[chunk], most, panel, me_arr, current[0],
+                    *[piece for each in count for piece in stored[each][-1]],
+                )
+            else:
+                value = call(
+                    functools.partial(forward_last, degree),
+                    blocks[chunk], step, x[chunk], most, panel, *diag,
+                )
             current[chunk] = value
             token = value
             if degree > 1:
@@ -352,11 +406,11 @@
         fars, cores = next_fars, next_cores
         pieces = [piece for chunk in count for piece in stored[chunk][-1]]
         place = after(me_arr, token)
-        token = write_columns(place, pieces)
-        rights.append(token)
-
-    current[-1], rc, token = lax.optimization_barrier((current[-1], rc, token))
-    rights[-1] = token
+        if degree > 1:
+            token = write_columns(place, pieces)
+            rights.append(token)
+
+    current[-1], rc = lax.optimization_barrier((current[-1], rc))
     swapped = over_cuts(current[-1].reshape(group, part, pad))
     field, cmap, coupled, sums = call(
         functools.partial(merge, levels, rows),
@@ -408,13 +462,24 @@
             far = over_row(sent, 2)
             token = sent
             pending[chunk] = (near, core, far)
-    lefts = [*scaled_all[:-1], after(scaled_all[-1], token)]
+            if degree == 1 and chunk == CHUNKS - 1:
+                token = call(columns_from, shape(columns, full, dtype=BF16), after(pile, token))
+                rights.append(token)
+            if degree == TAYLOR - 1 and chunk == CHUNKS - 1:
+                early = call(
+                    outer_early,
+                    shape(pad, full),
+                    *scaled_all[:-1], after(scaled_all[-1], token), *rights[:0:-1],
+                    limit=12,
+                )
+                token = early
+    lefts = [*scaled_all[-CHUNKS:-1], after(scaled_all[-1], token)]
     tiles = -(-rows // LANES)
     top = tiles * 3 // 5
-    grad_matrix = outer_rows(0, top, lefts, rights, None, rows, full)
+    grad_matrix = outer_rows(0, top, lefts, rights[0], early, None, rows, full)
     for late in pending[:-1]:
         grad_matrix = after(grad_matrix, late[2])
-    grad_matrix = outer_rows(top, tiles - top, lefts, rights, grad_matrix, rows, full)
+    grad_matrix = outer_rows(top, tiles - top, lefts, rights[0], early, grad_matrix, rows, full)
     args = []
     for chunk in count:
         near, core, far = pending[chunk]

time: 116 us -> 114 us (0.983)
  waiting for transfers between devices: 14.3 us -> 10.6 us
  Pallas kernels: 32.8 us -> 35.3 us
  local copies, waits for them, and re-layouts: 4.2 us -> 1.86 us
  starting transfers between devices: 30.2 us -> 31.6 us
    ppermute x51, waiting for transfers between devices: 14.3 us -> 10.6 us  [over_row(): return lax.ppermute(value, 'row', pairs)]
    pallas_call x2 -> x3, Pallas kernels: 6.4 us -> 8.82 us  [the longest x2 5.05 us: outer_rows(): pl.pallas_call(functools.partial(outer, len(lefts), first), grid=(tiles,)...]
    unnamed x18 -> x14, local copies, waits for them, and re-layouts: 4.2 us -> 1.86 us
    ppermute x51, starting transfers between devices: 22.9 us -> 24.3 us  [over_row(): return lax.ppermute(value, 'row', pairs)]
  transfers between devices with their start and end apart: 52 -> 52, of which waited for: 21 -> 19; matrix products, arithmetic and copies ran while one was open for 0% -> 0% of each run, Pallas kernels for 23% -> 24%
where the time goes in v4:
time: 114 us
  Pallas kernels  35.3 us (31%)
  blocking collectives  32.5 us (29%)
  starting transfers between devices  31.6 us (28%)
  waiting for transfers between devices  10.6 us (9%)
  local copies, waits for them, and re-layouts  1.86 us (2%)
  between operations  1.82 us (2%)
    all_to_all x2, blocking collectives, over_cuts(): lax.all_to_all(value, 'cuts', 0, 0, axis_index_groups=groups, tiled=True)  32.5 us
    pallas_call x45, Pallas kernels, call(): pl.pallas_call(body, out_shape=out_shape, in_specs=[SCALAR if arg.size <=...  26.5 us
    ppermute x51, starting transfers between devices, over_row(): return lax.ppermute(value, 'row', pairs)  24.3 us
    ppermute x51, waiting for transfers between devices, over_row(): return lax.ppermute(value, 'row', pairs)  10.6 us
    all_to_all x1, starting transfers between devices, over_cuts(): lax.all_to_all(value, 'cuts', 0, 0, axis_index_groups=groups, tiled=True)  7.25 us
    pallas_call x2, Pallas kernels, outer_rows(): pl.pallas_call(functools.partial(outer, len(lefts), first), grid=(tiles,)...  5.05 us
    pallas_call x1, Pallas kernels, local(): pl.pallas_call(functools.partial(coupling, levels), grid=(levels + 1,), o...  3.77 us
  transfers between devices with their start and end apart: 52, of which 19 were waited for; matrix products, arithmetic and copies ran while one was open for 0% of the time, Pallas kernels for 24%

profile of v4, /device:TPU:0, one launch (start us, length us, event | category | flops | bytes accessed | tf_op | source)
XLA Modules:
  0.0 113.7 jit_solution(8861046758953539600)
XLA Ops:
  0.7 3.8 %shard_map.86 = bf16[8,32,2048]{2,1,0:T(8,128)(2,1)} custom-call(f32[3,601,1,256]{3,2,1,0:T(1,128)} %bitcast.15, f32[64,256]{1,0:T(8,128)} %bitcast.18), custom_call_target="tpu_custom_call" | custom-call | bytes 1 | tf_op jit(solution)/shard_map/pallas_call | solution.py:337
  4.4 7.3 %all-to-all-start = ((bf16[8,32,2048]{2,1,0:T(8,128)(2,1)}), bf16[8,32,2048]{2,1,0:T(8,128)(2,1)}, u32[]{:S(2)}, u32[]{:S(2)}) async-start(bf16[8,32,2048]{2,1,0:T(8,128)(2,1)} %shard_map.86), calls=%async_computation | async-start | bytes 2097152 | tf_op jit(solution)/shard_map/all_to_all | solution.py:67
  11.9 1.6 %collective-permute-start.3 = (bf16[128,640]{1,0:T(8,128)(2,1)S(1)}, bf16[128,640]{1,0:T(8,128)(2,1)S(1)}, u32[]{:S(2)}, u32[]{:S(2)}) collective-permute-start(bf16[128,640]{1,0:T(8,128)(2,1)S(1)} %get-tuple-element.102.own_ref.x_ref.refs_0_), channel_id=1, source_target_pairs={{0,2},{1,3},{2,0},{3,1},{4,6},{5,7},{6,4},{7,5},{8,10},{9,11},{10,... | collective-permute-start | bytes 491528 | tf_op jit(solution)/shard_map/ppermute | solution.py:58
  14.6 1.8 %copy-done.2 = bf16[1,601,2404]{2,1,0:T(8,128)(2,1)S(1)} copy-done((bf16[1,601,2404]{2,1,0:T(8,128)(2,1)S(1)}, bf16[1,601,2404]{2,1,0:T(8,128)(2,1)}, u32[]{:S(2)}) %copy-start.2) | copy-done | bytes 2889632
  16.5 1.4 %shard_map.88 = (bf16[4,640,640]{2,1,0:T(8,128)(2,1)S(1)}, f32[8,128]{1,0:T(8,128)S(1)}) custom-call(s32[1]{0:T(128)} %bitcast.me_ref, s32[1]{0:T(128)S(6)} %copy.11.profile_ref, f32[8]{0:T(128)S(1)} %copy-done.5, bf16[601,2404]{1,0:T(8,128)(2,1)S(1)} %bitcast.10), custom_call_target="tpu_custom_call" | custom-call | bytes 1 | tf_op jit(solution)/shard_map/pallas_call | solution.py:30
  19.3 0.8 shard_map.90.most_ref
  20.5 2.0 %collective-permute-start.11 = (bf16[128,640]{1,0:T(8,128)(2,1)S(1)}, bf16[128,640]{1,0:T(8,128)(2,1)S(1)}, u32[]{:S(2)}, u32[]{:S(2)}) collective-permute-start(bf16[128,640]{1,0:T(8,128)(2,1)S(1)} %shard_map.91.own_ref.refs_0_), channel_id=1, source_target_pairs={{0,2},{1,3},{2,0},{3,1},{4,6},{5,7},{6,4},{7,5},{8,10},{9,11},{10,... | collective-permute-start | bytes 491528 | tf_op jit(solution)/shard_map/ppermute | solution.py:58
  24.9 1.5 %shard_map.95.refs_2_ = bf16[256,2404]{1,0:T(8,128)(2,1)} custom-call(s32[1]{0:T(128)} %bitcast.me_ref, bf16[128,640]{1,0:T(8,128)(2,1)S(1)} %get-tuple-element.102.own_ref.x_ref.refs_0_, bf16[128,640]{1,0:T(8,128)(2,1)S(1)} %collective-permute-done.2.core_ref.refs_1_, bf16[128,640]{1,0:T(8,128)(2,1)S(1)} %collective-permute-done.3.value_ref.far_ref.refs_2_, ...), custom_call_target="tpu_custom_call" | custom-call | bytes 1 | tf_op jit(solution)/shard_map/pallas_call | solution.py:30
  26.4 0.9 collective-permute-done.11.value_ref.far_ref.refs_2_
  28.0 0.8 shard_map.97.most_ref
  29.3 2.3 %collective-permute-start.19 = (bf16[128,640]{1,0:T(8,128)(2,1)S(1)}, bf16[128,640]{1,0:T(8,128)(2,1)S(1)}, u32[]{:S(2)}, u32[]{:S(2)}) collective-permute-start(bf16[128,640]{1,0:T(8,128)(2,1)S(1)} %shard_map.98.own_ref.refs_0_), channel_id=1, source_target_pairs={{0,2},{1,3},{2,0},{3,1},{4,6},{5,7},{6,4},{7,5},{8,10},{9,11},{10,... | collective-permute-start | bytes 491528 | tf_op jit(solution)/shard_map/ppermute | solution.py:58
  32.3 0.8 shard_map.100.most_ref
  33.5 1.1 collective-permute-start.17
  34.6 1.5 %shard_map.102.refs_5_ = bf16[256,2404]{1,0:T(8,128)(2,1)} custom-call(s32[1]{0:T(128)} %bitcast.me_ref, bf16[128,640]{1,0:T(8,128)(2,1)S(1)} %shard_map.91.own_ref.refs_0_, bf16[128,640]{1,0:T(8,128)(2,1)S(1)} %collective-permute-done.10.core_ref.refs_1_, bf16[128,640]{1,0:T(8,128)(2,1)S(1)} %collective-permute-done.11.value_ref.far_ref.refs_2_, ...), custom_call_target="tpu_custom_call" | custom-call | bytes 1 | tf_op jit(solution)/shard_map/pallas_call | solution.py:30
  37.0 0.8 shard_map.104.most_ref
  38.2 1.8 %collective-permute-done.17.value_ref.far_ref.refs_7_ = bf16[128,640]{1,0:T(8,128)(2,1)S(1)} collective-permute-done((bf16[128,640]{1,0:T(8,128)(2,1)S(1)}, bf16[128,640]{1,0:T(8,128)(2,1)S(1)}, u32[]{:S(2)}, u32[]{:S(2)}) %collective-permute-start.17) | collective-permute-done | bytes 163872 | tf_op jit(solution)/shard_map/ppermute | solution.py:58
  40.6 0.8 shard_map.107.most_ref
  41.6 1.6 %shard_map.108 = (bf16[256,640]{1,0:T(8,128)(2,1)}, bf16[4,256,640]{2,1,0:T(8,128)(2,1)}) custom-call(f32[8,128]{1,0:T(8,128)S(1)} %get-tuple-element.104.step_ref, bf16[128,640]{1,0:T(8,128)(2,1)S(1)} %get-tuple-element.105.own_ref.x_ref.refs_5_, f32[128,640]{1,0:T(8,128)S(1)} %shard_map.107.most_ref, ...), custom_call_target="tpu_custom_call" | custom-call | bytes 1 | tf_op jit(solution)/shard_map/pallas_call | solution.py:30
  43.2 17.4 %all_to_all.15.w_ref = bf16[8,32,640]{2,1,0:T(8,128)(2,1)S(1)} all-to-all(bf16[8,32,640]{2,1,0:T(8,128)(2,1)} %bitcast.17), channel_id=1, replica_groups=mesh['cuts'=8,'row'=4] {'cuts'}, dimensions={0} | all-to-all | bytes 655360 | tf_op jit(solution)/shard_map/all_to_all | solution.py:67
  60.6 2.0 %shard_map.109 = (f32[8,32,640]{2,1,0:T(8,128)S(1)}, f32[8,32,640]{2,1,0:T(8,128)S(1)}, bf16[8,32,1920]{2,1,0:T(8,128)(2,1)S(1)}, f32[8,256]{1,0:T(8,128)S(1)}) custom-call(s32[1]{0:T(128)} %bitcast.me_ref, s32[1,64]{1,0:T(1,128)S(1)} %bitcast.13, bf16[8,32,640]{2,1,0:T(8,128)(2,1)S(1)} %all_to_all.15.w_ref, bf16[8,32,2048]{2,1,0:T(8,128)(2,1)} %all-to-all-done.rc_ref), custom_call_target="tpu_custom_call" | custom-call | bytes 1 | tf_op jit(solution)/shard_map/pallas_call | solution.py:30
  62.6 1.6 %collective-permute-start.25 = (f32[8,256]{1,0:T(8,128)S(1)}, f32[8,256]{1,0:T(8,128)S(1)}, u32[]{:S(2)}, u32[]{:S(2)}) collective-permute-start(f32[8,256]{1,0:T(8,128)S(1)} %get-tuple-element.139.s0), channel_id=1, source_target_pairs={{0,2},{1,3},{2,0},{3,1},{4,6},{5,7},{6,4},{7,5},{8,10},{9,11},{10,... | collective-permute-start | bytes 24584 | tf_op jit(solution)/shard_map/ppermute | solution.py:58
  64.4 1.2 %collective-permute-done.26.s3 = f32[8,256]{1,0:T(8,128)S(1)} collective-permute-done((f32[8,256]{1,0:T(8,128)S(1)}, f32[8,256]{1,0:T(8,128)S(1)}, u32[]{:S(2)}, u32[]{:S(2)}) %collective-permute-start.26) | collective-permute-done | bytes 8224 | tf_op jit(solution)/shard_map/ppermute | solution.py:58
  66.3 1.2 %shard_map.110 = bf16[8,32,640]{2,1,0:T(8,128)(2,1)} custom-call(f32[8,32,640]{2,1,0:T(8,128)S(1)} %get-tuple-element.136.field_ref, f32[8,32,640]{2,1,0:T(8,128)S(1)} %get-tuple-element.137.cmap_ref, bf16[8,32,1920]{2,1,0:T(8,128)(2,1)S(1)} %get-tuple-element.138.rc_ref, f32[8,256]{1,0:T(8,128)S(1)} %get-tuple-element.139.s0, ...), custom_call_target="tpu_custom_call" | custom-call | bytes 1 | tf_op jit(solution)/shard_map/pallas_call | solution.py:30
  67.6 15.1 %all_to_all.16 = bf16[8,32,640]{2,1,0:T(8,128)(2,1)S(1)} all-to-all(bf16[8,32,640]{2,1,0:T(8,128)(2,1)} %shard_map.110), channel_id=1, replica_groups=mesh['cuts'=8,'row'=4] {'cuts'}, dimensions={0} | all-to-all | bytes 655360 | tf_op jit(solution)/shard_map/all_to_all | solution.py:67
  87.4 1.5 %collective-permute-start.38 = (bf16[128,640]{1,0:T(8,128)(2,1)S(1)}, bf16[128,640]{1,0:T(8,128)(2,1)S(1)}, u32[]{:S(2)}, u32[]{:S(2)}) collective-permute-start(bf16[128,640]{1,0:T(8,128)(2,1)S(1)} %shard_map.116), channel_id=1, source_target_pairs={{0,2},{1,3},{2,0},{3,1},{4,6},{5,7},{6,4},{7,5},{8,10},{9,11},{10,... | collective-permute-start | bytes 491528 | tf_op jit(solution)/shard_map/ppermute | solution.py:58
  89.3 2.3 %collective-permute-done.30.far_ref = bf16[128,640]{1,0:T(8,128)(2,1)S(1)} collective-permute-done((bf16[128,640]{1,0:T(8,128)(2,1)S(1)}, bf16[128,640]{1,0:T(8,128)(2,1)S(1)}, u32[]{:S(2)}, u32[]{:S(2)}) %collective-permute-start.30) | collective-permute-done | bytes 163872 | tf_op jit(solution)/shard_map/ppermute | solution.py:58
  96.5 1.4 %collective-permute-start.42 = (bf16[128,640]{1,0:T(8,128)(2,1)S(1)}, bf16[128,640]{1,0:T(8,128)(2,1)S(1)}, u32[]{:S(2)}, u32[]{:S(2)}) collective-permute-start(bf16[128,640]{1,0:T(8,128)(2,1)S(1)} %shard_map.123), channel_id=1, source_target_pairs={{0,2},{1,3},{2,0},{3,1},{4,6},{5,7},{6,4},{7,5},{8,10},{9,11},{10,... | collective-permute-start | bytes 491528 | tf_op jit(solution)/shard_map/ppermute | solution.py:58
  97.9 2.7 %shard_map.124.refs_3_ = f32[640,2404]{1,0:T(8,128)S(1)} custom-call(bf16[128,640]{1,0:T(8,128)(2,1)S(1)} %get-tuple-element.142.scaled_ref.refs_0_, bf16[128,640]{1,0:T(8,128)(2,1)S(1)} %get-tuple-element.152.scaled_ref.refs_1_, bf16[128,640]{1,0:T(8,128)(2,1)S(1)} %get-tuple-element.160.scaled_ref.refs_2_, ...), custom_call_target="tpu_custom_call" | custom-call | bytes 1 | tf_op jit(solution)/shard_map/pallas_call | solution.py:30
  105.7 1.2 %collective-permute-start.50 = (bf16[128,640]{1,0:T(8,128)(2,1)S(1)}, bf16[128,640]{1,0:T(8,128)(2,1)S(1)}, u32[]{:S(2)}, u32[]{:S(2)}) collective-permute-start(bf16[128,640]{1,0:T(8,128)(2,1)S(1)} %shard_map.130), channel_id=1, source_target_pairs={{0,2},{1,3},{2,0},{3,1},{4,6},{5,7},{6,4},{7,5},{8,10},{9,11},{10,... | collective-permute-start | bytes 491528 | tf_op jit(solution)/shard_map/ppermute | solution.py:58
  106.9 3.1 %shard_map.131.refs_4_ = f32[601,1,2404]{2,1,0:T(1,128)} custom-call(bf16[128,640]{1,0:T(8,128)(2,1)S(1)} %get-tuple-element.181.scaled_ref.refs_0_, bf16[128,640]{1,0:T(8,128)(2,1)S(1)} %get-tuple-element.191.scaled_ref.refs_1_, bf16[256,2404]{1,0:T(8,128)(2,1)S(1)} %copy-done, f32[640,2404]{1,0:T(8,128)S(1)} %shard_map.124.refs_3_), custom_call_target="tpu_custom_call" | custom-call | bytes 1 | tf_op jit(solution)/shard_map/pallas_call | solution.py:298
  110.0 2.0 %shard_map.132 = f32[601,1,2404]{2,1,0:T(1,128)} custom-call(bf16[128,640]{1,0:T(8,128)(2,1)S(1)} %get-tuple-element.181.scaled_ref.refs_0_, bf16[128,640]{1,0:T(8,128)(2,1)S(1)} %get-tuple-element.191.scaled_ref.refs_1_, bf16[256,2404]{1,0:T(8,128)(2,1)S(1)} %copy-done, f32[640,2404]{1,0:T(8,128)S(1)} %shard_map.124.refs_3_, ...), custom_call_target="tpu_custom_call", output_to_operand_aliasing={{}: (4, {})} | custom-call | flops 5000000000 | bytes 1 | tf_op jit(solution)/shard_map/pallas_call | solution.py:298
  112.6 1.1 %shard_map.133 = f32[601,1,256]{2,1,0:T(1,128)} custom-call(f32[128,640]{1,0:T(8,128)S(1)} %get-tuple-element.193.refs_0_, f32[128,640]{1,0:T(8,128)S(1)} %get-tuple-element.194.refs_1_, bf16[128,640]{1,0:T(8,128)(2,1)S(1)} %collective-permute-done.48.refs_2_, bf16[128,640]{1,0:T(8,128)(2,1)S(1)} %collective-permute-done.47.refs_3_, ...), custom_call_target="tpu_custom_call" | custom-call | bytes 1 | tf_op jit(solution)/shard_map/pallas_call | solution.py:30
  (136 shorter events, 25.3 us)
Async XLA Ops:
  4.4 38.7 %all-to-all-start = ((bf16[8,32,2048]{2,1,0:T(8,128)(2,1)}), bf16[8,32,2048]{2,1,0:T(8,128)(2,1)}, u32[]{:S(2)}, u32[]{:S(2)}) async-start(bf16[8,32,2048]{2,1,0:T(8,128)(2,1)} %shard_map.86), calls=%async_computation | async-start | bytes 2097152 | tf_op jit(solution)/shard_map/all_to_all | solution.py:67
  11.9 6.8 %collective-permute-start.3 = (bf16[128,640]{1,0:T(8,128)(2,1)S(1)}, bf16[128,640]{1,0:T(8,128)(2,1)S(1)}, u32[]{:S(2)}, u32[]{:S(2)}) collective-permute-start(bf16[128,640]{1,0:T(8,128)(2,1)S(1)} %get-tuple-element.102.own_ref.x_ref.refs_0_), channel_id=1, source_target_pairs={{0,2},{1,3},{2,0},{3,1},{4,6},{5,7},{6,4},{7,5},{8,10},{9,11},{10,... | collective-permute-start | bytes 491528 | tf_op jit(solution)/shard_map/ppermute | solution.py:58
  13.4 5.8 %collective-permute-start.2 = (bf16[128,640]{1,0:T(8,128)(2,1)S(1)}, bf16[128,640]{1,0:T(8,128)(2,1)S(1)}, u32[]{:S(2)}, u32[]{:S(2)}) collective-permute-start(bf16[128,640]{1,0:T(8,128)(2,1)S(1)} %get-tuple-element.102.own_ref.x_ref.refs_0_), channel_id=1, source_target_pairs={{0,1},{1,0},{2,3},{3,2},{4,5},{5,4},{6,7},{7,6},{8,9},{9,8},{10,11... | collective-permute-start | bytes 491528 | tf_op jit(solution)/shard_map/ppermute | solution.py:58
  13.4 9.1 %collective-permute-start.1 = (bf16[128,640]{1,0:T(8,128)(2,1)S(1)}, bf16[128,640]{1,0:T(8,128)(2,1)S(1)}, u32[]{:S(2)}, u32[]{:S(2)}) collective-permute-start(bf16[128,640]{1,0:T(8,128)(2,1)S(1)} %get-tuple-element.105.own_ref.x_ref.refs_5_), channel_id=1, source_target_pairs={{0,2},{1,3},{2,0},{3,1},{4,6},{5,7},{6,4},{7,5},{8,10},{9,11},{10,... | collective-permute-start | bytes 491528 | tf_op jit(solution)/shard_map/ppermute | solution.py:58
  19.2 4.1 %collective-permute-start = (bf16[128,640]{1,0:T(8,128)(2,1)S(1)}, bf16[128,640]{1,0:T(8,128)(2,1)S(1)}, u32[]{:S(2)}, u32[]{:S(2)}) collective-permute-start(bf16[128,640]{1,0:T(8,128)(2,1)S(1)} %get-tuple-element.105.own_ref.x_ref.refs_5_), channel_id=1, source_target_pairs={{0,1},{1,0},{2,3},{3,2},{4,5},{5,4},{6,7},{7,6},{8,9},{9,8},{10,11... | collective-permute-start | bytes 491528 | tf_op jit(solution)/shard_map/ppermute | solution.py:58
  20.5 6.8 %collective-permute-start.11 = (bf16[128,640]{1,0:T(8,128)(2,1)S(1)}, bf16[128,640]{1,0:T(8,128)(2,1)S(1)}, u32[]{:S(2)}, u32[]{:S(2)}) collective-permute-start(bf16[128,640]{1,0:T(8,128)(2,1)S(1)} %shard_map.91.own_ref.refs_0_), channel_id=1, source_target_pairs={{0,2},{1,3},{2,0},{3,1},{4,6},{5,7},{6,4},{7,5},{8,10},{9,11},{10,... | collective-permute-start | bytes 491528 | tf_op jit(solution)/shard_map/ppermute | solution.py:58
  22.6 1.6 %collective-permute-start.7 = (bf16[64,640]{1,0:T(8,128)(2,1)S(1)}, bf16[64,640]{1,0:T(8,128)(2,1)S(1)}, u32[]{:S(2)}, u32[]{:S(2)}) collective-permute-start(bf16[64,640]{1,0:T(8,128)(2,1)S(1)} %get-tuple-element.114), channel_id=1, source_target_pairs={{0,1},{1,0},{2,3},{3,2},{4,5},{5,4},{6,7},{7,6},{8,9},{9,8},{10,11... | collective-permute-start | bytes 245768 | tf_op jit(solution)/shard_map/ppermute | solution.py:58
  23.1 4.9 %collective-permute-start.10 = (bf16[128,640]{1,0:T(8,128)(2,1)S(1)}, bf16[128,640]{1,0:T(8,128)(2,1)S(1)}, u32[]{:S(2)}, u32[]{:S(2)}) collective-permute-start(bf16[128,640]{1,0:T(8,128)(2,1)S(1)} %shard_map.91.own_ref.refs_0_), channel_id=1, source_target_pairs={{0,1},{1,0},{2,3},{3,2},{4,5},{5,4},{6,7},{7,6},{8,9},{9,8},{10,11... | collective-permute-start | bytes 491528 | tf_op jit(solution)/shard_map/ppermute | solution.py:58
  24.5 7.0 %collective-permute-start.9 = (bf16[128,640]{1,0:T(8,128)(2,1)S(1)}, bf16[128,640]{1,0:T(8,128)(2,1)S(1)}, u32[]{:S(2)}, u32[]{:S(2)}) collective-permute-start(bf16[128,640]{1,0:T(8,128)(2,1)S(1)} %shard_map.94.own_ref.refs_5_), channel_id=1, source_target_pairs={{0,2},{1,3},{2,0},{3,1},{4,6},{5,7},{6,4},{7,5},{8,10},{9,11},{10,... | collective-permute-start | bytes 491528 | tf_op jit(solution)/shard_map/ppermute | solution.py:58
  27.9 4.4 %collective-permute-start.8 = (bf16[128,640]{1,0:T(8,128)(2,1)S(1)}, bf16[128,640]{1,0:T(8,128)(2,1)S(1)}, u32[]{:S(2)}, u32[]{:S(2)}) collective-permute-start(bf16[128,640]{1,0:T(8,128)(2,1)S(1)} %shard_map.94.own_ref.refs_5_), channel_id=1, source_target_pairs={{0,1},{1,0},{2,3},{3,2},{4,5},{5,4},{6,7},{7,6},{8,9},{9,8},{10,11... | collective-permute-start | bytes 491528 | tf_op jit(solution)/shard_map/ppermute | solution.py:58
  29.3 7.1 %collective-permute-start.19 = (bf16[128,640]{1,0:T(8,128)(2,1)S(1)}, bf16[128,640]{1,0:T(8,128)(2,1)S(1)}, u32[]{:S(2)}, u32[]{:S(2)}) collective-permute-start(bf16[128,640]{1,0:T(8,128)(2,1)S(1)} %shard_map.98.own_ref.refs_0_), channel_id=1, source_target_pairs={{0,2},{1,3},{2,0},{3,1},{4,6},{5,7},{6,4},{7,5},{8,10},{9,11},{10,... | collective-permute-start | bytes 491528 | tf_op jit(solution)/shard_map/ppermute | solution.py:58
  32.1 4.9 %collective-permute-start.18 = (bf16[128,640]{1,0:T(8,128)(2,1)S(1)}, bf16[128,640]{1,0:T(8,128)(2,1)S(1)}, u32[]{:S(2)}, u32[]{:S(2)}) collective-permute-start(bf16[128,640]{1,0:T(8,128)(2,1)S(1)} %shard_map.98.own_ref.refs_0_), channel_id=1, source_target_pairs={{0,1},{1,0},{2,3},{3,2},{4,5},{5,4},{6,7},{7,6},{8,9},{9,8},{10,11... | collective-permute-start | bytes 491528 | tf_op jit(solution)/shard_map/ppermute | solution.py:58
  33.5 6.5 %collective-permute-start.17 = (bf16[128,640]{1,0:T(8,128)(2,1)S(1)}, bf16[128,640]{1,0:T(8,128)(2,1)S(1)}, u32[]{:S(2)}, u32[]{:S(2)}) collective-permute-start(bf16[128,640]{1,0:T(8,128)(2,1)S(1)} %shard_map.101.own_ref.refs_5_), channel_id=1, source_target_pairs={{0,2},{1,3},{2,0},{3,1},{4,6},{5,7},{6,4},{7,5},{8,10},{9,11},{10,... | collective-permute-start | bytes 491528 | tf_op jit(solution)/shard_map/ppermute | solution.py:58
  36.9 3.7 %collective-permute-start.16 = (bf16[128,640]{1,0:T(8,128)(2,1)S(1)}, bf16[128,640]{1,0:T(8,128)(2,1)S(1)}, u32[]{:S(2)}, u32[]{:S(2)}) collective-permute-start(bf16[128,640]{1,0:T(8,128)(2,1)S(1)} %shard_map.101.own_ref.refs_5_), channel_id=1, source_target_pairs={{0,1},{1,0},{2,3},{3,2},{4,5},{5,4},{6,7},{7,6},{8,9},{9,8},{10,11... | collective-permute-start | bytes 491528 | tf_op jit(solution)/shard_map/ppermute | solution.py:58
  62.5 3.1 %collective-permute-start.26 = (f32[8,256]{1,0:T(8,128)S(1)}, f32[8,256]{1,0:T(8,128)S(1)}, u32[]{:S(2)}, u32[]{:S(2)}) collective-permute-start(f32[8,256]{1,0:T(8,128)S(1)} %get-tuple-element.139.s0), channel_id=1, source_target_pairs={{0,3},{1,2},{2,1},{3,0},{4,7},{5,6},{6,5},{7,4},{8,11},{9,10},{10,... | collective-permute-start | bytes 24584 | tf_op jit(solution)/shard_map/ppermute | solution.py:58
  62.6 3.7 %collective-permute-start.25 = (f32[8,256]{1,0:T(8,128)S(1)}, f32[8,256]{1,0:T(8,128)S(1)}, u32[]{:S(2)}, u32[]{:S(2)}) collective-permute-start(f32[8,256]{1,0:T(8,128)S(1)} %get-tuple-element.139.s0), channel_id=1, source_target_pairs={{0,2},{1,3},{2,0},{3,1},{4,6},{5,7},{6,4},{7,5},{8,10},{9,11},{10,... | collective-permute-start | bytes 24584 | tf_op jit(solution)/shard_map/ppermute | solution.py:58
  64.2 2.1 %collective-permute-start.24 = (f32[8,256]{1,0:T(8,128)S(1)}, f32[8,256]{1,0:T(8,128)S(1)}, u32[]{:S(2)}, u32[]{:S(2)}) collective-permute-start(f32[8,256]{1,0:T(8,128)S(1)} %get-tuple-element.139.s0), channel_id=1, source_target_pairs={{0,1},{1,0},{2,3},{3,2},{4,5},{5,4},{6,7},{7,6},{8,9},{9,8},{10,11... | collective-permute-start | bytes 24584 | tf_op jit(solution)/shard_map/ppermute | solution.py:58
  84.5 7.1 %collective-permute-start.30 = (bf16[128,640]{1,0:T(8,128)(2,1)S(1)}, bf16[128,640]{1,0:T(8,128)(2,1)S(1)}, u32[]{:S(2)}, u32[]{:S(2)}) collective-permute-start(bf16[128,640]{1,0:T(8,128)(2,1)S(1)} %shard_map.113), channel_id=1, source_target_pairs={{0,2},{1,3},{2,0},{3,1},{4,6},{5,7},{6,4},{7,5},{8,10},{9,11},{10,... | collective-permute-start | bytes 491528 | tf_op jit(solution)/shard_map/ppermute | solution.py:58
  85.2 6.4 %collective-permute-start.27 = (bf16[128,640]{1,0:T(8,128)(2,1)S(1)}, bf16[128,640]{1,0:T(8,128)(2,1)S(1)}, u32[]{:S(2)}, u32[]{:S(2)}) collective-permute-start(bf16[128,640]{1,0:T(8,128)(2,1)S(1)} %get-tuple-element.144), channel_id=1, source_target_pairs={{0,1},{1,0},{2,3},{3,2},{4,5},{5,4},{6,7},{7,6},{8,9},{9,8},{10,11... | collective-permute-start | bytes 491528 | tf_op jit(solution)/shard_map/ppermute | solution.py:58
  85.6 1.7 %collective-permute-start.32 = (bf16[64,640]{1,0:T(8,128)(2,1)S(1)}, bf16[64,640]{1,0:T(8,128)(2,1)S(1)}, u32[]{:S(2)}, u32[]{:S(2)}) collective-permute-start(bf16[64,640]{1,0:T(8,128)(2,1)S(1)} %get-tuple-element.154), channel_id=1, source_target_pairs={{0,1},{1,0},{2,3},{3,2},{4,5},{5,4},{6,7},{7,6},{8,9},{9,8},{10,11... | collective-permute-start | bytes 245768 | tf_op jit(solution)/shard_map/ppermute | solution.py:58
  86.8 7.8 %collective-permute-start.37 = (bf16[128,640]{1,0:T(8,128)(2,1)S(1)}, bf16[128,640]{1,0:T(8,128)(2,1)S(1)}, u32[]{:S(2)}, u32[]{:S(2)}) collective-permute-start(bf16[128,640]{1,0:T(8,128)(2,1)S(1)} %get-tuple-element.166), channel_id=1, source_target_pairs={{0,1},{1,0},{2,3},{3,2},{4,5},{5,4},{6,7},{7,6},{8,9},{9,8},{10,11... | collective-permute-start | bytes 491528 | tf_op jit(solution)/shard_map/ppermute | solution.py:58
  87.4 7.2 %collective-permute-start.38 = (bf16[128,640]{1,0:T(8,128)(2,1)S(1)}, bf16[128,640]{1,0:T(8,128)(2,1)S(1)}, u32[]{:S(2)}, u32[]{:S(2)}) collective-permute-start(bf16[128,640]{1,0:T(8,128)(2,1)S(1)} %shard_map.116), channel_id=1, source_target_pairs={{0,2},{1,3},{2,0},{3,1},{4,6},{5,7},{6,4},{7,5},{8,10},{9,11},{10,... | collective-permute-start | bytes 491528 | tf_op jit(solution)/shard_map/ppermute | solution.py:58
  93.5 7.1 %collective-permute-start.36 = (bf16[128,640]{1,0:T(8,128)(2,1)S(1)}, bf16[128,640]{1,0:T(8,128)(2,1)S(1)}, u32[]{:S(2)}, u32[]{:S(2)}) collective-permute-start(bf16[128,640]{1,0:T(8,128)(2,1)S(1)} %shard_map.120), channel_id=1, source_target_pairs={{0,2},{1,3},{2,0},{3,1},{4,6},{5,7},{6,4},{7,5},{8,10},{9,11},{10,... | collective-permute-start | bytes 491528 | tf_op jit(solution)/shard_map/ppermute | solution.py:58
  93.6 7.1 %collective-permute-start.33 = (bf16[128,640]{1,0:T(8,128)(2,1)S(1)}, bf16[128,640]{1,0:T(8,128)(2,1)S(1)}, u32[]{:S(2)}, u32[]{:S(2)}) collective-permute-start(bf16[128,640]{1,0:T(8,128)(2,1)S(1)} %get-tuple-element.162), channel_id=1, source_target_pairs={{0,1},{1,0},{2,3},{3,2},{4,5},{5,4},{6,7},{7,6},{8,9},{9,8},{10,11... | collective-permute-start | bytes 491528 | tf_op jit(solution)/shard_map/ppermute | solution.py:58
  96.1 7.4 %collective-permute-start.41 = (bf16[128,640]{1,0:T(8,128)(2,1)S(1)}, bf16[128,640]{1,0:T(8,128)(2,1)S(1)}, u32[]{:S(2)}, u32[]{:S(2)}) collective-permute-start(bf16[128,640]{1,0:T(8,128)(2,1)S(1)} %get-tuple-element.179), channel_id=1, source_target_pairs={{0,1},{1,0},{2,3},{3,2},{4,5},{5,4},{6,7},{7,6},{8,9},{9,8},{10,11... | collective-permute-start | bytes 491528 | tf_op jit(solution)/shard_map/ppermute | solution.py:58
  96.5 7.1 %collective-permute-start.42 = (bf16[128,640]{1,0:T(8,128)(2,1)S(1)}, bf16[128,640]{1,0:T(8,128)(2,1)S(1)}, u32[]{:S(2)}, u32[]{:S(2)}) collective-permute-start(bf16[128,640]{1,0:T(8,128)(2,1)S(1)} %shard_map.123), channel_id=1, source_target_pairs={{0,2},{1,3},{2,0},{3,1},{4,6},{5,7},{6,4},{7,5},{8,10},{9,11},{10,... | collective-permute-start | bytes 491528 | tf_op jit(solution)/shard_map/ppermute | solution.py:58
  102.5 7.4 %collective-permute-start.47 = (bf16[128,640]{1,0:T(8,128)(2,1)S(1)}, bf16[128,640]{1,0:T(8,128)(2,1)S(1)}, u32[]{:S(2)}, u32[]{:S(2)}) collective-permute-start(bf16[128,640]{1,0:T(8,128)(2,1)S(1)} %shard_map.127), channel_id=1, source_target_pairs={{0,2},{1,3},{2,0},{3,1},{4,6},{5,7},{6,4},{7,5},{8,10},{9,11},{10,... | collective-permute-start | bytes 491528 | tf_op jit(solution)/shard_map/ppermute | solution.py:58
  103.9 1.8 %collective-permute-start.46 = (bf16[64,640]{1,0:T(8,128)(2,1)S(1)}, bf16[64,640]{1,0:T(8,128)(2,1)S(1)}, u32[]{:S(2)}, u32[]{:S(2)}) collective-permute-start(bf16[64,640]{1,0:T(8,128)(2,1)S(1)} %get-tuple-element.190), channel_id=1, source_target_pairs={{0,1},{1,0},{2,3},{3,2},{4,5},{5,4},{6,7},{7,6},{8,9},{9,8},{10,11... | collective-permute-start | bytes 245768 | tf_op jit(solution)/shard_map/ppermute | solution.py:58
  104.0 1.7 %collective-permute-start.45 = (bf16[64,640]{1,0:T(8,128)(2,1)S(1)}, bf16[64,640]{1,0:T(8,128)(2,1)S(1)}, u32[]{:S(2)}, u32[]{:S(2)}) collective-permute-start(bf16[64,640]{1,0:T(8,128)(2,1)S(1)} %get-tuple-element.187), channel_id=1, source_target_pairs={{0,1},{1,0},{2,3},{3,2},{4,5},{5,4},{6,7},{7,6},{8,9},{9,8},{10,11... | collective-permute-start | bytes 245768 | tf_op jit(solution)/shard_map/ppermute | solution.py:58
  104.5 8.1 %collective-permute-start.48 = (bf16[128,640]{1,0:T(8,128)(2,1)S(1)}, bf16[128,640]{1,0:T(8,128)(2,1)S(1)}, u32[]{:S(2)}, u32[]{:S(2)}) collective-permute-start(bf16[128,640]{1,0:T(8,128)(2,1)S(1)} %get-tuple-element.195), channel_id=1, source_target_pairs={{0,1},{1,0},{2,3},{3,2},{4,5},{5,4},{6,7},{7,6},{8,9},{9,8},{10,11... | collective-permute-start | bytes 491528 | tf_op jit(solution)/shard_map/ppermute | solution.py:58
  105.2 7.4 %collective-permute-start.49 = (bf16[128,640]{1,0:T(8,128)(2,1)S(1)}, bf16[128,640]{1,0:T(8,128)(2,1)S(1)}, u32[]{:S(2)}, u32[]{:S(2)}) collective-permute-start(bf16[128,640]{1,0:T(8,128)(2,1)S(1)} %get-tuple-element.198), channel_id=1, source_target_pairs={{0,1},{1,0},{2,3},{3,2},{4,5},{5,4},{6,7},{7,6},{8,9},{9,8},{10,11... | collective-permute-start | bytes 491528 | tf_op jit(solution)/shard_map/ppermute | solution.py:58
  105.7 6.8 %collective-permute-start.50 = (bf16[128,640]{1,0:T(8,128)(2,1)S(1)}, bf16[128,640]{1,0:T(8,128)(2,1)S(1)}, u32[]{:S(2)}, u32[]{:S(2)}) collective-permute-start(bf16[128,640]{1,0:T(8,128)(2,1)S(1)} %shard_map.130), channel_id=1, source_target_pairs={{0,2},{1,3},{2,0},{3,1},{4,6},{5,7},{6,4},{7,5},{8,10},{9,11},{10,... | collective-permute-start | bytes 491528 | tf_op jit(solution)/shard_map/ppermute | solution.py:58
  (27 other events, 83.9 us)

commit v5 on v4

--- a/solution.py
+++ b/solution.py
@@ -20,6 +20,7 @@
 BF16 = jnp.bfloat16
 WHOLE = pl.BlockSpec(memory_space=pltpu.VMEM)
 SCALAR = pl.BlockSpec(memory_space=pltpu.SMEM)
+ANY = pl.BlockSpec(memory_space=pl.ANY)
 
 
 def shape(*dims, dtype=F32):
@@ -162,10 +163,20 @@
         out_ref[:, block * rows : (block + 1) * rows] = pile_ref[block, :, :rows]
 
 
-def merge(levels, rows, me_ref, order_ref, w_ref, rc_ref, field_ref, cmap_ref, level_ref, sums_ref):
+def merge(levels, rows, me_ref, order_ref, w_ref, rc_ref, field_ref, cmap_ref, level_ref, sums_ref, tail_ref, sems):
     group, part, pad = w_ref.shape
     tracked = order_ref.shape[1]
     tail = level_ref.shape[2]
+    copies = [
+        pltpu.make_async_copy(rc_ref.at[:, :, pl.ds(tail, 2 * tracked)], tail_ref, sems.at[levels])
+    ]
+    for level in range(levels):
+        lanes = pl.ds(level * pad, pad)
+        copies.append(
+            pltpu.make_async_copy(rc_ref.at[:, :, lanes], level_ref.at[:, :, lanes], sems.at[level])
+        )
+    for copy in copies:
+        copy.start()
     place = lax.broadcasted_iota(jnp.int32, (pad, tracked), 0)
     order = place + lax.rem(me_ref[0] * rows, ORDERS)
     for _ in range(-(-rows // ORDERS)):
@@ -173,24 +184,23 @@
     order = jnp.where(place < rows, order, -1)
     onehot = jnp.where(order == order_ref[...], 1.0, 0.0).astype(BF16)
     onehot = jnp.concatenate([onehot, onehot], axis=1)
+    copies[0].wait()
+    cmap_ref[...] = times_t(tail_ref[...].reshape(group * part, 2 * tracked), onehot).reshape(group, part, pad)
     totals = []
     merged = [w_ref[s].astype(F32) for s in range(group)]
-    level_ref[...] = rc_ref[:, :, :tail]
     for level in range(levels):
+        copies[level + 1].wait()
         sent = [
-            rc_ref[s, :, level * pad : (level + 1) * pad].astype(F32) * merged[s] for s in range(group)
+            level_ref[s, :, level * pad : (level + 1) * pad].astype(F32) * merged[s] for s in range(group)
         ]
         merged = [merged[s] + sent[s ^ 2**level] for s in range(group)]
     lane = lax.broadcasted_iota(jnp.int32, (part, LANES), 1)
-    cmaps = times_t(rc_ref[:, :, tail:].reshape(group * part, 2 * tracked), onehot).reshape(group, part, pad)
     for s in range(group):
         field = merged[s]
-        cmap = cmaps[s]
         squared = field * field
         power = jnp.sum(squared, axis=1, keepdims=True)
-        weighted = jnp.sum(cmap * squared, axis=1, keepdims=True)
+        weighted = jnp.sum(cmap_ref[s] * squared, axis=1, keepdims=True)
         field_ref[s] = field
-        cmap_ref[s] = cmap
         totals.append(jnp.where(lane == 0, power, jnp.where(lane == 1, weighted, 0.0)))
     sums_ref[...] = jnp.concatenate(totals, axis=0).T[: sums_ref.shape[0]]
 
@@ -412,16 +422,27 @@
 
     current[-1], rc = lax.optimization_barrier((current[-1], rc))
     swapped = over_cuts(current[-1].reshape(group, part, pad))
-    field, cmap, coupled, sums = call(
+    field, cmap, coupled, sums = pl.pallas_call(
         functools.partial(merge, levels, rows),
-        (
+        out_shape=(
             shape(group, part, pad),
             shape(group, part, pad),
             shape(group, part, levels * pad, dtype=BF16),
             shape(8, group * part),
         ),
-        me_arr, order_index.reshape(1, tracked), swapped, rc,
-        limit=12,
+        in_specs=[SCALAR, WHOLE, WHOLE, ANY],
+        out_specs=(WHOLE,) * 4,
+        scratch_shapes=[
+            pltpu.VMEM((group, part, 2 * tracked), BF16),
+            pltpu.SemaphoreType.DMA((levels + 1,)),
+        ],
+        compiler_params=pltpu.CompilerParams(vmem_limit_bytes=12 * 2**20),
+        cost_estimate=pl.CostEstimate(flops=0, transcendentals=0, bytes_accessed=1),
+    )(
+        me_arr,
+        order_index.reshape(1, tracked),
+        swapped,
+        pltpu.with_memory_space_constraint(rc, pltpu.HBM),
     )
     s1, s2, s3 = (over_row(sums, mask) for mask in (1, 2, 3))
     grad = call(

time: 114 us -> 114 us (level)
    pallas_call x45 -> x44, Pallas kernels: 26.5 us -> 24.5 us  [call(): pl.pallas_call(body, out_shape=out_shape, in_specs=[SCALAR if arg.size <=...]
    pallas_call x0 -> x1, Pallas kernels: none -> 1.65 us  [local(): pl.pallas_call(functools.partial(merge, levels, rows), out_shape=(shape(g...]
where the time goes in v5:
time: 114 us; the launch traced here: 113 us
  Pallas kernels  35 us (31%)
  blocking collectives  32.5 us (29%)
  starting transfers between devices  31.6 us (28%)
  waiting for transfers between devices  10.6 us (9%)
  local copies, waits for them, and re-layouts  1.86 us (2%)
  between operations  1.83 us (2%)
    all_to_all x2, blocking collectives, over_cuts(): lax.all_to_all(value, 'cuts', 0, 0, axis_index_groups=groups, tiled=True)  32.5 us
    pallas_call x44, Pallas kernels, call(): pl.pallas_call(body, out_shape=out_shape, in_specs=[SCALAR if arg.size <=...  24.5 us
    ppermute x51, starting transfers between devices, over_row(): return lax.ppermute(value, 'row', pairs)  24.4 us
    ppermute x51, waiting for transfers between devices, over_row(): return lax.ppermute(value, 'row', pairs)  10.6 us
    all_to_all x1, starting transfers between devices, over_cuts(): lax.all_to_all(value, 'cuts', 0, 0, axis_index_groups=groups, tiled=True)  7.25 us
    pallas_call x2, Pallas kernels, outer_rows(): pl.pallas_call(functools.partial(outer, len(lefts), first), grid=(tiles,)...  5.05 us
    pallas_call x1, Pallas kernels, local(): pl.pallas_call(functools.partial(coupling, levels), grid=(levels + 1,), o...  3.77 us
  transfers between devices with their start and end apart: 52, of which 19 were waited for; matrix products, arithmetic and copies ran while one was open for 0% of the time, Pallas kernels for 24%

profile of v5, /device:TPU:0, one launch (start us, length us, event | category | flops | bytes accessed | tf_op | source)
XLA Modules:
  0.0 113.5 jit_solution(5475807810698943731)
XLA Ops:
  0.7 3.8 %shard_map.86 = bf16[8,32,2048]{2,1,0:T(8,128)(2,1)} custom-call(f32[3,601,1,256]{3,2,1,0:T(1,128)} %bitcast.15, f32[64,256]{1,0:T(8,128)} %bitcast.18), custom_call_target="tpu_custom_call" | custom-call | bytes 1 | tf_op jit(solution)/shard_map/pallas_call | solution.py:347
  4.4 7.3 %all-to-all-start = ((bf16[8,32,2048]{2,1,0:T(8,128)(2,1)}), bf16[8,32,2048]{2,1,0:T(8,128)(2,1)}, u32[]{:S(2)}, u32[]{:S(2)}) async-start(bf16[8,32,2048]{2,1,0:T(8,128)(2,1)} %shard_map.86), calls=%async_computation | async-start | bytes 2097152 | tf_op jit(solution)/shard_map/all_to_all | solution.py:68
  11.9 1.6 %collective-permute-start.3 = (bf16[128,640]{1,0:T(8,128)(2,1)S(1)}, bf16[128,640]{1,0:T(8,128)(2,1)S(1)}, u32[]{:S(2)}, u32[]{:S(2)}) collective-permute-start(bf16[128,640]{1,0:T(8,128)(2,1)S(1)} %get-tuple-element.102.own_ref.x_ref.refs_0_), channel_id=1, source_target_pairs={{0,2},{1,3},{2,0},{3,1},{4,6},{5,7},{6,4},{7,5},{8,10},{9,11},{10,... | collective-permute-start | bytes 491528 | tf_op jit(solution)/shard_map/ppermute | solution.py:59
  14.6 1.8 %copy-done.2 = bf16[1,601,2404]{2,1,0:T(8,128)(2,1)S(1)} copy-done((bf16[1,601,2404]{2,1,0:T(8,128)(2,1)S(1)}, bf16[1,601,2404]{2,1,0:T(8,128)(2,1)}, u32[]{:S(2)}) %copy-start.2) | copy-done | bytes 2889632
  16.5 1.4 %shard_map.88 = (bf16[4,640,640]{2,1,0:T(8,128)(2,1)S(1)}, f32[8,128]{1,0:T(8,128)S(1)}) custom-call(s32[1]{0:T(128)} %bitcast.me_ref, s32[1]{0:T(128)S(6)} %copy.11.profile_ref, f32[8]{0:T(128)S(1)} %copy-done.5, bf16[601,2404]{1,0:T(8,128)(2,1)S(1)} %bitcast.10), custom_call_target="tpu_custom_call" | custom-call | bytes 1 | tf_op jit(solution)/shard_map/pallas_call | solution.py:31
  19.3 0.8 shard_map.90.most_ref
  20.5 2.0 %collective-permute-start.11 = (bf16[128,640]{1,0:T(8,128)(2,1)S(1)}, bf16[128,640]{1,0:T(8,128)(2,1)S(1)}, u32[]{:S(2)}, u32[]{:S(2)}) collective-permute-start(bf16[128,640]{1,0:T(8,128)(2,1)S(1)} %shard_map.91.own_ref.refs_0_), channel_id=1, source_target_pairs={{0,2},{1,3},{2,0},{3,1},{4,6},{5,7},{6,4},{7,5},{8,10},{9,11},{10,... | collective-permute-start | bytes 491528 | tf_op jit(solution)/shard_map/ppermute | solution.py:59
  24.9 1.5 %shard_map.95.refs_2_ = bf16[256,2404]{1,0:T(8,128)(2,1)} custom-call(s32[1]{0:T(128)} %bitcast.me_ref, bf16[128,640]{1,0:T(8,128)(2,1)S(1)} %get-tuple-element.102.own_ref.x_ref.refs_0_, bf16[128,640]{1,0:T(8,128)(2,1)S(1)} %collective-permute-done.2.core_ref.refs_1_, bf16[128,640]{1,0:T(8,128)(2,1)S(1)} %collective-permute-done.3.value_ref.far_ref.refs_2_, ...), custom_call_target="tpu_custom_call" | custom-call | bytes 1 | tf_op jit(solution)/shard_map/pallas_call | solution.py:31
  26.4 0.9 collective-permute-done.11.value_ref.far_ref.refs_2_
  28.0 0.8 shard_map.97.most_ref
  29.3 2.3 %collective-permute-start.19 = (bf16[128,640]{1,0:T(8,128)(2,1)S(1)}, bf16[128,640]{1,0:T(8,128)(2,1)S(1)}, u32[]{:S(2)}, u32[]{:S(2)}) collective-permute-start(bf16[128,640]{1,0:T(8,128)(2,1)S(1)} %shard_map.98.own_ref.refs_0_), channel_id=1, source_target_pairs={{0,2},{1,3},{2,0},{3,1},{4,6},{5,7},{6,4},{7,5},{8,10},{9,11},{10,... | collective-permute-start | bytes 491528 | tf_op jit(solution)/shard_map/ppermute | solution.py:59
  32.3 0.8 shard_map.100.most_ref
  33.5 1.1 collective-permute-start.17
  34.6 1.5 %shard_map.102.refs_5_ = bf16[256,2404]{1,0:T(8,128)(2,1)} custom-call(s32[1]{0:T(128)} %bitcast.me_ref, bf16[128,640]{1,0:T(8,128)(2,1)S(1)} %shard_map.91.own_ref.refs_0_, bf16[128,640]{1,0:T(8,128)(2,1)S(1)} %collective-permute-done.10.core_ref.refs_1_, bf16[128,640]{1,0:T(8,128)(2,1)S(1)} %collective-permute-done.11.value_ref.far_ref.refs_2_, ...), custom_call_target="tpu_custom_call" | custom-call | bytes 1 | tf_op jit(solution)/shard_map/pallas_call | solution.py:31
  37.0 0.8 shard_map.104.most_ref
  38.2 1.8 %collective-permute-done.17.value_ref.far_ref.refs_7_ = bf16[128,640]{1,0:T(8,128)(2,1)S(1)} collective-permute-done((bf16[128,640]{1,0:T(8,128)(2,1)S(1)}, bf16[128,640]{1,0:T(8,128)(2,1)S(1)}, u32[]{:S(2)}, u32[]{:S(2)}) %collective-permute-start.17) | collective-permute-done | bytes 163872 | tf_op jit(solution)/shard_map/ppermute | solution.py:59
  40.6 0.8 shard_map.107.most_ref
  41.6 1.6 %shard_map.108 = (bf16[256,640]{1,0:T(8,128)(2,1)}, bf16[4,256,640]{2,1,0:T(8,128)(2,1)}) custom-call(f32[8,128]{1,0:T(8,128)S(1)} %get-tuple-element.104.step_ref, bf16[128,640]{1,0:T(8,128)(2,1)S(1)} %get-tuple-element.105.own_ref.x_ref.refs_5_, f32[128,640]{1,0:T(8,128)S(1)} %shard_map.107.most_ref, ...), custom_call_target="tpu_custom_call" | custom-call | bytes 1 | tf_op jit(solution)/shard_map/pallas_call | solution.py:31
  43.2 17.4 %all_to_all.15.w_ref = bf16[8,32,640]{2,1,0:T(8,128)(2,1)S(1)} all-to-all(bf16[8,32,640]{2,1,0:T(8,128)(2,1)} %bitcast.17), channel_id=1, replica_groups=mesh['cuts'=8,'row'=4] {'cuts'}, dimensions={0} | all-to-all | bytes 655360 | tf_op jit(solution)/shard_map/all_to_all | solution.py:68
  60.6 1.6 %shard_map.109 = (f32[8,32,640]{2,1,0:T(8,128)S(1)}, f32[8,32,640]{2,1,0:T(8,128)S(1)}, bf16[8,32,1920]{2,1,0:T(8,128)(2,1)S(1)}, f32[8,256]{1,0:T(8,128)S(1)}) custom-call(s32[1]{0:T(128)} %bitcast.me_ref, s32[1,64]{1,0:T(1,128)S(1)} %bitcast.13, bf16[8,32,640]{2,1,0:T(8,128)(2,1)S(1)} %all_to_all.15.w_ref, bf16[8,32,2048]{2,1,0:T(8,128)(2,1)} %all-to-all-done.rc_ref), custom_call_target="tpu_custom_call" | custom-call | bytes 1 | tf_op jit(solution)/shard_map/pallas_call | solution.py:425
  62.3 1.6 %collective-permute-start.25 = (f32[8,256]{1,0:T(8,128)S(1)}, f32[8,256]{1,0:T(8,128)S(1)}, u32[]{:S(2)}, u32[]{:S(2)}) collective-permute-start(f32[8,256]{1,0:T(8,128)S(1)} %get-tuple-element.139.s0), channel_id=1, source_target_pairs={{0,2},{1,3},{2,0},{3,1},{4,6},{5,7},{6,4},{7,5},{8,10},{9,11},{10,... | collective-permute-start | bytes 24584 | tf_op jit(solution)/shard_map/ppermute | solution.py:59
  64.2 1.2 %collective-permute-done.26.s3 = f32[8,256]{1,0:T(8,128)S(1)} collective-permute-done((f32[8,256]{1,0:T(8,128)S(1)}, f32[8,256]{1,0:T(8,128)S(1)}, u32[]{:S(2)}, u32[]{:S(2)}) %collective-permute-start.26) | collective-permute-done | bytes 8224 | tf_op jit(solution)/shard_map/ppermute | solution.py:59
  66.0 1.2 %shard_map.110 = bf16[8,32,640]{2,1,0:T(8,128)(2,1)} custom-call(f32[8,32,640]{2,1,0:T(8,128)S(1)} %get-tuple-element.136.field_ref, f32[8,32,640]{2,1,0:T(8,128)S(1)} %get-tuple-element.137.cmap_ref, bf16[8,32,1920]{2,1,0:T(8,128)(2,1)S(1)} %get-tuple-element.138.rc_ref, f32[8,256]{1,0:T(8,128)S(1)} %get-tuple-element.139.s0, ...), custom_call_target="tpu_custom_call" | custom-call | bytes 1 | tf_op jit(solution)/shard_map/pallas_call | solution.py:31
  67.3 15.1 %all_to_all.16 = bf16[8,32,640]{2,1,0:T(8,128)(2,1)S(1)} all-to-all(bf16[8,32,640]{2,1,0:T(8,128)(2,1)} %shard_map.110), channel_id=1, replica_groups=mesh['cuts'=8,'row'=4] {'cuts'}, dimensions={0} | all-to-all | bytes 655360 | tf_op jit(solution)/shard_map/all_to_all | solution.py:68
  87.2 1.5 %collective-permute-start.38 = (bf16[128,640]{1,0:T(8,128)(2,1)S(1)}, bf16[128,640]{1,0:T(8,128)(2,1)S(1)}, u32[]{:S(2)}, u32[]{:S(2)}) collective-permute-start(bf16[128,640]{1,0:T(8,128)(2,1)S(1)} %shard_map.116), channel_id=1, source_target_pairs={{0,2},{1,3},{2,0},{3,1},{4,6},{5,7},{6,4},{7,5},{8,10},{9,11},{10,... | collective-permute-start | bytes 491528 | tf_op jit(solution)/shard_map/ppermute | solution.py:59
  89.0 2.3 %collective-permute-done.30.far_ref = bf16[128,640]{1,0:T(8,128)(2,1)S(1)} collective-permute-done((bf16[128,640]{1,0:T(8,128)(2,1)S(1)}, bf16[128,640]{1,0:T(8,128)(2,1)S(1)}, u32[]{:S(2)}, u32[]{:S(2)}) %collective-permute-start.30) | collective-permute-done | bytes 163872 | tf_op jit(solution)/shard_map/ppermute | solution.py:59
  96.2 1.5 %collective-permute-start.42 = (bf16[128,640]{1,0:T(8,128)(2,1)S(1)}, bf16[128,640]{1,0:T(8,128)(2,1)S(1)}, u32[]{:S(2)}, u32[]{:S(2)}) collective-permute-start(bf16[128,640]{1,0:T(8,128)(2,1)S(1)} %shard_map.123), channel_id=1, source_target_pairs={{0,2},{1,3},{2,0},{3,1},{4,6},{5,7},{6,4},{7,5},{8,10},{9,11},{10,... | collective-permute-start | bytes 491528 | tf_op jit(solution)/shard_map/ppermute | solution.py:59
  97.7 2.7 %shard_map.124.refs_3_ = f32[640,2404]{1,0:T(8,128)S(1)} custom-call(bf16[128,640]{1,0:T(8,128)(2,1)S(1)} %get-tuple-element.142.scaled_ref.refs_0_, bf16[128,640]{1,0:T(8,128)(2,1)S(1)} %get-tuple-element.152.scaled_ref.refs_1_, bf16[128,640]{1,0:T(8,128)(2,1)S(1)} %get-tuple-element.160.scaled_ref.refs_2_, ...), custom_call_target="tpu_custom_call" | custom-call | bytes 1 | tf_op jit(solution)/shard_map/pallas_call | solution.py:31
  105.5 1.2 %collective-permute-start.50 = (bf16[128,640]{1,0:T(8,128)(2,1)S(1)}, bf16[128,640]{1,0:T(8,128)(2,1)S(1)}, u32[]{:S(2)}, u32[]{:S(2)}) collective-permute-start(bf16[128,640]{1,0:T(8,128)(2,1)S(1)} %shard_map.130), channel_id=1, source_target_pairs={{0,2},{1,3},{2,0},{3,1},{4,6},{5,7},{6,4},{7,5},{8,10},{9,11},{10,... | collective-permute-start | bytes 491528 | tf_op jit(solution)/shard_map/ppermute | solution.py:59
  106.6 3.1 %shard_map.131.refs_4_ = f32[601,1,2404]{2,1,0:T(1,128)} custom-call(bf16[128,640]{1,0:T(8,128)(2,1)S(1)} %get-tuple-element.181.scaled_ref.refs_0_, bf16[128,640]{1,0:T(8,128)(2,1)S(1)} %get-tuple-element.191.scaled_ref.refs_1_, bf16[256,2404]{1,0:T(8,128)(2,1)S(1)} %copy-done, f32[640,2404]{1,0:T(8,128)S(1)} %shard_map.124.refs_3_), custom_call_target="tpu_custom_call" | custom-call | bytes 1 | tf_op jit(solution)/shard_map/pallas_call | solution.py:308
  109.7 2.0 %shard_map.132 = f32[601,1,2404]{2,1,0:T(1,128)} custom-call(bf16[128,640]{1,0:T(8,128)(2,1)S(1)} %get-tuple-element.181.scaled_ref.refs_0_, bf16[128,640]{1,0:T(8,128)(2,1)S(1)} %get-tuple-element.191.scaled_ref.refs_1_, bf16[256,2404]{1,0:T(8,128)(2,1)S(1)} %copy-done, f32[640,2404]{1,0:T(8,128)S(1)} %shard_map.124.refs_3_, ...), custom_call_target="tpu_custom_call", output_to_operand_aliasing={{}: (4, {})} | custom-call | flops 5000000000 | bytes 1 | tf_op jit(solution)/shard_map/pallas_call | solution.py:308
  112.3 1.1 %shard_map.133 = f32[601,1,256]{2,1,0:T(1,128)} custom-call(f32[128,640]{1,0:T(8,128)S(1)} %get-tuple-element.193.refs_0_, f32[128,640]{1,0:T(8,128)S(1)} %get-tuple-element.194.refs_1_, bf16[128,640]{1,0:T(8,128)(2,1)S(1)} %collective-permute-done.48.refs_2_, bf16[128,640]{1,0:T(8,128)(2,1)S(1)} %collective-permute-done.47.refs_3_, ...), custom_call_target="tpu_custom_call" | custom-call | bytes 1 | tf_op jit(solution)/shard_map/pallas_call | solution.py:31
  (136 shorter events, 25.3 us)
Async XLA Ops:
  4.4 38.7 %all-to-all-start = ((bf16[8,32,2048]{2,1,0:T(8,128)(2,1)}), bf16[8,32,2048]{2,1,0:T(8,128)(2,1)}, u32[]{:S(2)}, u32[]{:S(2)}) async-start(bf16[8,32,2048]{2,1,0:T(8,128)(2,1)} %shard_map.86), calls=%async_computation | async-start | bytes 2097152 | tf_op jit(solution)/shard_map/all_to_all | solution.py:68
  11.9 6.8 %collective-permute-start.3 = (bf16[128,640]{1,0:T(8,128)(2,1)S(1)}, bf16[128,640]{1,0:T(8,128)(2,1)S(1)}, u32[]{:S(2)}, u32[]{:S(2)}) collective-permute-start(bf16[128,640]{1,0:T(8,128)(2,1)S(1)} %get-tuple-element.102.own_ref.x_ref.refs_0_), channel_id=1, source_target_pairs={{0,2},{1,3},{2,0},{3,1},{4,6},{5,7},{6,4},{7,5},{8,10},{9,11},{10,... | collective-permute-start | bytes 491528 | tf_op jit(solution)/shard_map/ppermute | solution.py:59
  13.4 5.8 %collective-permute-start.2 = (bf16[128,640]{1,0:T(8,128)(2,1)S(1)}, bf16[128,640]{1,0:T(8,128)(2,1)S(1)}, u32[]{:S(2)}, u32[]{:S(2)}) collective-permute-start(bf16[128,640]{1,0:T(8,128)(2,1)S(1)} %get-tuple-element.102.own_ref.x_ref.refs_0_), channel_id=1, source_target_pairs={{0,1},{1,0},{2,3},{3,2},{4,5},{5,4},{6,7},{7,6},{8,9},{9,8},{10,11... | collective-permute-start | bytes 491528 | tf_op jit(solution)/shard_map/ppermute | solution.py:59
  13.4 9.1 %collective-permute-start.1 = (bf16[128,640]{1,0:T(8,128)(2,1)S(1)}, bf16[128,640]{1,0:T(8,128)(2,1)S(1)}, u32[]{:S(2)}, u32[]{:S(2)}) collective-permute-start(bf16[128,640]{1,0:T(8,128)(2,1)S(1)} %get-tuple-element.105.own_ref.x_ref.refs_5_), channel_id=1, source_target_pairs={{0,2},{1,3},{2,0},{3,1},{4,6},{5,7},{6,4},{7,5},{8,10},{9,11},{10,... | collective-permute-start | bytes 491528 | tf_op jit(solution)/shard_map/ppermute | solution.py:59
  19.2 4.1 %collective-permute-start = (bf16[128,640]{1,0:T(8,128)(2,1)S(1)}, bf16[128,640]{1,0:T(8,128)(2,1)S(1)}, u32[]{:S(2)}, u32[]{:S(2)}) collective-permute-start(bf16[128,640]{1,0:T(8,128)(2,1)S(1)} %get-tuple-element.105.own_ref.x_ref.refs_5_), channel_id=1, source_target_pairs={{0,1},{1,0},{2,3},{3,2},{4,5},{5,4},{6,7},{7,6},{8,9},{9,8},{10,11... | collective-permute-start | bytes 491528 | tf_op jit(solution)/shard_map/ppermute | solution.py:59
  20.5 6.8 %collective-permute-start.11 = (bf16[128,640]{1,0:T(8,128)(2,1)S(1)}, bf16[128,640]{1,0:T(8,128)(2,1)S(1)}, u32[]{:S(2)}, u32[]{:S(2)}) collective-permute-start(bf16[128,640]{1,0:T(8,128)(2,1)S(1)} %shard_map.91.own_ref.refs_0_), channel_id=1, source_target_pairs={{0,2},{1,3},{2,0},{3,1},{4,6},{5,7},{6,4},{7,5},{8,10},{9,11},{10,... | collective-permute-start | bytes 491528 | tf_op jit(solution)/shard_map/ppermute | solution.py:59
  22.6 1.6 %collective-permute-start.7 = (bf16[64,640]{1,0:T(8,128)(2,1)S(1)}, bf16[64,640]{1,0:T(8,128)(2,1)S(1)}, u32[]{:S(2)}, u32[]{:S(2)}) collective-permute-start(bf16[64,640]{1,0:T(8,128)(2,1)S(1)} %get-tuple-element.114), channel_id=1, source_target_pairs={{0,1},{1,0},{2,3},{3,2},{4,5},{5,4},{6,7},{7,6},{8,9},{9,8},{10,11... | collective-permute-start | bytes 245768 | tf_op jit(solution)/shard_map/ppermute | solution.py:59
  23.1 4.9 %collective-permute-start.10 = (bf16[128,640]{1,0:T(8,128)(2,1)S(1)}, bf16[128,640]{1,0:T(8,128)(2,1)S(1)}, u32[]{:S(2)}, u32[]{:S(2)}) collective-permute-start(bf16[128,640]{1,0:T(8,128)(2,1)S(1)} %shard_map.91.own_ref.refs_0_), channel_id=1, source_target_pairs={{0,1},{1,0},{2,3},{3,2},{4,5},{5,4},{6,7},{7,6},{8,9},{9,8},{10,11... | collective-permute-start | bytes 491528 | tf_op jit(solution)/shard_map/ppermute | solution.py:59
  24.5 7.0 %collective-permute-start.9 = (bf16[128,640]{1,0:T(8,128)(2,1)S(1)}, bf16[128,640]{1,0:T(8,128)(2,1)S(1)}, u32[]{:S(2)}, u32[]{:S(2)}) collective-permute-start(bf16[128,640]{1,0:T(8,128)(2,1)S(1)} %shard_map.94.own_ref.refs_5_), channel_id=1, source_target_pairs={{0,2},{1,3},{2,0},{3,1},{4,6},{5,7},{6,4},{7,5},{8,10},{9,11},{10,... | collective-permute-start | bytes 491528 | tf_op jit(solution)/shard_map/ppermute | solution.py:59
  27.9 4.4 %collective-permute-start.8 = (bf16[128,640]{1,0:T(8,128)(2,1)S(1)}, bf16[128,640]{1,0:T(8,128)(2,1)S(1)}, u32[]{:S(2)}, u32[]{:S(2)}) collective-permute-start(bf16[128,640]{1,0:T(8,128)(2,1)S(1)} %shard_map.94.own_ref.refs_5_), channel_id=1, source_target_pairs={{0,1},{1,0},{2,3},{3,2},{4,5},{5,4},{6,7},{7,6},{8,9},{9,8},{10,11... | collective-permute-start | bytes 491528 | tf_op jit(solution)/shard_map/ppermute | solution.py:59
  29.3 7.1 %collective-permute-start.19 = (bf16[128,640]{1,0:T(8,128)(2,1)S(1)}, bf16[128,640]{1,0:T(8,128)(2,1)S(1)}, u32[]{:S(2)}, u32[]{:S(2)}) collective-permute-start(bf16[128,640]{1,0:T(8,128)(2,1)S(1)} %shard_map.98.own_ref.refs_0_), channel_id=1, source_target_pairs={{0,2},{1,3},{2,0},{3,1},{4,6},{5,7},{6,4},{7,5},{8,10},{9,11},{10,... | collective-permute-start | bytes 491528 | tf_op jit(solution)/shard_map/ppermute | solution.py:59
  32.1 4.9 %collective-permute-start.18 = (bf16[128,640]{1,0:T(8,128)(2,1)S(1)}, bf16[128,640]{1,0:T(8,128)(2,1)S(1)}, u32[]{:S(2)}, u32[]{:S(2)}) collective-permute-start(bf16[128,640]{1,0:T(8,128)(2,1)S(1)} %shard_map.98.own_ref.refs_0_), channel_id=1, source_target_pairs={{0,1},{1,0},{2,3},{3,2},{4,5},{5,4},{6,7},{7,6},{8,9},{9,8},{10,11... | collective-permute-start | bytes 491528 | tf_op jit(solution)/shard_map/ppermute | solution.py:59
  33.5 6.5 %collective-permute-start.17 = (bf16[128,640]{1,0:T(8,128)(2,1)S(1)}, bf16[128,640]{1,0:T(8,128)(2,1)S(1)}, u32[]{:S(2)}, u32[]{:S(2)}) collective-permute-start(bf16[128,640]{1,0:T(8,128)(2,1)S(1)} %shard_map.101.own_ref.refs_5_), channel_id=1, source_target_pairs={{0,2},{1,3},{2,0},{3,1},{4,6},{5,7},{6,4},{7,5},{8,10},{9,11},{10,... | collective-permute-start | bytes 491528 | tf_op jit(solution)/shard_map/ppermute | solution.py:59
  36.9 3.7 %collective-permute-start.16 = (bf16[128,640]{1,0:T(8,128)(2,1)S(1)}, bf16[128,640]{1,0:T(8,128)(2,1)S(1)}, u32[]{:S(2)}, u32[]{:S(2)}) collective-permute-start(bf16[128,640]{1,0:T(8,128)(2,1)S(1)} %shard_map.101.own_ref.refs_5_), channel_id=1, source_target_pairs={{0,1},{1,0},{2,3},{3,2},{4,5},{5,4},{6,7},{7,6},{8,9},{9,8},{10,11... | collective-permute-start | bytes 491528 | tf_op jit(solution)/shard_map/ppermute | solution.py:59
  62.2 3.1 %collective-permute-start.26 = (f32[8,256]{1,0:T(8,128)S(1)}, f32[8,256]{1,0:T(8,128)S(1)}, u32[]{:S(2)}, u32[]{:S(2)}) collective-permute-start(f32[8,256]{1,0:T(8,128)S(1)} %get-tuple-element.139.s0), channel_id=1, source_target_pairs={{0,3},{1,2},{2,1},{3,0},{4,7},{5,6},{6,5},{7,4},{8,11},{9,10},{10,... | collective-permute-start | bytes 24584 | tf_op jit(solution)/shard_map/ppermute | solution.py:59
  62.3 3.7 %collective-permute-start.25 = (f32[8,256]{1,0:T(8,128)S(1)}, f32[8,256]{1,0:T(8,128)S(1)}, u32[]{:S(2)}, u32[]{:S(2)}) collective-permute-start(f32[8,256]{1,0:T(8,128)S(1)} %get-tuple-element.139.s0), channel_id=1, source_target_pairs={{0,2},{1,3},{2,0},{3,1},{4,6},{5,7},{6,4},{7,5},{8,10},{9,11},{10,... | collective-permute-start | bytes 24584 | tf_op jit(solution)/shard_map/ppermute | solution.py:59
  63.9 2.1 %collective-permute-start.24 = (f32[8,256]{1,0:T(8,128)S(1)}, f32[8,256]{1,0:T(8,128)S(1)}, u32[]{:S(2)}, u32[]{:S(2)}) collective-permute-start(f32[8,256]{1,0:T(8,128)S(1)} %get-tuple-element.139.s0), channel_id=1, source_target_pairs={{0,1},{1,0},{2,3},{3,2},{4,5},{5,4},{6,7},{7,6},{8,9},{9,8},{10,11... | collective-permute-start | bytes 24584 | tf_op jit(solution)/shard_map/ppermute | solution.py:59
  84.3 7.1 %collective-permute-start.30 = (bf16[128,640]{1,0:T(8,128)(2,1)S(1)}, bf16[128,640]{1,0:T(8,128)(2,1)S(1)}, u32[]{:S(2)}, u32[]{:S(2)}) collective-permute-start(bf16[128,640]{1,0:T(8,128)(2,1)S(1)} %shard_map.113), channel_id=1, source_target_pairs={{0,2},{1,3},{2,0},{3,1},{4,6},{5,7},{6,4},{7,5},{8,10},{9,11},{10,... | collective-permute-start | bytes 491528 | tf_op jit(solution)/shard_map/ppermute | solution.py:59
  84.9 6.4 %collective-permute-start.27 = (bf16[128,640]{1,0:T(8,128)(2,1)S(1)}, bf16[128,640]{1,0:T(8,128)(2,1)S(1)}, u32[]{:S(2)}, u32[]{:S(2)}) collective-permute-start(bf16[128,640]{1,0:T(8,128)(2,1)S(1)} %get-tuple-element.144), channel_id=1, source_target_pairs={{0,1},{1,0},{2,3},{3,2},{4,5},{5,4},{6,7},{7,6},{8,9},{9,8},{10,11... | collective-permute-start | bytes 491528 | tf_op jit(solution)/shard_map/ppermute | solution.py:59
  85.3 1.7 %collective-permute-start.32 = (bf16[64,640]{1,0:T(8,128)(2,1)S(1)}, bf16[64,640]{1,0:T(8,128)(2,1)S(1)}, u32[]{:S(2)}, u32[]{:S(2)}) collective-permute-start(bf16[64,640]{1,0:T(8,128)(2,1)S(1)} %get-tuple-element.154), channel_id=1, source_target_pairs={{0,1},{1,0},{2,3},{3,2},{4,5},{5,4},{6,7},{7,6},{8,9},{9,8},{10,11... | collective-permute-start | bytes 245768 | tf_op jit(solution)/shard_map/ppermute | solution.py:59
  86.5 7.8 %collective-permute-start.37 = (bf16[128,640]{1,0:T(8,128)(2,1)S(1)}, bf16[128,640]{1,0:T(8,128)(2,1)S(1)}, u32[]{:S(2)}, u32[]{:S(2)}) collective-permute-start(bf16[128,640]{1,0:T(8,128)(2,1)S(1)} %get-tuple-element.166), channel_id=1, source_target_pairs={{0,1},{1,0},{2,3},{3,2},{4,5},{5,4},{6,7},{7,6},{8,9},{9,8},{10,11... | collective-permute-start | bytes 491528 | tf_op jit(solution)/shard_map/ppermute | solution.py:59
  87.2 7.2 %collective-permute-start.38 = (bf16[128,640]{1,0:T(8,128)(2,1)S(1)}, bf16[128,640]{1,0:T(8,128)(2,1)S(1)}, u32[]{:S(2)}, u32[]{:S(2)}) collective-permute-start(bf16[128,640]{1,0:T(8,128)(2,1)S(1)} %shard_map.116), channel_id=1, source_target_pairs={{0,2},{1,3},{2,0},{3,1},{4,6},{5,7},{6,4},{7,5},{8,10},{9,11},{10,... | collective-permute-start | bytes 491528 | tf_op jit(solution)/shard_map/ppermute | solution.py:59
  93.2 7.1 %collective-permute-start.36 = (bf16[128,640]{1,0:T(8,128)(2,1)S(1)}, bf16[128,640]{1,0:T(8,128)(2,1)S(1)}, u32[]{:S(2)}, u32[]{:S(2)}) collective-permute-start(bf16[128,640]{1,0:T(8,128)(2,1)S(1)} %shard_map.120), channel_id=1, source_target_pairs={{0,2},{1,3},{2,0},{3,1},{4,6},{5,7},{6,4},{7,5},{8,10},{9,11},{10,... | collective-permute-start | bytes 491528 | tf_op jit(solution)/shard_map/ppermute | solution.py:59
  93.4 7.0 %collective-permute-start.33 = (bf16[128,640]{1,0:T(8,128)(2,1)S(1)}, bf16[128,640]{1,0:T(8,128)(2,1)S(1)}, u32[]{:S(2)}, u32[]{:S(2)}) collective-permute-start(bf16[128,640]{1,0:T(8,128)(2,1)S(1)} %get-tuple-element.162), channel_id=1, source_target_pairs={{0,1},{1,0},{2,3},{3,2},{4,5},{5,4},{6,7},{7,6},{8,9},{9,8},{10,11... | collective-permute-start | bytes 491528 | tf_op jit(solution)/shard_map/ppermute | solution.py:59
  95.9 7.4 %collective-permute-start.41 = (bf16[128,640]{1,0:T(8,128)(2,1)S(1)}, bf16[128,640]{1,0:T(8,128)(2,1)S(1)}, u32[]{:S(2)}, u32[]{:S(2)}) collective-permute-start(bf16[128,640]{1,0:T(8,128)(2,1)S(1)} %get-tuple-element.179), channel_id=1, source_target_pairs={{0,1},{1,0},{2,3},{3,2},{4,5},{5,4},{6,7},{7,6},{8,9},{9,8},{10,11... | collective-permute-start | bytes 491528 | tf_op jit(solution)/shard_map/ppermute | solution.py:59
  96.2 7.1 %collective-permute-start.42 = (bf16[128,640]{1,0:T(8,128)(2,1)S(1)}, bf16[128,640]{1,0:T(8,128)(2,1)S(1)}, u32[]{:S(2)}, u32[]{:S(2)}) collective-permute-start(bf16[128,640]{1,0:T(8,128)(2,1)S(1)} %shard_map.123), channel_id=1, source_target_pairs={{0,2},{1,3},{2,0},{3,1},{4,6},{5,7},{6,4},{7,5},{8,10},{9,11},{10,... | collective-permute-start | bytes 491528 | tf_op jit(solution)/shard_map/ppermute | solution.py:59
  102.3 7.4 %collective-permute-start.47 = (bf16[128,640]{1,0:T(8,128)(2,1)S(1)}, bf16[128,640]{1,0:T(8,128)(2,1)S(1)}, u32[]{:S(2)}, u32[]{:S(2)}) collective-permute-start(bf16[128,640]{1,0:T(8,128)(2,1)S(1)} %shard_map.127), channel_id=1, source_target_pairs={{0,2},{1,3},{2,0},{3,1},{4,6},{5,7},{6,4},{7,5},{8,10},{9,11},{10,... | collective-permute-start | bytes 491528 | tf_op jit(solution)/shard_map/ppermute | solution.py:59
  103.6 1.8 %collective-permute-start.46 = (bf16[64,640]{1,0:T(8,128)(2,1)S(1)}, bf16[64,640]{1,0:T(8,128)(2,1)S(1)}, u32[]{:S(2)}, u32[]{:S(2)}) collective-permute-start(bf16[64,640]{1,0:T(8,128)(2,1)S(1)} %get-tuple-element.190), channel_id=1, source_target_pairs={{0,1},{1,0},{2,3},{3,2},{4,5},{5,4},{6,7},{7,6},{8,9},{9,8},{10,11... | collective-permute-start | bytes 245768 | tf_op jit(solution)/shard_map/ppermute | solution.py:59
  103.7 1.7 %collective-permute-start.45 = (bf16[64,640]{1,0:T(8,128)(2,1)S(1)}, bf16[64,640]{1,0:T(8,128)(2,1)S(1)}, u32[]{:S(2)}, u32[]{:S(2)}) collective-permute-start(bf16[64,640]{1,0:T(8,128)(2,1)S(1)} %get-tuple-element.187), channel_id=1, source_target_pairs={{0,1},{1,0},{2,3},{3,2},{4,5},{5,4},{6,7},{7,6},{8,9},{9,8},{10,11... | collective-permute-start | bytes 245768 | tf_op jit(solution)/shard_map/ppermute | solution.py:59
  104.2 8.1 %collective-permute-start.48 = (bf16[128,640]{1,0:T(8,128)(2,1)S(1)}, bf16[128,640]{1,0:T(8,128)(2,1)S(1)}, u32[]{:S(2)}, u32[]{:S(2)}) collective-permute-start(bf16[128,640]{1,0:T(8,128)(2,1)S(1)} %get-tuple-element.195), channel_id=1, source_target_pairs={{0,1},{1,0},{2,3},{3,2},{4,5},{5,4},{6,7},{7,6},{8,9},{9,8},{10,11... | collective-permute-start | bytes 491528 | tf_op jit(solution)/shard_map/ppermute | solution.py:59
  104.9 7.4 %collective-permute-start.49 = (bf16[128,640]{1,0:T(8,128)(2,1)S(1)}, bf16[128,640]{1,0:T(8,128)(2,1)S(1)}, u32[]{:S(2)}, u32[]{:S(2)}) collective-permute-start(bf16[128,640]{1,0:T(8,128)(2,1)S(1)} %get-tuple-element.198), channel_id=1, source_target_pairs={{0,1},{1,0},{2,3},{3,2},{4,5},{5,4},{6,7},{7,6},{8,9},{9,8},{10,11... | collective-permute-start | bytes 491528 | tf_op jit(solution)/shard_map/ppermute | solution.py:59
  105.5 6.8 %collective-permute-start.50 = (bf16[128,640]{1,0:T(8,128)(2,1)S(1)}, bf16[128,640]{1,0:T(8,128)(2,1)S(1)}, u32[]{:S(2)}, u32[]{:S(2)}) collective-permute-start(bf16[128,640]{1,0:T(8,128)(2,1)S(1)} %shard_map.130), channel_id=1, source_target_pairs={{0,2},{1,3},{2,0},{3,1},{4,6},{5,7},{6,4},{7,5},{8,10},{9,11},{10,... | collective-permute-start | bytes 491528 | tf_op jit(solution)/shard_map/ppermute | solution.py:59
  (27 other events, 83.9 us)
